TPU v7x, 32 devices: a whole 2x2x4 slice. The times are simulated.
32 devices in a mesh: ops: 2 (over x), sec: 16 (over z, y, core).
Axes of the slice: x: 2, y: 2, z: 4, core: 2. Of those that a mesh axis runs over, the one named last changes fastest.
Arguments:
- wavefunction: float32 [128, 2, 128, 128], P('sec'), may hold values from -6 to 6
- left_blocks: float32 [16, 128, 128, 128], P('ops', 'sec'), may hold values from -0.5 to 0.5
- right_blocks: float32 [16, 128, 128, 128], P('ops', 'sec'), may hold values from -0.125 to 0.125
- target_owner: int32 [2, 16, 8, 8, 1], P('ops'), may hold values from 0 to 15; in each aligned block of 64 rows (0 to 63, 64 to 127, ..., all dimensions but the last counted through in order) at most 5 rows name the same one
- target_local: int32 [2, 16, 8, 8], P('ops'), may hold values from 0 to 7
Outputs:
- sigma: float32 [128, 2, 128, 128], P('sec', None, 'ops')
Inputs may be any that keep to these rules, and one draw needn't show every extreme that they name: `target_owner`: among the 64 pairs [o, d, :, :, 0] of one device, at most 5 name the same owner, and some device's pairs name one owner exactly 5 times.
All inputs are finite; a program needn't handle non-finite values.
Results may differ from a plain program's by a relative error of at most 0.00013.
Values sent between devices are 32-bit elements; how exact they have to be, the bound alone decides.
No kernel may reach another device: no remote copies, remote signals or barrier semaphores. Data moves between devices by JAX's collectives and lax.ppermute only.
A program may use at most 192 MiB of HBM per device.

v0:
```python
import jax
import jax.numpy as jnp
from jax import lax
from jax.sharding import PartitionSpec as P

exact_mode = lax.Precision.HIGHEST


def shards(wavefunction, left_blocks, right_blocks, target_owner, target_local):
    sec_count = lax.axis_size("sec")
    term_local = left_blocks.shape[0]
    sector_local = left_blocks.shape[1]
    vectors = wavefunction.shape[1]
    states = wavefunction.shape[2]
    pair_count = term_local * sector_local
    capacity = (pair_count + sec_count - 1) // sec_count + 1
    slot_count = sec_count * capacity
    my_index = lax.axis_index("sec")
    owner_all = target_owner[0, :, :, :, 0].reshape(sec_count, pair_count)
    local_all = target_local[0].reshape(sec_count, pair_count)
    own_owner = lax.dynamic_index_in_dim(owner_all, my_index, 0, keepdims=False)
    peer_onehot = (own_owner[:, None] == jnp.arange(sec_count, dtype=jnp.int32)[None, :]).astype(
        jnp.int32
    )
    earlier = jnp.cumsum(peer_onehot, axis=0) - peer_onehot
    send_slot = own_owner * capacity + jnp.sum(earlier * peer_onehot, axis=1)
    is_mine = owner_all == my_index
    mine_count = is_mine.astype(jnp.int32)
    position = jnp.cumsum(mine_count, axis=1) - mine_count
    source_base = jnp.arange(sec_count, dtype=jnp.int32)[:, None] * capacity
    recv_slot = jnp.where(is_mine, source_base + position, slot_count)
    slot_sector = (
        jnp.zeros((slot_count,), jnp.int32)
        .at[recv_slot.reshape(-1)]
        .set(local_all.reshape(-1), mode="drop")
    )
    half_applied = jnp.einsum("jvbe,kjde->kjvbd", wavefunction, right_blocks, precision=exact_mode)
    contrib = jnp.einsum("kjab,kjvbd->kjvad", left_blocks, half_applied, precision=exact_mode)
    contrib = contrib.reshape(pair_count, vectors, states, states)
    routed = (
        jnp.zeros((slot_count, vectors, states, states), jnp.float32).at[send_slot].set(contrib)
    )
    arrived = lax.all_to_all(routed, "sec", split_axis=0, concat_axis=0, tiled=True)
    flat_rows = arrived.reshape(slot_count, vectors * states * states)
    selector = (slot_sector[None, :] == jnp.arange(sector_local, dtype=jnp.int32)[:, None]).astype(
        jnp.float32
    )
    partial_sum = jnp.dot(
        selector, flat_rows, precision=exact_mode, preferred_element_type=jnp.float32
    )
    partial_sum = partial_sum.reshape(sector_local, vectors, states, states)
    return lax.psum_scatter(partial_sum, "ops", scatter_dimension=2, tiled=True)


def solution(mesh):
    placed = (
        P("sec", None, None, None),
        P("ops", "sec", None, None),
        P("ops", "sec", None, None),
        P("ops", None, None, None, None),
        P("ops", None, None, None),
    )
    return jax.shard_map(
        shards, mesh=mesh, in_specs=placed, out_specs=P("sec", None, "ops", None), check_vma=False
    )
```

profile of v0, /device:TPU:0, one launch (start us, length us, event | category | flops | bytes accessed | tf_op | source)
XLA Modules:
  0.0 353.0 jit_solution(12535534341774651220)
XLA Ops:
  6.5 0.0 copy-start
  6.5 0.9 copy.17
  7.5 0.1 fusion.8
  7.5 0.1 reduce_window_sum.26
  7.6 0.0 copy-start.2
  7.6 0.2 select_reduce_fusion
  7.8 0.0 copy-done
  7.8 9.2 %fusion.5 = f32[8,8,128,2,128]{4,2,3,0,1:T(8,128)S(1)} fusion(f32[8,8,128,128]{3,2,1,0:T(8,128)} %param.7, f32[8,2,128,128]{3,2,1,0:T(8,128)S(1)} %copy-done), kind=kOutput, calls=%fused_computation.8 | convolution fusion | flops 3221225472 | bytes 13631488 | tf_op jit(solution)/shard_map/jvbe,kjde->kjvbd/dot_general | solution.py:37
  17.0 0.0 copy-done.2
  17.0 10.0 %fusion.2 = f32[8,8,2,128,128]{4,3,2,1,0:T(8,128)} fusion(f32[8,8,128,2,128]{4,2,3,0,1:T(8,128)S(1)} %fusion.5, f32[8,8,128,128]{3,2,1,0:T(8,128)S(1)} %copy-done.2), kind=kOutput, calls=%fused_computation.5 | convolution fusion | flops 3221225472 | bytes 20971520 | tf_op jit(solution)/shard_map/kjab,kjvbd->kjvad/dot_general | solution.py:38
  27.1 9.0 %copy.20 = f32[64,2,128,128]{3,2,1,0:T(8,128)} copy(f32[64,2,128,128]{2,3,1,0:T(8,128)} %bitcast.72) | data formatting | bytes 16777216 | tf_op jit(solution)/shard_map/reshape | solution.py:39
  36.1 5.2 %broadcast_in_dim.10 = f32[80,2,128,128]{3,2,1,0:T(8,128)} broadcast(f32[]{:T(128)} %constant.12.clone.1), dimensions={} | broadcast | bytes 10485764 | tf_op jit(solution)/shard_map/broadcast_in_dim | solution.py:41
  41.2 16.1 %scatter_fusion = f32[80,2,128,128]{3,2,1,0:T(8,128)} fusion(f32[80,2,128,128]{3,2,1,0:T(8,128)} %broadcast_in_dim.10, s32[64]{0:T(128)S(1)} %fusion.12, f32[64,2,128,128]{3,2,1,0:T(8,128)} %copy.20), kind=kCustom, calls=%fused_computation.1 | custom fusion | bytes 25166080 | tf_op jit(solution)/shard_map/scatter | solution.py:41
  57.3 0.0 copy-start.3
  57.3 0.0 copy-start.4
  57.3 7.7 %all-to-all-start = ((f32[80,2,128,128]{3,2,1,0:T(8,128)}), f32[80,2,128,128]{3,2,1,0:T(8,128)}, u32[]{:S(2)}, u32[]{:S(2)}) async-start(f32[80,2,128,128]{3,2,1,0:T(8,128)} %scatter_fusion), calls=%async_computation | async-start | bytes 20971520 | tf_op jit(solution)/shard_map/all_to_all | solution.py:43
  65.0 0.0 reduce-scatter.5.cloned.1.call-start
  65.0 0.1 add.58
  65.1 0.1 add.59
  65.2 0.2 reduce_window_sum.24
  65.4 0.1 reduce_window_sum.25
  65.5 0.0 copy-done.3
  65.5 0.1 copy.16
  65.7 0.1 eq.51
  65.8 0.0 copy-done.4
  65.8 0.1 copy.18
  65.9 0.1 reshape.101
  66.0 4.5 %scatter_custom_fusion = s32[80]{0:T(128)S(1)} fusion(s32[1024]{0:T(1024)S(1)} %bitcast.78, s32[1024]{0:T(1024)S(1)} %reshape.101, s32[]{:T(128)} %constant.8.clone.1), kind=kCustom, calls=%fused_computation.25 | custom fusion | bytes 324 | tf_op jit(solution)/shard_map/scatter | solution.py:35
  70.5 181.7 %all-to-all-done = f32[80,2,128,128]{3,2,1,0:T(8,128)} async-done(((f32[80,2,128,128]{3,2,1,0:T(8,128)}), f32[80,2,128,128]{3,2,1,0:T(8,128)}, u32[]{:S(2)}, u32[]{:S(2)}) %all-to-all-start) | async-done | bytes 10485792 | tf_op jit(solution)/shard_map/all_to_all | solution.py:43
  252.2 14.3 %copy.37 = f32[10,8,256,128]{3,1,2,0:T(8,128)} copy(f32[10,8,256,128]{3,2,1,0:T(8,128)} %bitcast.30) | data formatting | bytes 20971520
  266.5 5.8 %copy.30 = f32[10,8,256,128]{3,2,1,0:T(8,128)S(1)} copy(f32[10,8,256,128]{3,1,2,0:T(8,128)} %copy.37) | data formatting | bytes 20971520
  272.3 0.0 copy-start.1
  272.3 9.6 %fusion = f32[8,2,128,128]{3,0,2,1:T(8,128)S(1)} fusion(f32[2,128,128,80]{2,1,0,3:T(8,128)S(1)} %bitcast.71, s32[80]{0:T(128)S(1)} %scatter_custom_fusion), kind=kOutput, calls=%fused_computation.3 | convolution fusion | flops 251658880 | bytes 11534656 | tf_op jit(solution)/shard_map/dot_general | solution.py:48
  282.0 0.1 copy.26
  282.0 1.3 copy.38
  283.4 0.0 reduce-scatter.5.cloned.1.call-update
  283.4 60.6 %reduce-scatter.5.cloned.1.call-done = f32[64,2048]{1,0:T(8,128)} async-done(((f32[128,2048]{1,0:T(8,128)}), f32[64,2048]{1,0:T(8,128)}) %reduce-scatter.5.cloned.1.call-update) | async-done | bytes 524304
  344.0 1.1 copy.32
  345.2 1.0 copy.22
  346.1 0.0 copy-done.1
  (6 shorter events, 0.1 us)
Async XLA Ops:
  6.5 1.3 copy-start
  7.6 9.4 %copy-start.2 = (f32[8,8,128,128]{3,2,1,0:T(8,128)S(1)}, f32[8,8,128,128]{3,2,1,0:T(8,128)}, u32[]{:S(2)}) copy-start(f32[8,8,128,128]{3,2,1,0:T(8,128)} %param.6) | copy-start | bytes 12582916
  57.3 8.2 %copy-start.3 = (s32[1,16,8,8,1]{1,4,3,2,0:T(1,128)S(1)}, s32[1,16,8,8,1]{1,4,3,2,0:T(1,128)}, u32[]{:S(2)}) copy-start(s32[1,16,8,8,1]{1,4,3,2,0:T(1,128)} %param.8) | copy-start | bytes 12292
  57.3 8.5 %copy-start.4 = (s32[1,16,8,8]{1,3,2,0:T(8,128)S(1)}, s32[1,16,8,8]{1,3,2,0:T(8,128)}, u32[]{:S(2)}) copy-start(s32[1,16,8,8]{1,3,2,0:T(8,128)} %param.9) | copy-start | bytes 12292
  57.3 194.9 %all-to-all-start = ((f32[80,2,128,128]{3,2,1,0:T(8,128)}), f32[80,2,128,128]{3,2,1,0:T(8,128)}, u32[]{:S(2)}, u32[]{:S(2)}) async-start(f32[80,2,128,128]{3,2,1,0:T(8,128)} %scatter_fusion), calls=%async_computation | async-start | bytes 20971520 | tf_op jit(solution)/shard_map/all_to_all | solution.py:43
  65.0 279.0 %reduce-scatter.5.cloned.1.call-start = ((), (), s32[]{:S(2)}) async-start(), calls=%async_computation.2 | async-start | bytes 1572864
  272.3 73.8 %copy-start.1 = (f32[8,2,128,128]{3,2,1,0:T(8,128)S(1)}, f32[8,2,128,128]{3,2,1,0:T(8,128)}, u32[]{:S(2)}) copy-start(f32[8,2,128,128]{3,2,1,0:T(8,128)} %param.5) | copy-start | bytes 3145732
Sparse Core Ops, SparseCore 0:
  283.5 60.4 reduce-scatter.4
where the time goes:
time: 354 us; the launch traced here: 353 us
  waiting for transfers between devices  242 us (68%)
  local copies, waits for them, and re-layouts  59.9 us (17%)
  matrix products  28.8 us (8%)
  between operations  13.5 us (4%)
  starting transfers between devices  7.72 us (2%)
    all_to_all x1, waiting for transfers between devices, shards(): lax.all_to_all(routed, 'sec', split_axis=0, concat_axis=0, tiled=True)  182 us
    unnamed x2, waiting for transfers between devices  60.6 us
    unnamed x16, local copies, waits for them, and re-layouts  22.8 us
    scatter x1, local copies, waits for them, and re-layouts, shards(): jnp.zeros((slot_count, vectors, states, states), jnp.float32).at[send_slot]  16.1 us
    dot_general x1, matrix products, shards(): jnp.einsum('kjab,kjvbd->kjvad', left_blocks, half_applied, precision=exac...  10 us
    dot_general x1, matrix products, shards(): jnp.dot(selector, flat_rows, precision=exact_mode, preferred_element_type...  9.62 us
    dot_general x1, matrix products, shards(): jnp.einsum('jvbe,kjde->kjvbd', wavefunction, right_blocks, precision=exac...  9.18 us
    reshape x1, local copies, waits for them, and re-layouts, shards(): contrib = contrib.reshape(pair_count, vectors, states, states)  9 us
  transfers between devices with their start and end apart: 2, of which 2 were waited for; matrix products, arithmetic and copies ran while one was open for 2% of the time, Pallas kernels for 0%

commit v1 on v0

v1 whole, which is shorter than its diff:
```python
import functools

import jax
import jax.numpy as jnp
from jax import lax
from jax.experimental import pallas as pl
from jax.experimental.pallas import tpu as pltpu
from jax.sharding import PartitionSpec as P

CORES = 2
PLANES = 2
GROUP = 4


def coords(sec_count):
    me = lax.axis_index("sec")
    return me, me // (PLANES * CORES), (me // CORES) % PLANES, me % CORES


def find(code, sector_local, depth, z, y, rels):
    owner = code // sector_local
    local = code % sector_local
    core = owner % CORES
    y_rel = ((owner // CORES) % PLANES - y + PLANES) % PLANES
    z_rel = (owner // (CORES * PLANES) - z + depth) % depth
    inside = z_rel == rels[0]
    place = jnp.int32(0)
    for i, r in enumerate(rels[1:], 1):
        inside = inside | (z_rel == r)
        place = place + jnp.where(z_rel == r, i, 0)
    return inside, core, (place * PLANES + y_rel) * sector_local + local


def split(x):
    hi = x.astype(jnp.bfloat16)
    lo = (x - hi.astype(jnp.float32)).astype(jnp.bfloat16)
    return hi, lo


def apply_pair(left, right, psi_pair):
    m = left.shape[0]
    right_hi, right_lo = split(right)
    stacked = jnp.concatenate([right_hi, right_lo], axis=0)
    stacked = jnp.concatenate([stacked, stacked], axis=1)
    both = lax.dot_general(
        psi_pair, stacked, (((1,), (1,)), ((), ())), preferred_element_type=jnp.float32
    )
    half = both[:, :m] + both[:, m:]
    vectors = half.shape[0] // m
    half = jnp.concatenate([half[v * m : (v + 1) * m] for v in range(vectors)], axis=1)
    half_hi, half_lo = split(half)
    left_hi, left_lo = split(left)
    left_pair = jnp.concatenate([left_hi, left_lo], axis=1)
    out = jnp.dot(
        left_pair,
        jnp.concatenate([half_hi, half_hi], axis=0),
        preferred_element_type=jnp.float32,
    )
    return out + jnp.dot(left_hi, half_lo, preferred_element_type=jnp.float32)


def prepare(psi, psi_raw, psi_pairs, psi_sem):
    copy = pltpu.make_async_copy(psi, psi_raw, psi_sem)
    copy.wait()
    sectors, vectors, m, _ = psi_raw.shape

    def one(j, carry):
        hi, lo = split(psi_raw[j].reshape(vectors * m, m))
        psi_pairs[j] = jnp.concatenate([hi, lo], axis=1)
        return carry

    lax.fori_loop(0, sectors, one, 0)


def fetch(left, right, left_buf, right_buf, sems, pair, i, sectors):
    k, j = pair // sectors, pair % sectors
    return (
        pltpu.make_async_copy(left.at[k, j], left_buf.at[i], sems.at[i, 0]),
        pltpu.make_async_copy(right.at[k, j], right_buf.at[i], sems.at[i, 1]),
    )


def collect(table, base, pairs, wanted, note, begin):
    def one(p, count):
        hit, row = wanted(table[base + p])

        @pl.when(hit)
        def _():
            note(count, p, row)
            begin(count, p)

        return count + hit.astype(jnp.int32)

    return lax.fori_loop(0, pairs, one, jnp.int32(0))


def padded(count, note, begin, row):
    groups = (count + GROUP - 1) // GROUP
    for q in range(GROUP - 1):

        @pl.when(count + q < groups * GROUP)
        def _():
            note(count + q, 0, row)
            begin(count + q, 0)

    return groups


def group_products(g, listed, left, right, left_buf, right_buf, sems, psi_pairs, sectors):
    at = [g * GROUP + u for u in range(GROUP)]
    for i in at:
        for copy in fetch(left, right, left_buf, right_buf, sems, listed[i], i, sectors):
            copy.wait()
    return at, [
        apply_pair(left_buf[i], right_buf[i], psi_pairs[listed[i] % sectors]) for i in at
    ]


def sibling_kernel(
    rels, depth, table, psi, left, right, out,
    listed, left_buf, right_buf, psi_raw, psi_pairs, results, sems, psi_sem, out_sem,
):
    terms, sectors, m, _ = left.shape
    pairs = terms * sectors
    me, z, y, c = coords(None)
    pltpu.make_async_copy(psi, psi_raw, psi_sem).start()

    def wanted(code):
        inside, core, row = find(code, sectors, depth, z, y, rels)
        return inside & (core != c), row

    def note(i, p, row):
        listed[i] = p

    def begin(i, p):
        for copy in fetch(left, right, left_buf, right_buf, sems, p, i, sectors):
            copy.start()

    count = collect(table, me * pairs, pairs, wanted, note, begin)
    groups = padded(count, note, begin, 0)
    prepare(psi, psi_raw, psi_pairs, psi_sem)
    vectors = psi_raw.shape[1]

    def one(g, carry):
        at, products = group_products(
            g, listed, left, right, left_buf, right_buf, sems, psi_pairs, sectors
        )
        for i, product in zip(at, products):
            for v in range(vectors):
                results[i, v] = product[:, v * m : (v + 1) * m]
        for i in at:

            @pl.when(i < count)
            def _():
                pltpu.make_async_copy(results.at[i], out.at[i], out_sem.at[i]).start()

        return carry

    lax.fori_loop(0, groups, one, 0)

    def finish(i, carry):
        pltpu.make_async_copy(results.at[i], out.at[i], out_sem.at[i]).wait()
        return carry

    lax.fori_loop(0, count, finish, 0)


def dense_kernel(rels, depth, x_count, table, psi, left, right, arrived, *refs):
    terms, sectors, m, _ = left.shape
    vectors = psi.shape[1]
    pairs = terms * sectors
    planes = len(rels)
    out_count = x_count + PLANES + 2 * planes
    outs, refs = refs[:out_count], refs[out_count:]
    (
        listed, rows, rows_in, left_buf, right_buf, psi_raw, psi_pairs, arrivals, total,
        sems, psi_sem, in_sem, out_sems,
    ) = refs
    me, z, y, c = coords(None)
    x = lax.axis_index("ops")
    pltpu.make_async_copy(psi, psi_raw, psi_sem).start()
    pltpu.make_async_copy(arrived, arrivals, in_sem).start()
    target_count = total.shape[0] - 1

    def wanted(code):
        inside, core, row = find(code, sectors, depth, z, y, rels)
        return inside & (core == c), row

    def note(i, p, row):
        listed[i] = p
        rows[i] = row

    def begin(i, p):
        for copy in fetch(left, right, left_buf, right_buf, sems, p, i, sectors):
            copy.start()

    def note_in(i, p, row):
        rows_in[i] = row

    count = collect(table, me * pairs, pairs, wanted, note, begin)
    groups = padded(count, note, begin, target_count)
    sibling = me + 1 - 2 * c
    count_in = collect(table, sibling * pairs, pairs, wanted, note_in, lambda i, p: None)

    def clear(t, carry):
        total[t] = jnp.zeros(total.shape[1:], jnp.float32)
        return carry

    lax.fori_loop(0, target_count + 1, clear, 0)
    prepare(psi, psi_raw, psi_pairs, psi_sem)

    def one(g, carry):
        at, products = group_products(
            g, listed, left, right, left_buf, right_buf, sems, psi_pairs, sectors
        )
        for i, product in zip(at, products):
            row = rows[i]
            for v in range(vectors):
                total[row, v] += product[:, v * m : (v + 1) * m]
        return carry

    lax.fori_loop(0, groups, one, 0)
    pltpu.make_async_copy(arrived, arrivals, in_sem).wait()

    def merge(i, carry):
        total[rows_in[i]] += arrivals[i]
        return carry

    lax.fori_loop(0, count_in, merge, 0)

    first, second = pl.ds(0, sectors // 2), pl.ds(sectors // 2, sectors - sectors // 2)
    height = m // x_count
    copies = []

    def send(piece, iz, iy, which, v, x_rel):
        start = pl.multiple_of(((x + x_rel) % x_count) * height, 8)
        base = (iz * PLANES + iy) * sectors
        local = pl.ds(base + which.start, which.size)
        copies.append(
            pltpu.make_async_copy(
                total.at[local, v, pl.ds(start, height), :], piece, out_sems.at[len(copies)]
            )
        )

    for r in range(x_count):
        for iy in range(PLANES):
            for iz in range(planes):
                send(outs[r].at[iy, iz], iz, iy, first, 0, r)
    for iy in range(PLANES):
        for r in range(x_count):
            for iz in range(planes):
                send(outs[x_count + iy].at[r, iz], iz, iy, second, 0, r)
    for iz in range(planes):
        for r in range(x_count):
            for iy in range(PLANES):
                send(outs[x_count + PLANES + iz].at[r, iy], iz, iy, first, 1, r)
                send(outs[x_count + PLANES + planes + iz].at[iy, r], iz, iy, second, 1, r)
    for copy in copies:
        copy.start()
    for copy in copies:
        copy.wait()


def run_sibling(rels, depth, capacity, table, psi, left, right):
    terms, sectors, m, _ = left.shape
    vectors = psi.shape[1]
    slots = len(rels) * PLANES * capacity
    room = slots + GROUP - 1
    return pl.pallas_call(
        functools.partial(sibling_kernel, rels, depth),
        out_shape=jax.ShapeDtypeStruct((slots, vectors, m, m), jnp.float32),
        in_specs=[pl.BlockSpec(memory_space=pltpu.SMEM)] + [pl.BlockSpec(memory_space=pl.ANY)] * 3,
        out_specs=pl.BlockSpec(memory_space=pl.ANY),
        scratch_shapes=[
            pltpu.SMEM((room,), jnp.int32),
            pltpu.VMEM((room, m, m), jnp.float32),
            pltpu.VMEM((room, m, m), jnp.float32),
            pltpu.VMEM((sectors, vectors, m, m), jnp.float32),
            pltpu.VMEM((sectors, vectors * m, 2 * m), jnp.bfloat16),
            pltpu.VMEM((room, vectors, m, m), jnp.float32),
            pltpu.SemaphoreType.DMA((room, 2)),
            pltpu.SemaphoreType.DMA,
            pltpu.SemaphoreType.DMA((room,)),
        ],
        compiler_params=pltpu.CompilerParams(vmem_limit_bytes=48 << 20),
        name="sibling_contributions",
    )(table, psi, left, right)


def run_dense(rels, depth, capacity, x_count, table, psi, left, right, arrived):
    terms, sectors, m, _ = left.shape
    vectors = psi.shape[1]
    planes = len(rels)
    slots = planes * PLANES * capacity
    room = slots + GROUP - 1
    targets = planes * PLANES * sectors
    half, height = sectors // 2, m // x_count
    shapes = (
        [(PLANES, planes, half, height, m)] * x_count
        + [(x_count, planes, half, height, m)] * PLANES
        + [(x_count, PLANES, half, height, m)] * planes
        + [(PLANES, x_count, half, height, m)] * planes
    )
    pieces = 4 * x_count * PLANES * planes
    return pl.pallas_call(
        functools.partial(dense_kernel, rels, depth, x_count),
        out_shape=[jax.ShapeDtypeStruct(s, jnp.float32) for s in shapes],
        in_specs=[pl.BlockSpec(memory_space=pltpu.SMEM)] + [pl.BlockSpec(memory_space=pl.ANY)] * 4,
        out_specs=[pl.BlockSpec(memory_space=pl.ANY)] * len(shapes),
        scratch_shapes=[
            pltpu.SMEM((room,), jnp.int32),
            pltpu.SMEM((room,), jnp.int32),
            pltpu.SMEM((room,), jnp.int32),
            pltpu.VMEM((room, m, m), jnp.float32),
            pltpu.VMEM((room, m, m), jnp.float32),
            pltpu.VMEM((sectors, vectors, m, m), jnp.float32),
            pltpu.VMEM((sectors, vectors * m, 2 * m), jnp.bfloat16),
            pltpu.VMEM((slots, vectors, m, m), jnp.float32),
            pltpu.VMEM((targets + 1, vectors, m, m), jnp.float32),
            pltpu.SemaphoreType.DMA((room, 2)),
            pltpu.SemaphoreType.DMA,
            pltpu.SemaphoreType.DMA,
            pltpu.SemaphoreType.DMA((pieces,)),
        ],
        compiler_params=pltpu.CompilerParams(vmem_limit_bytes=56 << 20),
        name="dense_sums",
    )(table, psi, left, right, arrived)


def shards(wavefunction, left_blocks, right_blocks, target_owner, target_local):
    sec_count = lax.axis_size("sec")
    x_count = lax.axis_size("ops")
    depth = sec_count // (PLANES * CORES)
    terms, sectors = left_blocks.shape[:2]
    pairs = terms * sectors
    capacity = (pairs + sec_count - 1) // sec_count + 1
    table = (target_owner[0, :, :, :, 0] * sectors + target_local[0]).reshape(sec_count * pairs)

    def at(z, y, c):
        return ((z % depth) * PLANES + y % PLANES) * CORES + c % CORES

    everyone = [(z, y, c) for z in range(depth) for y in range(PLANES) for c in range(CORES)]
    swap_core = [(at(z, y, c), at(z, y, c + 1)) for z, y, c in everyone]
    next_y = [(at(z, y, c), at(z, y + 1, c)) for z, y, c in everyone]
    up = [(at(z, y, c), at(z + 1, y, c)) for z, y, c in everyone]
    down = [(at(z, y, c), at(z - 1, y, c)) for z, y, c in everyone]
    next_x = [(i, (i + 1) % x_count) for i in range(x_count)]

    def ring(parts, axis, steps):
        moving = parts[0]
        for part in parts[1:]:
            moving = lax.ppermute(moving, axis, steps) + part
        return moving

    def over_x(parts):
        return ring([parts[r] for r in range(x_count - 1, -1, -1)], "ops", next_x)

    def over_y(parts):
        return ring([parts[r] for r in range(PLANES - 1, -1, -1)], "sec", next_y)

    def over_z_up(parts):
        return ring([parts[r] for r in range(depth - 1, -1, -1)], "sec", up)

    def over_z_down(parts):
        return ring([parts[r] for r in [*range(1, depth), 0]], "sec", down)

    near = sorted({1 % depth, (depth - 1) % depth} - {0})
    chunks = [c for c in (near, [r for r in range(depth) if r not in near]) if c]
    moved = [
        lax.ppermute(
            run_sibling(rels, depth, capacity, table, wavefunction, left_blocks, right_blocks),
            "sec",
            swap_core,
        )
        for rels in chunks
    ]
    first_a, second_a, first_b, second_b = {}, {}, {}, {}
    for rels, arrived in zip(chunks, moved):
        sums = run_dense(
            rels, depth, capacity, x_count, table, wavefunction, left_blocks, right_blocks, arrived
        )
        planes = len(rels)
        by_x, by_y = sums[:x_count], sums[x_count : x_count + PLANES]
        rest = sums[x_count + PLANES :]
        a1, a2 = over_y(over_x(by_x)), over_x(over_y(by_y))
        for i, r in enumerate(rels):
            first_a[r], second_a[r] = a1[i], a2[i]
            first_b[r], second_b[r] = rest[i], rest[planes + i]
    b1 = over_y(over_x(over_z_up(first_b)))
    b2 = over_x(over_y(over_z_down(second_b)))
    a1, a2 = over_z_up(first_a), over_z_down(second_a)
    return jnp.stack([jnp.concatenate([a1, a2], 0), jnp.concatenate([b1, b2], 0)], axis=1)


def solution(mesh):
    placed = (
        P("sec", None, None, None),
        P("ops", "sec", None, None),
        P("ops", "sec", None, None),
        P("ops", None, None, None, None),
        P("ops", None, None, None),
    )
    return jax.shard_map(
        shards, mesh=mesh, in_specs=placed, out_specs=P("sec", None, "ops", None), check_vma=False
    )
```

time: 354 us -> 166 us (0.47)
  waiting for transfers between devices: 242 us -> 72.2 us
  local copies, waits for them, and re-layouts: 59.9 us -> 6.31 us
  Pallas kernels: 0 us -> 46.7 us
  starting transfers between devices: 7.72 us -> 38.1 us
  matrix products: 28.8 us -> 0 us
  between operations: 13.5 us -> 0.48 us
    all_to_all x1 -> x0, waiting for transfers between devices: 182 us -> none  [shards(): lax.all_to_all(routed, 'sec', split_axis=0, concat_axis=0, tiled=True)]
    ppermute x0 -> x26, waiting for transfers between devices: none -> 72.2 us  [the longest x24 72.2 us: ring(): moving = lax.ppermute(moving, axis, steps) + part]
    unnamed x2 -> x0, waiting for transfers between devices: 60.6 us -> none
    pallas_call x0 -> x4, Pallas kernels: none -> 46.7 us  [the longest x2 26.2 us: run_dense(): pl.pallas_call(functools.partial(dense_kernel, rels, depth, x_count), out...]
    ppermute x0 -> x26, starting transfers between devices: none -> 38.1 us  [the longest x24 35.7 us: ring(): moving = lax.ppermute(moving, axis, steps) + part]
    dot_general x3 -> x0, matrix products: 28.8 us -> none  [the longest x1 10 us: shards(): jnp.einsum('kjab,kjvbd->kjvad', left_blocks, half_applied, precision=exac...]
    scatter x2 -> x0, local copies, waits for them, and re-layouts: 20.5 us -> none  [the longest x1 16.1 us: shards(): jnp.zeros((slot_count, vectors, states, states), jnp.float32).at[send_slot]]
    unnamed x16 -> x31, local copies, waits for them, and re-layouts: 22.8 us -> 5.06 us
  transfers between devices with their start and end apart: 2 -> 26, of which waited for: 2 -> 13; matrix products, arithmetic and copies ran while one was open for 2% -> 1% of each run, Pallas kernels for 0% -> 22%
where the time goes in v1:
time: 166 us
  waiting for transfers between devices  72.2 us (43%)
  Pallas kernels  46.7 us (28%)
  starting transfers between devices  38.1 us (23%)
  local copies, waits for them, and re-layouts  6.31 us (4%)
  other arithmetic  1.75 us (1%)
    ppermute x24, waiting for transfers between devices, ring(): moving = lax.ppermute(moving, axis, steps) + part  72.2 us
    ppermute x24, starting transfers between devices, ring(): moving = lax.ppermute(moving, axis, steps) + part  35.7 us
    pallas_call x2, Pallas kernels, run_dense(): pl.pallas_call(functools.partial(dense_kernel, rels, depth, x_count), out...  26.2 us
    pallas_call x2, Pallas kernels, run_sibling(): pl.pallas_call(functools.partial(sibling_kernel, rels, depth), out_shape=...  20.5 us
    unnamed x31, local copies, waits for them, and re-layouts  5.06 us
  transfers between devices with their start and end apart: 26, of which 13 were waited for; matrix products, arithmetic and copies ran while one was open for 1% of the time, Pallas kernels for 22%

profile of v1, /device:TPU:0, one launch (start us, length us, event | category | flops | bytes accessed | tf_op | source)
XLA Modules:
  0.0 165.5 jit_solution(2318112809577318062)
XLA Ops:
  0.0 0.8 broadcast_multiply_fusion
  0.8 0.1 copy.7
  0.9 0.1 mul.12
  1.0 0.8 copy.8
  1.8 0.1 squeeze.76
  1.9 1.2 copy-done
  3.2 10.9 %sibling_contributions.2 = f32[20,2,128,128]{3,2,1,0:T(8,128)S(1)} custom-call(s32[1024]{0:T(1024)S(1)} %add.76.table, f32[8,2,128,128]{3,2,1,0:T(8,128)S(1)} %copy-done, f32[8,8,128,128]{3,2,1,0:T(8,128)} %left.7, f32[8,8,128,128]{3,2,1,0:T(8,128)} %right.7), custom_call_target="tpu_custom_call" | custom-call | tf_op jit(solution)/shard_map/sibling_contributions/pallas_call | solution.py:269
  14.2 9.5 %sibling_contributions.3 = f32[20,2,128,128]{3,2,1,0:T(8,128)S(1)} custom-call(s32[1024]{0:T(1024)S(1)} %add.76.table, f32[8,2,128,128]{3,2,1,0:T(8,128)S(1)} %copy-done, f32[8,8,128,128]{3,2,1,0:T(8,128)} %left.7, f32[8,8,128,128]{3,2,1,0:T(8,128)} %right.7), custom_call_target="tpu_custom_call" | custom-call | tf_op jit(solution)/shard_map/sibling_contributions/pallas_call | solution.py:269
  23.7 2.3 %collective-permute-start.4 = (f32[20,2,128,128]{3,2,1,0:T(8,128)S(1)}, f32[20,2,128,128]{3,2,1,0:T(8,128)S(1)}, u32[]{:S(2)}, u32[]{:S(2)}) collective-permute-start(f32[20,2,128,128]{3,2,1,0:T(8,128)S(1)} %sibling_contributions.3), channel_id=1, source_target_pairs={{0,1},{1,0},{2,3},{3,2},{4,5},{5,4},{6,7},{7,6},{8,9},{9,8},{10,11... | collective-permute-start | bytes 7864328 | tf_op jit(solution)/shard_map/ppermute | solution.py:370
  26.0 1.5 copy-done.3
  27.5 12.6 %dense_sums.2 = (f32[2,2,4,64,128]{4,3,2,1,0:T(8,128)}, f32[2,2,4,64,128]{4,3,2,1,0:T(8,128)}, f32[2,2,4,64,128]{4,3,2,1,0:T(8,128)}, f32[2,2,4,64,128]{4,3,2,1,...) custom-call(s32[1024]{0:T(1024)} %copy-done.1, ...), custom_call_target="tpu_custom_call" | custom-call | tf_op jit(solution)/shard_map/dense_sums/pallas_call | solution.py:305
  40.1 1.9 %collective-permute-start.1 = (f32[2,2,4,64,128]{4,3,2,1,0:T(8,128)}, f32[2,2,4,64,128]{4,3,2,1,0:T(8,128)S(1)}, u32[]{:S(2)}, u32[]{:S(2)}) collective-permute-start(f32[2,2,4,64,128]{4,3,2,1,0:T(8,128)} %get-tuple-element.21), channel_id=1, source_target_pairs={{0,16},{16,0},{1,17},{17,1},{2,18},{18,2},{3,19},{19,3},{4,20},{20... | collective-permute-start | bytes 1572872 | tf_op jit(solution)/shard_map/ppermute | solution.py:352
  42.1 1.5 collective-permute-start.9
  43.6 1.5 copy-done.2
  45.0 13.6 %dense_sums.3 = (f32[2,2,4,64,128]{4,3,2,1,0:T(8,128)}, f32[2,2,4,64,128]{4,3,2,1,0:T(8,128)}, f32[2,2,4,64,128]{4,3,2,1,0:T(8,128)}, f32[2,2,4,64,128]{4,3,2,1,...) custom-call(s32[1024]{0:T(1024)} %copy-done.1, ...), custom_call_target="tpu_custom_call" | custom-call | tf_op jit(solution)/shard_map/dense_sums/pallas_call | solution.py:305
  58.7 0.3 collective-permute-start.5
  59.0 1.1 collective-permute-start.16
  60.1 2.7 %collective-permute-start.21 = (f32[2,2,4,64,128]{4,3,2,1,0:T(8,128)S(1)}, f32[2,2,4,64,128]{4,3,2,1,0:T(8,128)S(1)}, u32[]{:S(2)}, u32[]{:S(2)}) collective-permute-start(f32[2,2,4,64,128]{4,3,2,1,0:T(8,128)S(1)} %copy-done.14), channel_id=1, source_target_pairs={{0,12},{1,13},{2,14},{3,15},{4,0},{5,1},{6,2},{7,3},{8,4},{9,5},{1... | collective-permute-start | bytes 1572872 | tf_op jit(solution)/shard_map/ppermute | solution.py:352
  62.8 0.7 collective-permute-start.12
  63.6 1.4 collective-permute-start.2
  65.1 6.2 %collective-permute-done.5 = f32[2,2,4,64,128]{4,3,2,1,0:T(8,128)S(1)} collective-permute-done((f32[2,2,4,64,128]{4,3,2,1,0:T(8,128)}, f32[2,2,4,64,128]{4,3,2,1,0:T(8,128)S(1)}, u32[]{:S(2)}, u32[]{:S(2)}) %collective-permute-start.5) | collective-permute-done | bytes 524320 | tf_op jit(solution)/shard_map/ppermute | solution.py:352
  71.3 1.1 collective-permute-start.10
  72.5 5.4 %collective-permute-done.12 = f32[2,2,4,64,128]{4,3,2,1,0:T(8,128)S(1)} collective-permute-done((f32[2,2,4,64,128]{4,3,2,1,0:T(8,128)}, f32[2,2,4,64,128]{4,3,2,1,0:T(8,128)S(1)}, u32[]{:S(2)}, u32[]{:S(2)}) %collective-permute-start.12) | collective-permute-done | bytes 524320 | tf_op jit(solution)/shard_map/ppermute | solution.py:352
  77.9 0.7 collective-permute-start.6
  78.6 1.7 %collective-permute-start.13 = (f32[2,4,64,128]{3,2,1,0:T(8,128)S(1)}, f32[2,4,64,128]{3,2,1,0:T(8,128)S(1)}, u32[]{:S(2)}, u32[]{:S(2)}) collective-permute-start(f32[2,4,64,128]{3,2,1,0:T(8,128)S(1)} %slice_bitcast_fusion.5), channel_id=1, source_target_pairs={{0,16},{16,0},{1,17},{17,1},{2,18},{18,2},{3,19},{19,3},{4,20},{20... | collective-permute-start | bytes 786440 | tf_op jit(solution)/shard_map/ppermute | solution.py:352
  80.4 3.3 %collective-permute-done.21 = f32[2,2,4,64,128]{4,3,2,1,0:T(8,128)S(1)} collective-permute-done((f32[2,2,4,64,128]{4,3,2,1,0:T(8,128)S(1)}, f32[2,2,4,64,128]{4,3,2,1,0:T(8,128)S(1)}, u32[]{:S(2)}, u32[]{:S(2)}) %collective-permute-start.21) | collective-permute-done | bytes 524320 | tf_op jit(solution)/shard_map/ppermute | solution.py:352
  83.8 1.7 %collective-permute-start.17 = (f32[2,2,4,64,128]{4,3,2,1,0:T(8,128)S(1)}, f32[2,2,4,64,128]{4,3,2,1,0:T(8,128)S(1)}, u32[]{:S(2)}, u32[]{:S(2)}) collective-permute-start(f32[2,2,4,64,128]{4,3,2,1,0:T(8,128)S(1)} %add.91), channel_id=1, source_target_pairs={{0,4},{1,5},{2,6},{3,7},{4,8},{5,9},{6,10},{7,11},{8,12},{9,13},{1... | collective-permute-start | bytes 1572872 | tf_op jit(solution)/shard_map/ppermute | solution.py:352
  85.6 2.1 %collective-permute-start.22 = (f32[2,2,4,64,128]{4,3,2,1,0:T(8,128)S(1)}, f32[2,2,4,64,128]{4,3,2,1,0:T(8,128)S(1)}, u32[]{:S(2)}, u32[]{:S(2)}) collective-permute-start(f32[2,2,4,64,128]{4,3,2,1,0:T(8,128)S(1)} %add.96), channel_id=1, source_target_pairs={{0,12},{1,13},{2,14},{3,15},{4,0},{5,1},{6,2},{7,3},{8,4},{9,5},{1... | collective-permute-start | bytes 1572872 | tf_op jit(solution)/shard_map/ppermute | solution.py:352
  87.8 0.1 collective-permute-start.3
  87.9 3.8 %collective-permute-start.11 = (f32[4,64,128]{2,1,0:T(8,128)S(1)}, f32[4,64,128]{2,1,0:T(8,128)S(1)}, u32[]{:S(2)}, u32[]{:S(2)}) collective-permute-start(f32[4,64,128]{2,1,0:T(8,128)S(1)} %slice_bitcast_fusion.19), channel_id=1, source_target_pairs={{0,12},{1,13},{2,14},{3,15},{4,0},{5,1},{6,2},{7,3},{8,4},{9,5},{1... | collective-permute-start | bytes 393224 | tf_op jit(solution)/shard_map/ppermute | solution.py:352
  91.9 21.7 %collective-permute-done.3 = f32[4,64,128]{2,1,0:T(8,128)S(1)} collective-permute-done((f32[4,64,128]{2,1,0:T(8,128)S(1)}, f32[4,64,128]{2,1,0:T(8,128)S(1)}, u32[]{:S(2)}, u32[]{:S(2)}) %collective-permute-start.3) | collective-permute-done | bytes 131104 | tf_op jit(solution)/shard_map/ppermute | solution.py:352
  113.6 0.9 collective-permute-start.7
  114.5 0.8 collective-permute-done.11
  115.4 3.7 %collective-permute-start.14 = (f32[4,64,128]{2,1,0:T(8,128)S(1)}, f32[4,64,128]{2,1,0:T(8,128)S(1)}, u32[]{:S(2)}, u32[]{:S(2)}) collective-permute-start(f32[4,64,128]{2,1,0:T(8,128)S(1)} %fusion.10), channel_id=1, source_target_pairs={{0,12},{1,13},{2,14},{3,15},{4,0},{5,1},{6,2},{7,3},{8,4},{9,5},{1... | collective-permute-start | bytes 393224 | tf_op jit(solution)/shard_map/ppermute | solution.py:352
  119.1 1.6 collective-permute-done.7
  120.9 2.6 %collective-permute-done.14 = f32[4,64,128]{2,1,0:T(8,128)S(1)} collective-permute-done((f32[4,64,128]{2,1,0:T(8,128)S(1)}, f32[4,64,128]{2,1,0:T(8,128)S(1)}, u32[]{:S(2)}, u32[]{:S(2)}) %collective-permute-start.14) | collective-permute-done | bytes 131104 | tf_op jit(solution)/shard_map/ppermute | solution.py:352
  123.5 3.9 %collective-permute-start.15 = (f32[4,64,128]{2,1,0:T(8,128)S(1)}, f32[4,64,128]{2,1,0:T(8,128)S(1)}, u32[]{:S(2)}, u32[]{:S(2)}) collective-permute-start(f32[4,64,128]{2,1,0:T(8,128)S(1)} %fusion.9), channel_id=1, source_target_pairs={{0,12},{1,13},{2,14},{3,15},{4,0},{5,1},{6,2},{7,3},{8,4},{9,5},{1... | collective-permute-start | bytes 393224 | tf_op jit(solution)/shard_map/ppermute | solution.py:352
  127.5 1.5 collective-permute-done.8
  129.1 10.8 %collective-permute-done.15 = f32[4,64,128]{2,1,0:T(8,128)S(1)} collective-permute-done((f32[4,64,128]{2,1,0:T(8,128)S(1)}, f32[4,64,128]{2,1,0:T(8,128)S(1)}, u32[]{:S(2)}, u32[]{:S(2)}) %collective-permute-start.15) | collective-permute-done | bytes 131104 | tf_op jit(solution)/shard_map/ppermute | solution.py:352
  139.9 0.3 collective-permute-done.18
  140.3 2.0 %collective-permute-start.19 = (f32[2,4,64,128]{3,2,1,0:T(8,128)S(1)}, f32[2,4,64,128]{3,2,1,0:T(8,128)S(1)}, u32[]{:S(2)}, u32[]{:S(2)}) collective-permute-start(f32[2,4,64,128]{3,2,1,0:T(8,128)S(1)} %slice_bitcast_fusion.3), channel_id=1, source_target_pairs={{0,16},{16,0},{1,17},{17,1},{2,18},{18,2},{3,19},{19,3},{4,20},{20... | collective-permute-start | bytes 786440 | tf_op jit(solution)/shard_map/ppermute | solution.py:352
  142.3 7.9 %collective-permute-done.23 = f32[2,2,4,64,128]{4,3,2,1,0:T(8,128)S(1)} collective-permute-done((f32[2,2,4,64,128]{4,3,2,1,0:T(8,128)S(1)}, f32[2,2,4,64,128]{4,3,2,1,0:T(8,128)S(1)}, u32[]{:S(2)}, u32[]{:S(2)}) %collective-permute-start.23) | collective-permute-done | bytes 524320 | tf_op jit(solution)/shard_map/ppermute | solution.py:352
  150.3 2.0 %collective-permute-start.24 = (f32[2,4,64,128]{3,2,1,0:T(8,128)S(1)}, f32[2,4,64,128]{3,2,1,0:T(8,128)S(1)}, u32[]{:S(2)}, u32[]{:S(2)}) collective-permute-start(f32[2,4,64,128]{3,2,1,0:T(8,128)S(1)} %slice_bitcast_fusion.1), channel_id=1, source_target_pairs={{0,2},{1,3},{2,0},{3,1},{4,6},{5,7},{6,4},{7,5},{8,10},{9,11},{10,... | collective-permute-start | bytes 786440 | tf_op jit(solution)/shard_map/ppermute | solution.py:352
  152.4 0.1 collective-permute-start.20
  152.5 7.0 %collective-permute-done.24 = f32[2,4,64,128]{3,2,1,0:T(8,128)S(1)} collective-permute-done((f32[2,4,64,128]{3,2,1,0:T(8,128)S(1)}, f32[2,4,64,128]{3,2,1,0:T(8,128)S(1)}, u32[]{:S(2)}, u32[]{:S(2)}) %collective-permute-start.24) | collective-permute-done | bytes 262176 | tf_op jit(solution)/shard_map/ppermute | solution.py:352
  159.5 1.9 %collective-permute-start.25 = (f32[4,64,128]{2,1,0:T(8,128)S(1)}, f32[4,64,128]{2,1,0:T(8,128)S(1)}, u32[]{:S(2)}, u32[]{:S(2)}) collective-permute-start(f32[4,64,128]{2,1,0:T(8,128)S(1)} %slice_bitcast_fusion.13), channel_id=1, source_target_pairs={{0,16},{16,0},{1,17},{17,1},{2,18},{18,2},{3,19},{19,3},{4,20},{20... | collective-permute-start | bytes 393224 | tf_op jit(solution)/shard_map/ppermute | solution.py:352
  161.5 3.1 %collective-permute-done.25 = f32[4,64,128]{2,1,0:T(8,128)S(1)} collective-permute-done((f32[4,64,128]{2,1,0:T(8,128)S(1)}, f32[4,64,128]{2,1,0:T(8,128)S(1)}, u32[]{:S(2)}, u32[]{:S(2)}) %collective-permute-start.25) | collective-permute-done | bytes 131104 | tf_op jit(solution)/shard_map/ppermute | solution.py:352
  164.7 0.8 copy.9
  (82 shorter events, 1.5 us)
Async XLA Ops:
  1.9 1.2 copy-start
  3.2 11.0 %copy-start.1 = (s32[1024]{0:T(1024)}, s32[1024]{0:T(1024)S(1)}, u32[]{:S(2)}) copy-start(s32[1024]{0:T(1024)S(1)} %add.76.table) | copy-start | bytes 12292
  14.1 11.9 %collective-permute-start = (f32[20,2,128,128]{3,2,1,0:T(8,128)S(1)}, f32[20,2,128,128]{3,2,1,0:T(8,128)S(1)}, u32[]{:S(2)}, u32[]{:S(2)}) collective-permute-start(f32[20,2,128,128]{3,2,1,0:T(8,128)S(1)} %sibling_contributions.2), channel_id=1, source_target_pairs={{0,1},{1,0},{2,3},{3,2},{4,5},{5,4},{6,7},{7,6},{8,9},{9,8},{10,11... | collective-permute-start | bytes 7864328 | tf_op jit(solution)/shard_map/ppermute | solution.py:370
  23.7 19.8 %collective-permute-start.4 = (f32[20,2,128,128]{3,2,1,0:T(8,128)S(1)}, f32[20,2,128,128]{3,2,1,0:T(8,128)S(1)}, u32[]{:S(2)}, u32[]{:S(2)}) collective-permute-start(f32[20,2,128,128]{3,2,1,0:T(8,128)S(1)} %sibling_contributions.3), channel_id=1, source_target_pairs={{0,1},{1,0},{2,3},{3,2},{4,5},{5,4},{6,7},{7,6},{8,9},{9,8},{10,11... | collective-permute-start | bytes 7864328 | tf_op jit(solution)/shard_map/ppermute | solution.py:370
  26.0 1.5 copy-start.3
  40.1 22.7 %collective-permute-start.1 = (f32[2,2,4,64,128]{4,3,2,1,0:T(8,128)}, f32[2,2,4,64,128]{4,3,2,1,0:T(8,128)S(1)}, u32[]{:S(2)}, u32[]{:S(2)}) collective-permute-start(f32[2,2,4,64,128]{4,3,2,1,0:T(8,128)} %get-tuple-element.21), channel_id=1, source_target_pairs={{0,16},{16,0},{1,17},{17,1},{2,18},{18,2},{3,19},{19,3},{4,20},{20... | collective-permute-start | bytes 1572872 | tf_op jit(solution)/shard_map/ppermute | solution.py:352
  42.1 18.0 %copy-start.14 = (f32[2,2,4,64,128]{4,3,2,1,0:T(8,128)S(1)}, f32[2,2,4,64,128]{4,3,2,1,0:T(8,128)}, u32[]{:S(2)}) copy-start(f32[2,2,4,64,128]{4,3,2,1,0:T(8,128)} %get-tuple-element.33) | copy-start | bytes 1572868
  42.1 21.4 %copy-start.13 = (f32[2,2,4,64,128]{4,3,2,1,0:T(8,128)S(1)}, f32[2,2,4,64,128]{4,3,2,1,0:T(8,128)}, u32[]{:S(2)}) copy-start(f32[2,2,4,64,128]{4,3,2,1,0:T(8,128)} %get-tuple-element.22) | copy-start | bytes 1572868
  42.1 22.9 %copy-start.11 = (f32[2,2,4,64,128]{4,3,2,1,0:T(8,128)S(1)}, f32[2,2,4,64,128]{4,3,2,1,0:T(8,128)}, u32[]{:S(2)}) copy-start(f32[2,2,4,64,128]{4,3,2,1,0:T(8,128)} %get-tuple-element.26) | copy-start | bytes 1572868
  42.1 21.5 %collective-permute-start.9 = (f32[2,2,4,64,128]{4,3,2,1,0:T(8,128)}, f32[2,2,4,64,128]{4,3,2,1,0:T(8,128)S(1)}, u32[]{:S(2)}, u32[]{:S(2)}) collective-permute-start(f32[2,2,4,64,128]{4,3,2,1,0:T(8,128)} %get-tuple-element.25), channel_id=1, source_target_pairs={{0,2},{1,3},{2,0},{3,1},{4,6},{5,7},{6,4},{7,5},{8,10},{9,11},{10,... | collective-permute-start | bytes 1572872 | tf_op jit(solution)/shard_map/ppermute | solution.py:352
  43.6 1.5 copy-start.2
  58.7 13.7 %copy-start.12 = (f32[2,2,4,64,128]{4,3,2,1,0:T(8,128)S(1)}, f32[2,2,4,64,128]{4,3,2,1,0:T(8,128)}, u32[]{:S(2)}) copy-start(f32[2,2,4,64,128]{4,3,2,1,0:T(8,128)} %get-tuple-element.24) | copy-start | bytes 1572868
  58.7 12.6 %collective-permute-start.5 = (f32[2,2,4,64,128]{4,3,2,1,0:T(8,128)}, f32[2,2,4,64,128]{4,3,2,1,0:T(8,128)S(1)}, u32[]{:S(2)}, u32[]{:S(2)}) collective-permute-start(f32[2,2,4,64,128]{4,3,2,1,0:T(8,128)} %get-tuple-element.23), channel_id=1, source_target_pairs={{0,16},{16,0},{1,17},{17,1},{2,18},{18,2},{3,19},{19,3},{4,20},{20... | collective-permute-start | bytes 1572872 | tf_op jit(solution)/shard_map/ppermute | solution.py:352
  59.0 19.7 %collective-permute-start.16 = (f32[2,2,4,64,128]{4,3,2,1,0:T(8,128)}, f32[2,2,4,64,128]{4,3,2,1,0:T(8,128)S(1)}, u32[]{:S(2)}, u32[]{:S(2)}) collective-permute-start(f32[2,2,4,64,128]{4,3,2,1,0:T(8,128)} %get-tuple-element.29), channel_id=1, source_target_pairs={{0,4},{1,5},{2,6},{3,7},{4,8},{5,9},{6,10},{7,11},{8,12},{9,13},{1... | collective-permute-start | bytes 1572872 | tf_op jit(solution)/shard_map/ppermute | solution.py:352
  60.1 23.7 %collective-permute-start.21 = (f32[2,2,4,64,128]{4,3,2,1,0:T(8,128)S(1)}, f32[2,2,4,64,128]{4,3,2,1,0:T(8,128)S(1)}, u32[]{:S(2)}, u32[]{:S(2)}) collective-permute-start(f32[2,2,4,64,128]{4,3,2,1,0:T(8,128)S(1)} %copy-done.14), channel_id=1, source_target_pairs={{0,12},{1,13},{2,14},{3,15},{4,0},{5,1},{6,2},{7,3},{8,4},{9,5},{1... | collective-permute-start | bytes 1572872 | tf_op jit(solution)/shard_map/ppermute | solution.py:352
  62.8 15.1 %collective-permute-start.12 = (f32[2,2,4,64,128]{4,3,2,1,0:T(8,128)}, f32[2,2,4,64,128]{4,3,2,1,0:T(8,128)S(1)}, u32[]{:S(2)}, u32[]{:S(2)}) collective-permute-start(f32[2,2,4,64,128]{4,3,2,1,0:T(8,128)} %get-tuple-element.27), channel_id=1, source_target_pairs={{0,2},{1,3},{2,0},{3,1},{4,6},{5,7},{6,4},{7,5},{8,10},{9,11},{10,... | collective-permute-start | bytes 1572872 | tf_op jit(solution)/shard_map/ppermute | solution.py:352
  63.5 15.0 %copy-start.10 = (f32[2,2,4,64,128]{4,3,2,1,0:T(8,128)S(1)}, f32[2,2,4,64,128]{4,3,2,1,0:T(8,128)}, u32[]{:S(2)}) copy-start(f32[2,2,4,64,128]{4,3,2,1,0:T(8,128)} %get-tuple-element.28) | copy-start | bytes 1572868
  63.6 22.0 %collective-permute-start.2 = (f32[2,4,64,128]{3,2,1,0:T(8,128)S(1)}, f32[2,4,64,128]{3,2,1,0:T(8,128)S(1)}, u32[]{:S(2)}, u32[]{:S(2)}) collective-permute-start(f32[2,4,64,128]{3,2,1,0:T(8,128)S(1)} %slice_bitcast_fusion.11), channel_id=1, source_target_pairs={{0,2},{1,3},{2,0},{3,1},{4,6},{5,7},{6,4},{7,5},{8,10},{9,11},{10,... | collective-permute-start | bytes 786440 | tf_op jit(solution)/shard_map/ppermute | solution.py:352
  65.1 15.3 %copy-start.9 = (f32[2,2,4,64,128]{4,3,2,1,0:T(8,128)S(1)}, f32[2,2,4,64,128]{4,3,2,1,0:T(8,128)}, u32[]{:S(2)}) copy-start(f32[2,2,4,64,128]{4,3,2,1,0:T(8,128)} %get-tuple-element.30) | copy-start | bytes 1572868
  71.3 16.5 %collective-permute-start.10 = (f32[2,4,64,128]{3,2,1,0:T(8,128)S(1)}, f32[2,4,64,128]{3,2,1,0:T(8,128)S(1)}, u32[]{:S(2)}, u32[]{:S(2)}) collective-permute-start(f32[2,4,64,128]{3,2,1,0:T(8,128)S(1)} %slice_bitcast_fusion.7), channel_id=1, source_target_pairs={{0,16},{16,0},{1,17},{17,1},{2,18},{18,2},{3,19},{19,3},{4,20},{20... | collective-permute-start | bytes 786440 | tf_op jit(solution)/shard_map/ppermute | solution.py:352
  72.4 13.1 %copy-start.8 = (f32[2,2,4,64,128]{4,3,2,1,0:T(8,128)S(1)}, f32[2,2,4,64,128]{4,3,2,1,0:T(8,128)}, u32[]{:S(2)}) copy-start(f32[2,2,4,64,128]{4,3,2,1,0:T(8,128)} %get-tuple-element.34) | copy-start | bytes 1572868
  77.9 10.1 %collective-permute-start.6 = (f32[2,4,64,128]{3,2,1,0:T(8,128)S(1)}, f32[2,4,64,128]{3,2,1,0:T(8,128)S(1)}, u32[]{:S(2)}, u32[]{:S(2)}) collective-permute-start(f32[2,4,64,128]{3,2,1,0:T(8,128)S(1)} %slice_bitcast_fusion.9), channel_id=1, source_target_pairs={{0,2},{1,3},{2,0},{3,1},{4,6},{5,7},{6,4},{7,5},{8,10},{9,11},{10,... | collective-permute-start | bytes 786440 | tf_op jit(solution)/shard_map/ppermute | solution.py:352
  78.6 13.2 %collective-permute-start.13 = (f32[2,4,64,128]{3,2,1,0:T(8,128)S(1)}, f32[2,4,64,128]{3,2,1,0:T(8,128)S(1)}, u32[]{:S(2)}, u32[]{:S(2)}) collective-permute-start(f32[2,4,64,128]{3,2,1,0:T(8,128)S(1)} %slice_bitcast_fusion.5), channel_id=1, source_target_pairs={{0,16},{16,0},{1,17},{17,1},{2,18},{18,2},{3,19},{19,3},{4,20},{20... | collective-permute-start | bytes 786440 | tf_op jit(solution)/shard_map/ppermute | solution.py:352
  83.8 37.0 %collective-permute-start.17 = (f32[2,2,4,64,128]{4,3,2,1,0:T(8,128)S(1)}, f32[2,2,4,64,128]{4,3,2,1,0:T(8,128)S(1)}, u32[]{:S(2)}, u32[]{:S(2)}) collective-permute-start(f32[2,2,4,64,128]{4,3,2,1,0:T(8,128)S(1)} %add.91), channel_id=1, source_target_pairs={{0,4},{1,5},{2,6},{3,7},{4,8},{5,9},{6,10},{7,11},{8,12},{9,13},{1... | collective-permute-start | bytes 1572872 | tf_op jit(solution)/shard_map/ppermute | solution.py:352
  85.6 35.2 %copy-start.7 = (f32[2,2,4,64,128]{4,3,2,1,0:T(8,128)S(1)}, f32[2,2,4,64,128]{4,3,2,1,0:T(8,128)}, u32[]{:S(2)}) copy-start(f32[2,2,4,64,128]{4,3,2,1,0:T(8,128)} %get-tuple-element.31) | copy-start | bytes 1572868
  85.6 41.8 %collective-permute-start.22 = (f32[2,2,4,64,128]{4,3,2,1,0:T(8,128)S(1)}, f32[2,2,4,64,128]{4,3,2,1,0:T(8,128)S(1)}, u32[]{:S(2)}, u32[]{:S(2)}) collective-permute-start(f32[2,2,4,64,128]{4,3,2,1,0:T(8,128)S(1)} %add.96), channel_id=1, source_target_pairs={{0,12},{1,13},{2,14},{3,15},{4,0},{5,1},{6,2},{7,3},{8,4},{9,5},{1... | collective-permute-start | bytes 1572872 | tf_op jit(solution)/shard_map/ppermute | solution.py:352
  87.8 25.8 %collective-permute-start.3 = (f32[4,64,128]{2,1,0:T(8,128)S(1)}, f32[4,64,128]{2,1,0:T(8,128)S(1)}, u32[]{:S(2)}, u32[]{:S(2)}) collective-permute-start(f32[4,64,128]{2,1,0:T(8,128)S(1)} %slice_bitcast_fusion.23), channel_id=1, source_target_pairs={{0,4},{1,5},{2,6},{3,7},{4,8},{5,9},{6,10},{7,11},{8,12},{9,13},{1... | collective-permute-start | bytes 393224 | tf_op jit(solution)/shard_map/ppermute | solution.py:352
  87.9 39.5 %copy-start.6 = (f32[2,2,4,64,128]{4,3,2,1,0:T(8,128)S(1)}, f32[2,2,4,64,128]{4,3,2,1,0:T(8,128)}, u32[]{:S(2)}) copy-start(f32[2,2,4,64,128]{4,3,2,1,0:T(8,128)} %get-tuple-element.35) | copy-start | bytes 1572868
  87.9 27.4 %collective-permute-start.11 = (f32[4,64,128]{2,1,0:T(8,128)S(1)}, f32[4,64,128]{2,1,0:T(8,128)S(1)}, u32[]{:S(2)}, u32[]{:S(2)}) collective-permute-start(f32[4,64,128]{2,1,0:T(8,128)S(1)} %slice_bitcast_fusion.19), channel_id=1, source_target_pairs={{0,12},{1,13},{2,14},{3,15},{4,0},{5,1},{6,2},{7,3},{8,4},{9,5},{1... | collective-permute-start | bytes 393224 | tf_op jit(solution)/shard_map/ppermute | solution.py:352
  113.6 26.6 %copy-start.5 = (f32[2,2,4,64,128]{4,3,2,1,0:T(8,128)S(1)}, f32[2,2,4,64,128]{4,3,2,1,0:T(8,128)}, u32[]{:S(2)}) copy-start(f32[2,2,4,64,128]{4,3,2,1,0:T(8,128)} %get-tuple-element.32) | copy-start | bytes 1572868
  113.6 7.1 %collective-permute-start.7 = (f32[4,64,128]{2,1,0:T(8,128)S(1)}, f32[4,64,128]{2,1,0:T(8,128)S(1)}, u32[]{:S(2)}, u32[]{:S(2)}) collective-permute-start(f32[4,64,128]{2,1,0:T(8,128)S(1)} %fusion.13), channel_id=1, source_target_pairs={{0,4},{1,5},{2,6},{3,7},{4,8},{5,9},{6,10},{7,11},{8,12},{9,13},{1... | collective-permute-start | bytes 393224 | tf_op jit(solution)/shard_map/ppermute | solution.py:352
  115.4 8.1 %collective-permute-start.14 = (f32[4,64,128]{2,1,0:T(8,128)S(1)}, f32[4,64,128]{2,1,0:T(8,128)S(1)}, u32[]{:S(2)}, u32[]{:S(2)}) collective-permute-start(f32[4,64,128]{2,1,0:T(8,128)S(1)} %fusion.10), channel_id=1, source_target_pairs={{0,12},{1,13},{2,14},{3,15},{4,0},{5,1},{6,2},{7,3},{8,4},{9,5},{1... | collective-permute-start | bytes 393224 | tf_op jit(solution)/shard_map/ppermute | solution.py:352
  120.7 8.4 %collective-permute-start.8 = (f32[4,64,128]{2,1,0:T(8,128)S(1)}, f32[4,64,128]{2,1,0:T(8,128)S(1)}, u32[]{:S(2)}, u32[]{:S(2)}) collective-permute-start(f32[4,64,128]{2,1,0:T(8,128)S(1)} %fusion.12), channel_id=1, source_target_pairs={{0,4},{1,5},{2,6},{3,7},{4,8},{5,9},{6,10},{7,11},{8,12},{9,13},{1... | collective-permute-start | bytes 393224 | tf_op jit(solution)/shard_map/ppermute | solution.py:352
  120.8 29.3 %copy-start.4 = (f32[2,2,4,64,128]{4,3,2,1,0:T(8,128)S(1)}, f32[2,2,4,64,128]{4,3,2,1,0:T(8,128)}, u32[]{:S(2)}) copy-start(f32[2,2,4,64,128]{4,3,2,1,0:T(8,128)} %get-tuple-element.36) | copy-start | bytes 1572868
  120.8 19.4 %collective-permute-start.18 = (f32[2,2,4,64,128]{4,3,2,1,0:T(8,128)S(1)}, f32[2,2,4,64,128]{4,3,2,1,0:T(8,128)S(1)}, u32[]{:S(2)}, u32[]{:S(2)}) collective-permute-start(f32[2,2,4,64,128]{4,3,2,1,0:T(8,128)S(1)} %add.92), channel_id=1, source_target_pairs={{0,4},{1,5},{2,6},{3,7},{4,8},{5,9},{6,10},{7,11},{8,12},{9,13},{1... | collective-permute-start | bytes 1572872 | tf_op jit(solution)/shard_map/ppermute | solution.py:352
  123.5 16.4 %collective-permute-start.15 = (f32[4,64,128]{2,1,0:T(8,128)S(1)}, f32[4,64,128]{2,1,0:T(8,128)S(1)}, u32[]{:S(2)}, u32[]{:S(2)}) collective-permute-start(f32[4,64,128]{2,1,0:T(8,128)S(1)} %fusion.9), channel_id=1, source_target_pairs={{0,12},{1,13},{2,14},{3,15},{4,0},{5,1},{6,2},{7,3},{8,4},{9,5},{1... | collective-permute-start | bytes 393224 | tf_op jit(solution)/shard_map/ppermute | solution.py:352
  127.5 22.7 %collective-permute-start.23 = (f32[2,2,4,64,128]{4,3,2,1,0:T(8,128)S(1)}, f32[2,2,4,64,128]{4,3,2,1,0:T(8,128)S(1)}, u32[]{:S(2)}, u32[]{:S(2)}) collective-permute-start(f32[2,2,4,64,128]{4,3,2,1,0:T(8,128)S(1)} %add.97), channel_id=1, source_target_pairs={{0,12},{1,13},{2,14},{3,15},{4,0},{5,1},{6,2},{7,3},{8,4},{9,5},{1... | collective-permute-start | bytes 1572872 | tf_op jit(solution)/shard_map/ppermute | solution.py:352
  140.3 12.0 %collective-permute-start.19 = (f32[2,4,64,128]{3,2,1,0:T(8,128)S(1)}, f32[2,4,64,128]{3,2,1,0:T(8,128)S(1)}, u32[]{:S(2)}, u32[]{:S(2)}) collective-permute-start(f32[2,4,64,128]{3,2,1,0:T(8,128)S(1)} %slice_bitcast_fusion.3), channel_id=1, source_target_pairs={{0,16},{16,0},{1,17},{17,1},{2,18},{18,2},{3,19},{19,3},{4,20},{20... | collective-permute-start | bytes 786440 | tf_op jit(solution)/shard_map/ppermute | solution.py:352
  150.3 9.2 %collective-permute-start.24 = (f32[2,4,64,128]{3,2,1,0:T(8,128)S(1)}, f32[2,4,64,128]{3,2,1,0:T(8,128)S(1)}, u32[]{:S(2)}, u32[]{:S(2)}) collective-permute-start(f32[2,4,64,128]{3,2,1,0:T(8,128)S(1)} %slice_bitcast_fusion.1), channel_id=1, source_target_pairs={{0,2},{1,3},{2,0},{3,1},{4,6},{5,7},{6,4},{7,5},{8,10},{9,11},{10,... | collective-permute-start | bytes 786440 | tf_op jit(solution)/shard_map/ppermute | solution.py:352
  152.4 9.1 %collective-permute-start.20 = (f32[4,64,128]{2,1,0:T(8,128)S(1)}, f32[4,64,128]{2,1,0:T(8,128)S(1)}, u32[]{:S(2)}, u32[]{:S(2)}) collective-permute-start(f32[4,64,128]{2,1,0:T(8,128)S(1)} %slice_bitcast_fusion.15), channel_id=1, source_target_pairs={{0,2},{1,3},{2,0},{3,1},{4,6},{5,7},{6,4},{7,5},{8,10},{9,11},{10,... | collective-permute-start | bytes 393224 | tf_op jit(solution)/shard_map/ppermute | solution.py:352
  159.5 5.0 %collective-permute-start.25 = (f32[4,64,128]{2,1,0:T(8,128)S(1)}, f32[4,64,128]{2,1,0:T(8,128)S(1)}, u32[]{:S(2)}, u32[]{:S(2)}) collective-permute-start(f32[4,64,128]{2,1,0:T(8,128)S(1)} %slice_bitcast_fusion.13), channel_id=1, source_target_pairs={{0,16},{16,0},{1,17},{17,1},{2,18},{18,2},{3,19},{19,3},{4,20},{20... | collective-permute-start | bytes 393224 | tf_op jit(solution)/shard_map/ppermute | solution.py:352

commit v2 on v0

v2 whole, which is shorter than its diff:
```python
import functools

import jax
import jax.numpy as jnp
from jax import lax
from jax.experimental import pallas as pl
from jax.experimental.pallas import tpu as pltpu
from jax.sharding import PartitionSpec as P

CORES = 2
PLANES = 2
MOST_IN_GROUP = 10


def split(x):
    hi = x.astype(jnp.bfloat16)
    lo = (x - hi.astype(jnp.float32)).astype(jnp.bfloat16)
    return hi, lo


def apply_pair(left, right, psi_pair):
    m = left.shape[0]
    right_hi, right_lo = split(right)
    stacked = jnp.concatenate([right_hi, right_lo], axis=0)
    stacked = jnp.concatenate([stacked, stacked], axis=1)
    both = lax.dot_general(
        psi_pair, stacked, (((1,), (1,)), ((), ())), preferred_element_type=jnp.float32
    )
    half = both[:, :m] + both[:, m:]
    vectors = half.shape[0] // m
    half = jnp.concatenate([half[v * m : (v + 1) * m] for v in range(vectors)], axis=1)
    half_hi, half_lo = split(half)
    left_hi, left_lo = split(left)
    left_pair = jnp.concatenate([left_hi, left_lo], axis=1)
    out = jnp.dot(
        left_pair,
        jnp.concatenate([half_hi, half_hi], axis=0),
        preferred_element_type=jnp.float32,
    )
    return out + jnp.dot(left_hi, half_lo, preferred_element_type=jnp.float32)


def prepare(psi, psi_raw, psi_pairs, psi_sem):
    pltpu.make_async_copy(psi, psi_raw, psi_sem).wait()
    sectors, vectors, m, _ = psi_raw.shape

    def one(j, carry):
        hi, lo = split(psi_raw[j].reshape(vectors * m, m))
        psi_pairs[j] = jnp.concatenate([hi, lo], axis=1)
        return carry

    lax.fori_loop(0, sectors, one, 0)


def fetch(left, right, left_buf, right_buf, sems, pair, i, sectors):
    k, j = pair // sectors, pair % sectors
    return (
        pltpu.make_async_copy(left.at[k, j], left_buf.at[i], sems.at[i, 0]),
        pltpu.make_async_copy(right.at[k, j], right_buf.at[i], sems.at[i, 1]),
    )


def collect(codes, base, pairs, low, size, take):
    def one(p, count):
        row = codes[base + p] - low
        hit = (row >= 0) & (row < size)

        @pl.when(hit)
        def _():
            take(count, p, row)

        return count + hit.astype(jnp.int32)

    return lax.fori_loop(0, pairs, one, jnp.int32(0), unroll=4)


def padded(count, group, take, row):
    groups = (count + group - 1) // group

    def one(i, carry):
        take(i, 0, row)
        return carry

    lax.fori_loop(count, groups * group, one, 0)
    return groups


def group_products(g, group, listed, left, right, left_buf, right_buf, sems, psi_pairs, sectors):
    at = [g * group + u for u in range(group)]
    for i in at:
        for copy in fetch(left, right, left_buf, right_buf, sems, listed[i], i, sectors):
            copy.wait()
    return at, [
        apply_pair(left_buf[i], right_buf[i], psi_pairs[listed[i] % sectors]) for i in at
    ]


def sibling_kernel(
    low, size, group, codes, psi, left, right, out,
    listed, left_buf, right_buf, psi_raw, psi_pairs, sems, psi_sem,
):
    terms, sectors, m, _ = left.shape
    vectors = psi.shape[1]
    pltpu.make_async_copy(psi, psi_raw, psi_sem).start()

    def take(i, p, row):
        listed[i] = p
        for copy in fetch(left, right, left_buf, right_buf, sems, p, i, sectors):
            copy.start()

    count = collect(codes, 0, terms * sectors, low, size, take)
    groups = padded(count, group, take, 0)
    prepare(psi, psi_raw, psi_pairs, psi_sem)

    def one(g, carry):
        at, products = group_products(
            g, group, listed, left, right, left_buf, right_buf, sems, psi_pairs, sectors
        )
        for i, product in zip(at, products):
            for v in range(vectors):
                out[i, v] = product[:, v * m : (v + 1) * m]
        return carry

    lax.fori_loop(0, groups, one, 0)


def dense_kernel(
    low, size, group, x_count, codes, psi, left, right, arrived, total,
    listed, rows, rows_in, left_buf, right_buf, psi_raw, psi_pairs, sems, psi_sem,
):
    terms, sectors, m, _ = left.shape
    vectors = psi.shape[1]
    pairs = terms * sectors
    height = m // x_count
    x, core = lax.axis_index("ops"), lax.axis_index("sec") % CORES
    pltpu.make_async_copy(psi, psi_raw, psi_sem).start()

    def take(i, p, row):
        listed[i] = p
        rows[i] = row
        for copy in fetch(left, right, left_buf, right_buf, sems, p, i, sectors):
            copy.start()

    def take_in(i, p, row):
        rows_in[i] = row

    count = collect(codes, 0, pairs, low, size, take)
    groups = padded(count, group, take, size)
    count_in = collect(codes, pairs, pairs, low, size, take_in)

    def clear(t, carry):
        total[t] = jnp.zeros(total.shape[1:], jnp.float32)
        return carry

    lax.fori_loop(0, size // PLANES + 1, clear, 0)
    prepare(psi, psi_raw, psi_pairs, psi_sem)

    def add(code, block):
        row, y_rel = code // PLANES, code % PLANES
        for h in range(x_count):
            x_rel = lax.rem(h - x + x_count, x_count)
            place = x_rel * PLANES + y_rel
            if x_count == PLANES:
                place = jnp.where(core == 0, place, y_rel * PLANES + x_rel)
            for v in range(vectors):
                total[row, v, place] += block(v, h * height)

    def one(g, carry):
        at, products = group_products(
            g, group, listed, left, right, left_buf, right_buf, sems, psi_pairs, sectors
        )
        for i, product in zip(at, products):
            add(rows[i], lambda v, h: product[h : h + height, v * m : (v + 1) * m])
        return carry

    lax.fori_loop(0, groups, one, 0)

    def merge(i, carry):
        add(rows_in[i], lambda v, h: arrived[i, v, h : h + height])
        return carry

    lax.fori_loop(0, count_in, merge, 0)


def group_of(slots):
    return max(d for d in range(1, MOST_IN_GROUP + 1) if slots % d == 0)


def buffers(slots, sectors, vectors, m):
    return [
        pltpu.VMEM((slots, m, m), jnp.float32),
        pltpu.VMEM((slots, m, m), jnp.float32),
        pltpu.VMEM((sectors, vectors, m, m), jnp.float32),
        pltpu.VMEM((sectors, vectors * m, 2 * m), jnp.bfloat16),
        pltpu.SemaphoreType.DMA((slots, 2)),
        pltpu.SemaphoreType.DMA,
    ]


def cost(slots, vectors, m):
    return pl.CostEstimate(
        flops=slots * vectors * 16 * m**3,
        bytes_accessed=slots * (2 + vectors) * m * m * 4,
        transcendentals=0,
    )


def in_hbm(*arrays):
    return [pltpu.with_memory_space_constraint(a, pltpu.HBM) for a in arrays]


def run_sibling(low, size, slots, codes, psi, left, right):
    sectors, m = left.shape[1], left.shape[2]
    vectors = psi.shape[1]
    return pl.pallas_call(
        functools.partial(sibling_kernel, low, size, group_of(slots)),
        out_shape=pltpu.VMEM((slots, vectors, m, m), jnp.float32),
        in_specs=[pl.BlockSpec(memory_space=pltpu.SMEM)] + [pl.BlockSpec(memory_space=pl.ANY)] * 3,
        out_specs=pl.BlockSpec(memory_space=pltpu.VMEM),
        scratch_shapes=[pltpu.SMEM((slots,), jnp.int32), *buffers(slots, sectors, vectors, m)],
        compiler_params=pltpu.CompilerParams(vmem_limit_bytes=24 << 20),
        cost_estimate=cost(slots, vectors, m),
        name="sibling_contributions",
    )(codes, *in_hbm(psi, left, right))


def run_dense(low, size, slots, x_count, codes, psi, left, right, arrived):
    sectors, m = left.shape[1], left.shape[2]
    vectors = psi.shape[1]
    shape = (size // PLANES + 1, vectors, x_count * PLANES, m // x_count, m)
    return pl.pallas_call(
        functools.partial(dense_kernel, low, size, group_of(slots), x_count),
        out_shape=pltpu.VMEM(shape, jnp.float32),
        in_specs=[pl.BlockSpec(memory_space=pltpu.SMEM)]
        + [pl.BlockSpec(memory_space=pl.ANY)] * 3
        + [pl.BlockSpec(memory_space=pltpu.VMEM)],
        out_specs=pl.BlockSpec(memory_space=pltpu.VMEM),
        scratch_shapes=[pltpu.SMEM((slots,), jnp.int32)] * 3
        + buffers(slots, sectors, vectors, m),
        compiler_params=pltpu.CompilerParams(vmem_limit_bytes=32 << 20),
        cost_estimate=cost(slots, vectors, m),
        name="dense_sums",
    )(codes, *in_hbm(psi, left, right), arrived)


def shards(wavefunction, left_blocks, right_blocks, target_owner, target_local):
    sec_count = lax.axis_size("sec")
    x_count = lax.axis_size("ops")
    depth = sec_count // (PLANES * CORES)
    terms, sectors, m, _ = left_blocks.shape
    pairs = terms * sectors
    capacity = (pairs + sec_count - 1) // sec_count + 1
    me = lax.axis_index("sec")
    z, y, c = me // (PLANES * CORES), (me // CORES) % PLANES, me % CORES

    chunks = [list(range(1, depth // 2 + 1)), [*range(depth // 2 + 1, depth), 0]]
    order = [r for chunk in chunks for r in chunk]

    def rows_of(table):
        return jnp.concatenate(
            [lax.dynamic_slice_in_dim(table, d, 1, 0) for d in (me, me + 1 - 2 * c)]
        ).reshape(2 * pairs)

    owner = rows_of(target_owner[0, :, :, :, 0].reshape(sec_count, pairs))
    local = rows_of(target_local[0].reshape(sec_count, pairs))
    z_rel = (owner // (CORES * PLANES) - z + depth) % depth
    z_place = sum(jnp.where(z_rel == r, i, 0) for i, r in enumerate(order))
    y_rel = ((owner // CORES) % PLANES - y + PLANES) % PLANES
    c_rel = (owner % CORES - c + CORES) % CORES
    codes = ((c_rel * depth + z_place) * sectors + local) * PLANES + y_rel

    def at(x, z, y, c):
        place = ((z % depth) * PLANES + y % PLANES) * CORES + c % CORES
        return x % x_count * sec_count + place

    everyone = [
        (x, z, y, c)
        for x in range(x_count)
        for z in range(depth)
        for y in range(PLANES)
        for c in range(CORES)
    ]

    def to(target):
        return [(at(*d), at(*target(*d))) for d in everyone]

    swap_core = to(lambda x, z, y, c: (x, z, y, c + 1))
    next_x = to(lambda x, z, y, c: (x + 1, z, y, c))
    next_y = to(lambda x, z, y, c: (x, z, y + 1, c))
    shift = [to(lambda x, z, y, c, r=r: (x, z + r, y, c)) for r in range(depth)]
    first, second = next_x, next_y
    if x_count == PLANES:
        first = to(lambda x, z, y, c: (x + 1, z, y, c) if c == 0 else (x, z, y + 1, c))
        second = to(lambda x, z, y, c: (x, z, y + 1, c) if c == 0 else (x + 1, z, y, c))

    def send(message, perm):
        return lax.ppermute(message, ("ops", "sec"), perm)

    def ring(parts, perm):
        moving = parts[-1]
        for part in parts[-2::-1]:
            moving = send(moving, perm) + part
        return moving

    def fold_first(sums):
        return ring([sums[:, :, p] for p in range(x_count)], first)

    def fold_second(sums):
        return ring([sums[:, :, q] for q in range(PLANES)], second)

    moved, spans = [], []
    start = 0
    for rels in chunks:
        size = len(rels) * PLANES * sectors
        slots = len(rels) * PLANES * capacity
        low = start * PLANES * sectors
        spans.append((low, size, slots))
        start += len(rels)
        sent = run_sibling(
            low + depth * PLANES * sectors, size, slots, codes,
            wavefunction, left_blocks, right_blocks,
        )
        moved.append(send(sent, swap_core))
    height, cut = m // x_count, sectors - sectors // 4
    early, late = {}, {}
    for rels, arrived, (low, size, slots) in zip(chunks, moved, spans):
        planes = len(rels)
        sums = run_dense(
            low, size, slots, x_count, codes, wavefunction, left_blocks, right_blocks, arrived
        )
        sums = sums[: planes * sectors].reshape(planes, sectors, -1, x_count, PLANES, height, m)
        for i, r in enumerate(rels):
            early[r] = sums[i, cut:, 1][None]
        folded = fold_second(
            fold_first(jnp.concatenate([sums[:, :, 0], sums[:, :cut, 1]], axis=1))
        )
        for i, r in enumerate(rels):
            late[r] = folded[i]
    by_z = [(send(early[r], shift[r]) if r else early[r]) for r in order]
    tail = fold_second(fold_first(sum(by_z[1:], by_z[0])))[0]
    by_z = [(send(late[r], shift[r]) if r else late[r]) for r in order]
    main = sum(by_z[1:], by_z[0])
    return jnp.stack([main[:sectors], jnp.concatenate([main[sectors:], tail])], axis=1)


def solution(mesh):
    placed = (
        P("sec", None, None, None),
        P("ops", "sec", None, None),
        P("ops", "sec", None, None),
        P("ops", None, None, None, None),
        P("ops", None, None, None),
    )
    return jax.shard_map(
        shards, mesh=mesh, in_specs=placed, out_specs=P("sec", None, "ops", None), check_vma=False
    )
```

time: 354 us -> 118 us (0.33)
  waiting for transfers between devices: 242 us -> 66 us
  local copies, waits for them, and re-layouts: 59.9 us -> 3.49 us
  matrix products: 28.8 us -> 0 us
  Pallas kernels: 0 us -> 21.5 us
  starting transfers between devices: 7.72 us -> 23.1 us
  between operations: 13.5 us -> 0.29 us
    all_to_all x1 -> x0, waiting for transfers between devices: 182 us -> none  [shards(): lax.all_to_all(routed, 'sec', split_axis=0, concat_axis=0, tiled=True)]
    ppermute x0 -> x14, waiting for transfers between devices: none -> 66 us  [send(): return lax.ppermute(message, ('ops', 'sec'), perm)]
    unnamed x2 -> x0, waiting for transfers between devices: 60.6 us -> none
    dot_general x3 -> x0, matrix products: 28.8 us -> none  [the longest x1 10 us: shards(): jnp.einsum('kjab,kjvbd->kjvad', left_blocks, half_applied, precision=exac...]
    ppermute x0 -> x14, starting transfers between devices: none -> 23.1 us  [send(): return lax.ppermute(message, ('ops', 'sec'), perm)]
    unnamed x16 -> x7, local copies, waits for them, and re-layouts: 22.8 us -> 0.34 us
    pallas_call x0 -> x4, Pallas kernels: none -> 21.5 us  [the longest x2 11.3 us: run_dense(): pl.pallas_call(functools.partial(dense_kernel, low, size, group_of(slots)...]
    scatter x2 -> x0, local copies, waits for them, and re-layouts: 20.5 us -> none  [the longest x1 16.1 us: shards(): jnp.zeros((slot_count, vectors, states, states), jnp.float32).at[send_slot]]
  transfers between devices with their start and end apart: 2 -> 14, of which waited for: 2 -> 7; matrix products, arithmetic and copies ran while one was open for 2% -> 3% of each run, Pallas kernels for 0% -> 14%
where the time goes in v2:
time: 118 us; the launch traced here: 117 us
  waiting for transfers between devices  66 us (56%)
  starting transfers between devices  23.1 us (20%)
  Pallas kernels  21.5 us (18%)
  local copies, waits for them, and re-layouts  3.49 us (3%)
  other arithmetic  2.55 us (2%)
    ppermute x14, waiting for transfers between devices, send(): return lax.ppermute(message, ('ops', 'sec'), perm)  66 us
    ppermute x14, starting transfers between devices, send(): return lax.ppermute(message, ('ops', 'sec'), perm)  23.1 us
    pallas_call x2, Pallas kernels, run_dense(): pl.pallas_call(functools.partial(dense_kernel, low, size, group_of(slots)...  11.3 us
    pallas_call x2, Pallas kernels, run_sibling(): pl.pallas_call(functools.partial(sibling_kernel, low, size, group_of(slot...  10.3 us
  transfers between devices with their start and end apart: 14, of which 7 were waited for; matrix products, arithmetic and copies ran while one was open for 3% of the time, Pallas kernels for 14%

profile of v2, /device:TPU:0, one launch (start us, length us, event | category | flops | bytes accessed | tf_op | source)
XLA Modules:
  0.0 117.0 jit_solution(14934941926702025872)
XLA Ops:
  0.0 0.9 constant_dynamic-slice_fusion.1
  0.9 0.1 copy.21
  1.0 0.1 copy.22
  1.1 0.1 reshape.13
  1.2 0.1 copy.20
  1.4 0.1 reshape.12
  1.5 5.1 %sibling_contributions.2 = f32[20,2,128,128]{3,2,1,0:T(8,128)S(1)} custom-call(s32[128]{0:T(128)S(1)} %fusion.15.codes, f32[8,2,128,128]{3,2,1,0:T(8,128)} %psi.7, f32[8,8,128,128]{3,2,1,0:T(8,128)} %left.7, f32[8,8,128,128]{3,2,1,0:T(8,128)} %right.7), custom_call_target="tpu_custom_call" | custom-call | flops 1342177280 | bytes 5242880 | tf_op jit(solution)/shard_map/sibling_contributions/pallas_call | solution.py:215
  6.6 0.5 collective-permute-start
  7.1 5.1 %sibling_contributions.3 = f32[20,2,128,128]{3,2,1,0:T(8,128)S(1)} custom-call(s32[128]{0:T(128)S(1)} %fusion.15.codes, f32[8,2,128,128]{3,2,1,0:T(8,128)} %psi.7, f32[8,8,128,128]{3,2,1,0:T(8,128)} %left.7, f32[8,8,128,128]{3,2,1,0:T(8,128)} %right.7), custom_call_target="tpu_custom_call" | custom-call | flops 1342177280 | bytes 5242880 | tf_op jit(solution)/shard_map/sibling_contributions/pallas_call | solution.py:215
  12.3 0.2 collective-permute-start.5
  12.4 5.6 %dense_sums.2 = f32[17,2,4,64,128]{4,3,2,1,0:T(8,128)S(1)} custom-call(s32[128]{0:T(128)S(1)} %fusion.15.codes, f32[8,2,128,128]{3,2,1,0:T(8,128)} %psi.7, f32[8,8,128,128]{3,2,1,0:T(8,128)} %left.7, f32[8,8,128,128]{3,2,1,0:T(8,128)} %right.7, f32[20,2,128,128]{3,2,1,0:T(8,128)S(1)} %collective-permute-done.arrived), custom_call_target="tpu_custom_call" | custom-call | flops 1342177280 | bytes 5242880 | tf_op jit(solution)/shard_map/dense_sums/pallas_call | solution.py:231
  18.1 0.5 slice.112
  18.6 0.2 copy_bitcast_fusion.3
  18.8 0.2 copy_bitcast_fusion.1
  19.0 0.2 fusion.3
  19.2 3.1 %collective-permute-start.1 = (f32[2,14,2,64,128]{4,3,1,0,2:T(8,128)S(1)}, f32[2,14,2,64,128]{4,3,1,0,2:T(8,128)S(1)}, u32[]{:S(2)}, u32[]{:S(2)}) collective-permute-start(f32[2,14,2,64,128]{4,3,1,0,2:T(8,128)S(1)} %fusion.3), channel_id=1, source_target_pairs={{0,16},{1,3},{2,18},{3,1},{4,20},{5,7},{6,22},{7,5},{8,24},{9,11},... | collective-permute-start | bytes 5505032 | tf_op jit(solution)/shard_map/ppermute | solution.py:297
  22.3 5.6 %dense_sums.3 = f32[17,2,4,64,128]{4,3,2,1,0:T(8,128)S(1)} custom-call(s32[128]{0:T(128)S(1)} %fusion.15.codes, f32[8,2,128,128]{3,2,1,0:T(8,128)} %psi.7, f32[8,8,128,128]{3,2,1,0:T(8,128)} %left.7, f32[8,8,128,128]{3,2,1,0:T(8,128)} %right.7, f32[20,2,128,128]{3,2,1,0:T(8,128)S(1)} %collective-permute-done.5.arrived), custom_call_target="tpu_custom_call" | custom-call | flops 1342177280 | bytes 5242880 | tf_op jit(solution)/shard_map/dense_sums/pallas_call | solution.py:231
  27.9 0.3 slice.121
  28.3 0.2 copy_bitcast_fusion.2
  28.4 0.2 copy_bitcast_fusion
  28.7 0.2 fusion.1
  28.9 0.1 collective-permute-start.6
  29.1 2.1 %collective-permute-start.9 = (f32[1,2,2,2,64,128]{5,4,1,3,2,0:T(8,128)S(1)}, f32[1,2,2,2,64,128]{5,4,1,3,2,0:T(8,128)S(1)}, u32[]{:S(2)}, u32[]{:S(2)}) collective-permute-start(f32[1,2,2,2,64,128]{5,4,1,3,2,0:T(8,128)S(1)} %bitcast.88), channel_id=1, source_target_pairs={{0,4},{1,5},{2,6},{3,7},{4,8},{5,9},{6,10},{7,11},{8,12},{9,13},{1... | collective-permute-start | bytes 786440 | tf_op jit(solution)/shard_map/ppermute | solution.py:297
  31.2 2.6 %collective-permute-start.10 = (f32[1,2,2,2,64,128]{5,4,1,3,2,0:T(8,128)S(1)}, f32[1,2,2,2,64,128]{5,4,1,3,2,0:T(8,128)S(1)}, u32[]{:S(2)}, u32[]{:S(2)}) collective-permute-start(f32[1,2,2,2,64,128]{5,4,1,3,2,0:T(8,128)S(1)} %bitcast.87), channel_id=1, source_target_pairs={{0,8},{1,9},{2,10},{3,11},{4,12},{5,13},{6,14},{7,15},{8,0},{9,1},... | collective-permute-start | bytes 786440 | tf_op jit(solution)/shard_map/ppermute | solution.py:297
  33.8 1.5 %collective-permute-start.11 = (f32[1,2,2,2,64,128]{5,4,1,3,2,0:T(8,128)S(1)}, f32[1,2,2,2,64,128]{5,4,1,3,2,0:T(8,128)S(1)}, u32[]{:S(2)}, u32[]{:S(2)}) collective-permute-start(f32[1,2,2,2,64,128]{5,4,1,3,2,0:T(8,128)S(1)} %bitcast.89), channel_id=1, source_target_pairs={{0,12},{1,13},{2,14},{3,15},{4,0},{5,1},{6,2},{7,3},{8,4},{9,5},{1... | collective-permute-start | bytes 786440 | tf_op jit(solution)/shard_map/ppermute | solution.py:297
  35.3 5.2 %collective-permute-done.9 = f32[1,2,2,2,64,128]{5,4,1,3,2,0:T(8,128)S(1)} collective-permute-done((f32[1,2,2,2,64,128]{5,4,1,3,2,0:T(8,128)S(1)}, f32[1,2,2,2,64,128]{5,4,1,3,2,0:T(8,128)S(1)}, u32[]{:S(2)}, u32[]{:S(2)}) %collective-permute-start.9) | collective-permute-done | bytes 262176 | tf_op jit(solution)/shard_map/ppermute | solution.py:297
  40.5 10.0 %collective-permute-done.10 = f32[1,2,2,2,64,128]{5,4,1,3,2,0:T(8,128)S(1)} collective-permute-done((f32[1,2,2,2,64,128]{5,4,1,3,2,0:T(8,128)S(1)}, f32[1,2,2,2,64,128]{5,4,1,3,2,0:T(8,128)S(1)}, u32[]{:S(2)}, u32[]{:S(2)}) %collective-permute-start.10) | collective-permute-done | bytes 262176 | tf_op jit(solution)/shard_map/ppermute | solution.py:297
  50.6 1.6 %collective-permute-start.12 = (f32[1,2,2,64,128]{4,3,1,2,0:T(8,128)S(1)}, f32[1,2,2,64,128]{4,3,1,2,0:T(8,128)S(1)}, u32[]{:S(2)}, u32[]{:S(2)}) collective-permute-start(f32[1,2,2,64,128]{4,3,1,2,0:T(8,128)S(1)} %slice_bitcast_fusion.10), channel_id=1, source_target_pairs={{0,16},{1,3},{2,18},{3,1},{4,20},{5,7},{6,22},{7,5},{8,24},{9,11},... | collective-permute-start | bytes 393224 | tf_op jit(solution)/shard_map/ppermute | solution.py:297
  52.2 0.4 fusion.7
  52.6 0.1 slice_bitcast_fusion.3
  52.7 1.5 %collective-permute-start.2 = (f32[2,14,64,128]{3,2,1,0:T(8,128)S(1)}, f32[2,14,64,128]{3,2,1,0:T(8,128)S(1)}, u32[]{:S(2)}, u32[]{:S(2)}) collective-permute-start(f32[2,14,64,128]{3,2,1,0:T(8,128)S(1)} %slice_bitcast_fusion.3), channel_id=1, source_target_pairs={{0,2},{1,17},{2,0},{3,19},{4,6},{5,21},{6,4},{7,23},{8,10},{9,25},... | collective-permute-start | bytes 2752520 | tf_op jit(solution)/shard_map/ppermute | solution.py:297
  54.2 17.1 %collective-permute-done.6 = f32[2,14,2,64,128]{4,3,1,0,2:T(8,128)S(1)} collective-permute-done((f32[2,14,2,64,128]{4,3,1,0,2:T(8,128)S(1)}, f32[2,14,2,64,128]{4,3,1,0,2:T(8,128)S(1)}, u32[]{:S(2)}, u32[]{:S(2)}) %collective-permute-start.6) | collective-permute-done | bytes 1835040 | tf_op jit(solution)/shard_map/ppermute | solution.py:297
  71.3 0.3 fusion.5
  71.7 0.1 slice_bitcast_fusion.1
  71.8 3.5 %collective-permute-start.7 = (f32[2,14,64,128]{3,2,1,0:T(8,128)S(1)}, f32[2,14,64,128]{3,2,1,0:T(8,128)S(1)}, u32[]{:S(2)}, u32[]{:S(2)}) collective-permute-start(f32[2,14,64,128]{3,2,1,0:T(8,128)S(1)} %slice_bitcast_fusion.1), channel_id=1, source_target_pairs={{0,2},{1,17},{2,0},{3,19},{4,6},{5,21},{6,4},{7,23},{8,10},{9,25},... | collective-permute-start | bytes 2752520 | tf_op jit(solution)/shard_map/ppermute | solution.py:297
  75.3 0.1 fusion.9
  75.4 0.1 slice_bitcast_fusion.6
  75.5 1.3 %collective-permute-start.4 = (f32[14,64,128]{2,1,0:T(8,128)S(1)}, f32[14,64,128]{2,1,0:T(8,128)S(1)}, u32[]{:S(2)}, u32[]{:S(2)}) collective-permute-start(f32[14,64,128]{2,1,0:T(8,128)S(1)} %get-tuple-element.9), channel_id=1, source_target_pairs={{0,8},{1,9},{2,10},{3,11},{4,12},{5,13},{6,14},{7,15},{8,0},{9,1},... | collective-permute-start | bytes 1376264 | tf_op jit(solution)/shard_map/ppermute | solution.py:297
  76.8 1.6 %collective-permute-start.3 = (f32[14,64,128]{2,1,0:T(8,128)S(1)}, f32[14,64,128]{2,1,0:T(8,128)S(1)}, u32[]{:S(2)}, u32[]{:S(2)}) collective-permute-start(f32[14,64,128]{2,1,0:T(8,128)S(1)} %get-tuple-element.10), channel_id=1, source_target_pairs={{0,4},{1,5},{2,6},{3,7},{4,8},{5,9},{6,10},{7,11},{8,12},{9,13},{1... | collective-permute-start | bytes 1376264 | tf_op jit(solution)/shard_map/ppermute | solution.py:297
  78.4 8.3 %collective-permute-done.7 = f32[2,14,64,128]{3,2,1,0:T(8,128)S(1)} collective-permute-done((f32[2,14,64,128]{3,2,1,0:T(8,128)S(1)}, f32[2,14,64,128]{3,2,1,0:T(8,128)S(1)}, u32[]{:S(2)}, u32[]{:S(2)}) %collective-permute-start.7) | collective-permute-done | bytes 917536 | tf_op jit(solution)/shard_map/ppermute | solution.py:297
  86.6 0.1 fusion.8
  86.8 1.7 %collective-permute-start.8 = (f32[14,64,128]{2,1,0:T(8,128)S(1)}, f32[14,64,128]{2,1,0:T(8,128)S(1)}, u32[]{:S(2)}, u32[]{:S(2)}) collective-permute-start(f32[14,64,128]{2,1,0:T(8,128)S(1)} %slice_bitcast_fusion.5), channel_id=1, source_target_pairs={{0,12},{1,13},{2,14},{3,15},{4,0},{5,1},{6,2},{7,3},{8,4},{9,5},{1... | collective-permute-start | bytes 1376264 | tf_op jit(solution)/shard_map/ppermute | solution.py:297
  88.5 2.0 %collective-permute-start.13 = (f32[1,2,64,128]{3,2,1,0:T(8,128)S(1)}, f32[1,2,64,128]{3,2,1,0:T(8,128)S(1)}, u32[]{:S(2)}, u32[]{:S(2)}) collective-permute-start(f32[1,2,64,128]{3,2,1,0:T(8,128)S(1)} %slice_bitcast_fusion.12), channel_id=1, source_target_pairs={{0,2},{1,17},{2,0},{3,19},{4,6},{5,21},{6,4},{7,23},{8,10},{9,25},... | collective-permute-start | bytes 196616 | tf_op jit(solution)/shard_map/ppermute | solution.py:297
  90.5 2.2 %collective-permute-done.13 = f32[1,2,64,128]{3,2,1,0:T(8,128)S(1)} collective-permute-done((f32[1,2,64,128]{3,2,1,0:T(8,128)S(1)}, f32[1,2,64,128]{3,2,1,0:T(8,128)S(1)}, u32[]{:S(2)}, u32[]{:S(2)}) %collective-permute-start.13) | collective-permute-done | bytes 65568 | tf_op jit(solution)/shard_map/ppermute | solution.py:297
  92.8 16.6 %collective-permute-done.4 = f32[14,64,128]{2,1,0:T(8,128)S(1)} collective-permute-done((f32[14,64,128]{2,1,0:T(8,128)S(1)}, f32[14,64,128]{2,1,0:T(8,128)S(1)}, u32[]{:S(2)}, u32[]{:S(2)}) %collective-permute-start.4) | collective-permute-done | bytes 458784 | tf_op jit(solution)/shard_map/ppermute | solution.py:297
  109.4 6.6 %collective-permute-done.8 = f32[14,64,128]{2,1,0:T(8,128)S(1)} collective-permute-done((f32[14,64,128]{2,1,0:T(8,128)S(1)}, f32[14,64,128]{2,1,0:T(8,128)S(1)}, u32[]{:S(2)}, u32[]{:S(2)}) %collective-permute-start.8) | collective-permute-done | bytes 458784 | tf_op jit(solution)/shard_map/ppermute | solution.py:297
  116.0 0.1 fusion.10
  116.2 0.8 pad_maximum_fusion.2
  (25 shorter events, 0.5 us)
Async XLA Ops:
  6.6 5.8 %collective-permute-start = (f32[20,2,128,128]{3,2,1,0:T(8,128)S(1)}, f32[20,2,128,128]{3,2,1,0:T(8,128)S(1)}, u32[]{:S(2)}, u32[]{:S(2)}) collective-permute-start(f32[20,2,128,128]{3,2,1,0:T(8,128)S(1)} %sibling_contributions.2), channel_id=1, source_target_pairs={{0,1},{1,0},{2,3},{3,2},{4,5},{5,4},{6,7},{7,6},{8,9},{9,8},{10,11... | collective-permute-start | bytes 7864328 | tf_op jit(solution)/shard_map/ppermute | solution.py:297
  12.3 10.0 %collective-permute-start.5 = (f32[20,2,128,128]{3,2,1,0:T(8,128)S(1)}, f32[20,2,128,128]{3,2,1,0:T(8,128)S(1)}, u32[]{:S(2)}, u32[]{:S(2)}) collective-permute-start(f32[20,2,128,128]{3,2,1,0:T(8,128)S(1)} %sibling_contributions.3), channel_id=1, source_target_pairs={{0,1},{1,0},{2,3},{3,2},{4,5},{5,4},{6,7},{7,6},{8,9},{9,8},{10,11... | collective-permute-start | bytes 7864328 | tf_op jit(solution)/shard_map/ppermute | solution.py:297
  19.2 33.0 %collective-permute-start.1 = (f32[2,14,2,64,128]{4,3,1,0,2:T(8,128)S(1)}, f32[2,14,2,64,128]{4,3,1,0,2:T(8,128)S(1)}, u32[]{:S(2)}, u32[]{:S(2)}) collective-permute-start(f32[2,14,2,64,128]{4,3,1,0,2:T(8,128)S(1)} %fusion.3), channel_id=1, source_target_pairs={{0,16},{1,3},{2,18},{3,1},{4,20},{5,7},{6,22},{7,5},{8,24},{9,11},... | collective-permute-start | bytes 5505032 | tf_op jit(solution)/shard_map/ppermute | solution.py:297
  28.9 42.5 %collective-permute-start.6 = (f32[2,14,2,64,128]{4,3,1,0,2:T(8,128)S(1)}, f32[2,14,2,64,128]{4,3,1,0,2:T(8,128)S(1)}, u32[]{:S(2)}, u32[]{:S(2)}) collective-permute-start(f32[2,14,2,64,128]{4,3,1,0,2:T(8,128)S(1)} %fusion.1), channel_id=1, source_target_pairs={{0,16},{1,3},{2,18},{3,1},{4,20},{5,7},{6,22},{7,5},{8,24},{9,11},... | collective-permute-start | bytes 5505032 | tf_op jit(solution)/shard_map/ppermute | solution.py:297
  29.1 11.4 %collective-permute-start.9 = (f32[1,2,2,2,64,128]{5,4,1,3,2,0:T(8,128)S(1)}, f32[1,2,2,2,64,128]{5,4,1,3,2,0:T(8,128)S(1)}, u32[]{:S(2)}, u32[]{:S(2)}) collective-permute-start(f32[1,2,2,2,64,128]{5,4,1,3,2,0:T(8,128)S(1)} %bitcast.88), channel_id=1, source_target_pairs={{0,4},{1,5},{2,6},{3,7},{4,8},{5,9},{6,10},{7,11},{8,12},{9,13},{1... | collective-permute-start | bytes 786440 | tf_op jit(solution)/shard_map/ppermute | solution.py:297
  31.2 19.3 %collective-permute-start.10 = (f32[1,2,2,2,64,128]{5,4,1,3,2,0:T(8,128)S(1)}, f32[1,2,2,2,64,128]{5,4,1,3,2,0:T(8,128)S(1)}, u32[]{:S(2)}, u32[]{:S(2)}) collective-permute-start(f32[1,2,2,2,64,128]{5,4,1,3,2,0:T(8,128)S(1)} %bitcast.87), channel_id=1, source_target_pairs={{0,8},{1,9},{2,10},{3,11},{4,12},{5,13},{6,14},{7,15},{8,0},{9,1},... | collective-permute-start | bytes 786440 | tf_op jit(solution)/shard_map/ppermute | solution.py:297
  33.8 16.7 %collective-permute-start.11 = (f32[1,2,2,2,64,128]{5,4,1,3,2,0:T(8,128)S(1)}, f32[1,2,2,2,64,128]{5,4,1,3,2,0:T(8,128)S(1)}, u32[]{:S(2)}, u32[]{:S(2)}) collective-permute-start(f32[1,2,2,2,64,128]{5,4,1,3,2,0:T(8,128)S(1)} %bitcast.89), channel_id=1, source_target_pairs={{0,12},{1,13},{2,14},{3,15},{4,0},{5,1},{6,2},{7,3},{8,4},{9,5},{1... | collective-permute-start | bytes 786440 | tf_op jit(solution)/shard_map/ppermute | solution.py:297
  50.6 24.7 %collective-permute-start.12 = (f32[1,2,2,64,128]{4,3,1,2,0:T(8,128)S(1)}, f32[1,2,2,64,128]{4,3,1,2,0:T(8,128)S(1)}, u32[]{:S(2)}, u32[]{:S(2)}) collective-permute-start(f32[1,2,2,64,128]{4,3,1,2,0:T(8,128)S(1)} %slice_bitcast_fusion.10), channel_id=1, source_target_pairs={{0,16},{1,3},{2,18},{3,1},{4,20},{5,7},{6,22},{7,5},{8,24},{9,11},... | collective-permute-start | bytes 393224 | tf_op jit(solution)/shard_map/ppermute | solution.py:297
  52.7 22.6 %collective-permute-start.2 = (f32[2,14,64,128]{3,2,1,0:T(8,128)S(1)}, f32[2,14,64,128]{3,2,1,0:T(8,128)S(1)}, u32[]{:S(2)}, u32[]{:S(2)}) collective-permute-start(f32[2,14,64,128]{3,2,1,0:T(8,128)S(1)} %slice_bitcast_fusion.3), channel_id=1, source_target_pairs={{0,2},{1,17},{2,0},{3,19},{4,6},{5,21},{6,4},{7,23},{8,10},{9,25},... | collective-permute-start | bytes 2752520 | tf_op jit(solution)/shard_map/ppermute | solution.py:297
  71.8 14.9 %collective-permute-start.7 = (f32[2,14,64,128]{3,2,1,0:T(8,128)S(1)}, f32[2,14,64,128]{3,2,1,0:T(8,128)S(1)}, u32[]{:S(2)}, u32[]{:S(2)}) collective-permute-start(f32[2,14,64,128]{3,2,1,0:T(8,128)S(1)} %slice_bitcast_fusion.1), channel_id=1, source_target_pairs={{0,2},{1,17},{2,0},{3,19},{4,6},{5,21},{6,4},{7,23},{8,10},{9,25},... | collective-permute-start | bytes 2752520 | tf_op jit(solution)/shard_map/ppermute | solution.py:297
  75.5 33.8 %collective-permute-start.4 = (f32[14,64,128]{2,1,0:T(8,128)S(1)}, f32[14,64,128]{2,1,0:T(8,128)S(1)}, u32[]{:S(2)}, u32[]{:S(2)}) collective-permute-start(f32[14,64,128]{2,1,0:T(8,128)S(1)} %get-tuple-element.9), channel_id=1, source_target_pairs={{0,8},{1,9},{2,10},{3,11},{4,12},{5,13},{6,14},{7,15},{8,0},{9,1},... | collective-permute-start | bytes 1376264 | tf_op jit(solution)/shard_map/ppermute | solution.py:297
  76.8 32.5 %collective-permute-start.3 = (f32[14,64,128]{2,1,0:T(8,128)S(1)}, f32[14,64,128]{2,1,0:T(8,128)S(1)}, u32[]{:S(2)}, u32[]{:S(2)}) collective-permute-start(f32[14,64,128]{2,1,0:T(8,128)S(1)} %get-tuple-element.10), channel_id=1, source_target_pairs={{0,4},{1,5},{2,6},{3,7},{4,8},{5,9},{6,10},{7,11},{8,12},{9,13},{1... | collective-permute-start | bytes 1376264 | tf_op jit(solution)/shard_map/ppermute | solution.py:297
  86.8 29.1 %collective-permute-start.8 = (f32[14,64,128]{2,1,0:T(8,128)S(1)}, f32[14,64,128]{2,1,0:T(8,128)S(1)}, u32[]{:S(2)}, u32[]{:S(2)}) collective-permute-start(f32[14,64,128]{2,1,0:T(8,128)S(1)} %slice_bitcast_fusion.5), channel_id=1, source_target_pairs={{0,12},{1,13},{2,14},{3,15},{4,0},{5,1},{6,2},{7,3},{8,4},{9,5},{1... | collective-permute-start | bytes 1376264 | tf_op jit(solution)/shard_map/ppermute | solution.py:297
  88.5 4.3 %collective-permute-start.13 = (f32[1,2,64,128]{3,2,1,0:T(8,128)S(1)}, f32[1,2,64,128]{3,2,1,0:T(8,128)S(1)}, u32[]{:S(2)}, u32[]{:S(2)}) collective-permute-start(f32[1,2,64,128]{3,2,1,0:T(8,128)S(1)} %slice_bitcast_fusion.12), channel_id=1, source_target_pairs={{0,2},{1,17},{2,0},{3,19},{4,6},{5,21},{6,4},{7,23},{8,10},{9,25},... | collective-permute-start | bytes 196616 | tf_op jit(solution)/shard_map/ppermute | solution.py:297

commit v3 on v2

--- a/solution.py
+++ b/solution.py
@@ -149,7 +149,7 @@
     count_in = collect(codes, pairs, pairs, low, size, take_in)
 
     def clear(t, carry):
-        total[t] = jnp.zeros(total.shape[1:], jnp.float32)
+        total[t // sectors, t % sectors] = jnp.zeros(total.shape[2:], jnp.float32)
         return carry
 
     lax.fori_loop(0, size // PLANES + 1, clear, 0)
@@ -157,13 +157,14 @@
 
     def add(code, block):
         row, y_rel = code // PLANES, code % PLANES
+        plane, local = row // sectors, row % sectors
         for h in range(x_count):
             x_rel = lax.rem(h - x + x_count, x_count)
             place = x_rel * PLANES + y_rel
             if x_count == PLANES:
                 place = jnp.where(core == 0, place, y_rel * PLANES + x_rel)
             for v in range(vectors):
-                total[row, v, place] += block(v, h * height)
+                total[plane, local, v, place] += block(v, h * height)
 
     def one(g, carry):
         at, products = group_products(
@@ -227,7 +228,8 @@
 def run_dense(low, size, slots, x_count, codes, psi, left, right, arrived):
     sectors, m = left.shape[1], left.shape[2]
     vectors = psi.shape[1]
-    shape = (size // PLANES + 1, vectors, x_count * PLANES, m // x_count, m)
+    planes = size // (PLANES * sectors)
+    shape = (planes + 1, sectors, vectors, x_count * PLANES, m // x_count, m)
     return pl.pallas_call(
         functools.partial(dense_kernel, low, size, group_of(slots), x_count),
         out_shape=pltpu.VMEM(shape, jnp.float32),
@@ -253,7 +255,7 @@
     me = lax.axis_index("sec")
     z, y, c = me // (PLANES * CORES), (me // CORES) % PLANES, me % CORES
 
-    chunks = [list(range(1, depth // 2 + 1)), [*range(depth // 2 + 1, depth), 0]]
+    chunks = [list(range(depth // 2, 0, -1)), [*range(depth // 2 + 1, depth), 0]]
     order = [r for chunk in chunks for r in chunk]
 
     def rows_of(table):
@@ -296,51 +298,63 @@
     def send(message, perm):
         return lax.ppermute(message, ("ops", "sec"), perm)
 
-    def ring(parts, perm):
+    def ring(parts, perm, *done):
         moving = parts[-1]
         for part in parts[-2::-1]:
-            moving = send(moving, perm) + part
+            moving = after(send(moving, perm), *done) + part
         return moving
 
-    def fold_first(sums):
-        return ring([sums[:, :, p] for p in range(x_count)], first)
+    def fold_first(sums, *done):
+        parts = [sums[:, p * PLANES : (p + 1) * PLANES] for p in range(x_count)]
+        return ring(parts, first, *done)
 
     def fold_second(sums):
-        return ring([sums[:, :, q] for q in range(PLANES)], second)
-
-    moved, spans = [], []
+        return ring([sums[:, q] for q in range(PLANES)], second)
+
+    def after(value, *done):
+        return lax.optimization_barrier((value, done))[0]
+
+    arrays = (wavefunction, left_blocks, right_blocks)
+    spans, sent = [], []
     start = 0
     for rels in chunks:
-        size = len(rels) * PLANES * sectors
-        slots = len(rels) * PLANES * capacity
-        low = start * PLANES * sectors
-        spans.append((low, size, slots))
+        span = [PLANES * n for n in (start * sectors, len(rels) * sectors, len(rels) * capacity)]
+        spans.append(span)
+        sent.append(run_sibling(span[0] + depth * PLANES * sectors, *span[1:], codes, *arrays))
         start += len(rels)
-        sent = run_sibling(
-            low + depth * PLANES * sectors, size, slots, codes,
-            wavefunction, left_blocks, right_blocks,
-        )
-        moved.append(send(sent, swap_core))
-    height, cut = m // x_count, sectors - sectors // 4
-    early, late = {}, {}
-    for rels, arrived, (low, size, slots) in zip(chunks, moved, spans):
-        planes = len(rels)
-        sums = run_dense(
-            low, size, slots, x_count, codes, wavefunction, left_blocks, right_blocks, arrived
-        )
-        sums = sums[: planes * sectors].reshape(planes, sectors, -1, x_count, PLANES, height, m)
+    sums, arrived, by_rel = [], [], {}
+    for rels, span, message in zip(chunks, spans, sent):
+        arrived.append(send(after(message, *sums[-1:]), swap_core))
+        sums.append(run_dense(*span, x_count, codes, *arrays, arrived[-1]))
         for i, r in enumerate(rels):
-            early[r] = sums[i, cut:, 1][None]
-        folded = fold_second(
-            fold_first(jnp.concatenate([sums[:, :, 0], sums[:, :cut, 1]], axis=1))
-        )
-        for i, r in enumerate(rels):
-            late[r] = folded[i]
-    by_z = [(send(early[r], shift[r]) if r else early[r]) for r in order]
-    tail = fold_second(fold_first(sum(by_z[1:], by_z[0])))[0]
-    by_z = [(send(late[r], shift[r]) if r else late[r]) for r in order]
-    main = sum(by_z[1:], by_z[0])
-    return jnp.stack([main[:sectors], jnp.concatenate([main[sectors:], tail])], axis=1)
+            by_rel[r] = sums[-1][i]
+
+    cut = sectors // 2
+    early = {
+        r: send(after(by_rel[r][cut:, 1], arrived[-1]), shift[r]) for r in (1, depth - 1)
+    }
+
+    def piece_of(r):
+        count = cut if r == 0 or r in early else sectors
+        return jnp.concatenate([by_rel[r][:, 0], by_rel[r][:count, 1]])
+
+    halves, late = [], []
+    for i, r in enumerate(order):
+        piece = piece_of(r)
+        if i == 1:
+            piece = after(piece, arrived[-1])
+        if i > 1:
+            piece = after(piece, halves[i - 2])
+        done = [sums[-1]] if i == 0 else [whole] if i == 1 else []
+        halves.append(fold_first(piece, *done))
+        whole = fold_second(halves[i])
+        late.append(send(whole, shift[r]) if r else whole)
+    tail = after(by_rel[0][cut:, 1] + sum(early.values()), halves[-1])
+    tail = fold_second(after(fold_first(tail), late[0]))
+    common = sectors + cut
+    total = sum(w[:common] for w in late)
+    tail = tail + sum(w[common:] for w in late if w.shape[0] > common)
+    return jnp.stack([total[:sectors], jnp.concatenate([total[sectors:], tail])], axis=1)
 
 
 def solution(mesh):

time: 118 us -> 93.6 us (0.79)
  waiting for transfers between devices: 66 us -> 29.5 us
  starting transfers between devices: 23.1 us -> 35 us
  local copies, waits for them, and re-layouts: 3.49 us -> 4.68 us
    ppermute x14 -> x17, waiting for transfers between devices: 66 us -> 29.5 us  [send(): return lax.ppermute(message, ('ops', 'sec'), perm)]
    ppermute x14 -> x17, starting transfers between devices: 23.1 us -> 35 us  [send(): return lax.ppermute(message, ('ops', 'sec'), perm)]
  transfers between devices with their start and end apart: 14 -> 17, of which waited for: 7 -> 9; matrix products, arithmetic and copies ran while one was open for 3% -> 4% of each run, Pallas kernels for 14% -> 12%
where the time goes in v3:
time: 93.6 us; the launch traced here: 93.3 us
  starting transfers between devices  35 us (37%)
  waiting for transfers between devices  29.5 us (32%)
  Pallas kernels  22.1 us (24%)
  local copies, waits for them, and re-layouts  4.68 us (5%)
  other arithmetic  1.73 us (2%)
    ppermute x17, starting transfers between devices, send(): return lax.ppermute(message, ('ops', 'sec'), perm)  35 us
    ppermute x17, waiting for transfers between devices, send(): return lax.ppermute(message, ('ops', 'sec'), perm)  29.5 us
    pallas_call x2, Pallas kernels, run_dense(): pl.pallas_call(functools.partial(dense_kernel, low, size, group_of(slots)...  11.9 us
    pallas_call x2, Pallas kernels, run_sibling(): pl.pallas_call(functools.partial(sibling_kernel, low, size, group_of(slot...  10.2 us
  transfers between devices with their start and end apart: 17, of which 9 were waited for; matrix products, arithmetic and copies ran while one was open for 4% of the time, Pallas kernels for 12%

profile of v3, /device:TPU:0, one launch (start us, length us, event | category | flops | bytes accessed | tf_op | source)
XLA Modules:
  0.0 93.3 jit_solution(5558255202464012538)
XLA Ops:
  0.0 0.9 constant_dynamic-slice_fusion.1
  1.5 5.1 %sibling_contributions.2 = f32[20,2,128,128]{3,2,1,0:T(8,128)S(1)} custom-call(s32[128]{0:T(128)S(1)} %fusion.9.codes, f32[8,2,128,128]{3,2,1,0:T(8,128)} %psi.7, f32[8,8,128,128]{3,2,1,0:T(8,128)} %left.7, f32[8,8,128,128]{3,2,1,0:T(8,128)} %right.7), custom_call_target="tpu_custom_call" | custom-call | flops 1342177280 | bytes 5242880 | tf_op jit(solution)/shard_map/sibling_contributions/pallas_call | solution.py:216
  6.6 0.5 collective-permute-start
  7.1 5.1 %sibling_contributions.3 = f32[20,2,128,128]{3,2,1,0:T(8,128)S(1)} custom-call(s32[128]{0:T(128)S(1)} %fusion.9.codes, f32[8,2,128,128]{3,2,1,0:T(8,128)} %psi.7, f32[8,8,128,128]{3,2,1,0:T(8,128)} %left.7, f32[8,8,128,128]{3,2,1,0:T(8,128)} %right.7), custom_call_target="tpu_custom_call" | custom-call | flops 1342177280 | bytes 5242880 | tf_op jit(solution)/shard_map/sibling_contributions/pallas_call | solution.py:216
  12.3 5.9 %dense_sums.2 = f32[3,8,2,4,64,128]{5,4,3,2,1,0:T(8,128)S(1)} custom-call(s32[128]{0:T(128)S(1)} %fusion.9.codes, f32[8,2,128,128]{3,2,1,0:T(8,128)} %psi.7, f32[8,8,128,128]{3,2,1,0:T(8,128)} %left.7, f32[8,8,128,128]{3,2,1,0:T(8,128)} %right.7, f32[20,2,128,128]{3,2,1,0:T(8,128)S(1)} %collective-permute-done.arrived), custom_call_target="tpu_custom_call" | custom-call | flops 1342177280 | bytes 5242880 | tf_op jit(solution)/shard_map/dense_sums/pallas_call | solution.py:233
  18.2 0.1 collective-permute-start.2
  18.3 0.4 fusion.23
  18.7 0.1 copy.36
  18.8 0.2 copy.37
  19.1 0.2 slice_bitcast_fusion.3
  19.5 3.1 %collective-permute-start.1 = (f32[16,2,64,128]{3,2,0,1:T(8,128)S(1)}, f32[16,2,64,128]{3,2,0,1:T(8,128)S(1)}, u32[]{:S(2)}, u32[]{:S(2)}) collective-permute-start(f32[16,2,64,128]{3,2,0,1:T(8,128)S(1)} %fusion), channel_id=1, source_target_pairs={{0,16},{1,3},{2,18},{3,1},{4,20},{5,7},{6,22},{7,5},{8,24},{9,11},... | collective-permute-start | bytes 3145736 | tf_op jit(solution)/shard_map/ppermute | solution.py:299
  22.6 0.1 slice_bitcast_fusion.2
  22.8 0.2 pad_maximum_fusion
  22.9 0.2 collective-permute-done.2.arrived
  23.2 2.8 %collective-permute-start.13 = (f32[4,4,64,128]{3,2,0,1:T(8,128)S(1)}, f32[4,4,64,128]{3,2,0,1:T(8,128)S(1)}, u32[]{:S(2)}, u32[]{:S(2)}) collective-permute-start(f32[4,4,64,128]{3,2,0,1:T(8,128)S(1)} %get-tuple-element.21), channel_id=1, source_target_pairs={{0,4},{1,5},{2,6},{3,7},{4,8},{5,9},{6,10},{7,11},{8,12},{9,13},{1... | collective-permute-start | bytes 1572872 | tf_op jit(solution)/shard_map/ppermute | solution.py:299
  26.0 1.6 %collective-permute-start.5 = (f32[12,2,64,128]{3,2,0,1:T(8,128)S(1)}, f32[12,2,64,128]{3,2,0,1:T(8,128)S(1)}, u32[]{:S(2)}, u32[]{:S(2)}) collective-permute-start(f32[12,2,64,128]{3,2,0,1:T(8,128)S(1)} %slice.128), channel_id=1, source_target_pairs={{0,16},{1,3},{2,18},{3,1},{4,20},{5,7},{6,22},{7,5},{8,24},{9,11},... | collective-permute-start | bytes 2359304 | tf_op jit(solution)/shard_map/ppermute | solution.py:299
  27.6 6.0 %dense_sums.3 = f32[3,8,2,4,64,128]{5,4,3,2,1,0:T(8,128)S(1)} custom-call(s32[128]{0:T(128)S(1)} %fusion.9.codes, f32[8,2,128,128]{3,2,1,0:T(8,128)} %psi.7, f32[8,8,128,128]{3,2,1,0:T(8,128)} %left.7, f32[8,8,128,128]{3,2,1,0:T(8,128)} %right.7, f32[20,2,128,128]{3,2,1,0:T(8,128)S(1)} %collective-permute-done.2.arrived), custom_call_target="tpu_custom_call" | custom-call | flops 1342177280 | bytes 5242880 | tf_op jit(solution)/shard_map/dense_sums/pallas_call | solution.py:233
  33.5 0.3 fusion.22
  33.9 0.2 copy.35
  34.1 0.1 slice_bitcast_fusion.8
  34.2 0.1 slice_bitcast_fusion.1
  34.3 1.0 %collective-permute-done.1 = f32[16,2,64,128]{3,2,0,1:T(8,128)S(1)} collective-permute-done((f32[16,2,64,128]{3,2,0,1:T(8,128)S(1)}, f32[16,2,64,128]{3,2,0,1:T(8,128)S(1)}, u32[]{:S(2)}, u32[]{:S(2)}) %collective-permute-start.1) | collective-permute-done | bytes 1048608 | tf_op jit(solution)/shard_map/ppermute | solution.py:299
  35.3 0.2 fusion.1
  35.5 2.1 %collective-permute-start.3 = (f32[16,64,128]{2,1,0:T(8,128)S(1)}, f32[16,64,128]{2,1,0:T(8,128)S(1)}, u32[]{:S(2)}, u32[]{:S(2)}) collective-permute-start(f32[16,64,128]{2,1,0:T(8,128)S(1)} %slice_bitcast_fusion.11), channel_id=1, source_target_pairs={{0,2},{1,17},{2,0},{3,19},{4,6},{5,21},{6,4},{7,23},{8,10},{9,25},... | collective-permute-start | bytes 1572872 | tf_op jit(solution)/shard_map/ppermute | solution.py:299
  37.6 0.2 pad_maximum_fusion.1
  37.8 3.6 %collective-permute-start.14 = (f32[4,4,64,128]{3,2,0,1:T(8,128)S(1)}, f32[4,4,64,128]{3,2,0,1:T(8,128)S(1)}, u32[]{:S(2)}, u32[]{:S(2)}) collective-permute-start(f32[4,4,64,128]{3,2,0,1:T(8,128)S(1)} %get-tuple-element.22), channel_id=1, source_target_pairs={{0,12},{1,13},{2,14},{3,15},{4,0},{5,1},{6,2},{7,3},{8,4},{9,5},{1... | collective-permute-start | bytes 1572872 | tf_op jit(solution)/shard_map/ppermute | solution.py:299
  41.5 1.6 %collective-permute-start.8 = (f32[12,2,64,128]{3,2,0,1:T(8,128)S(1)}, f32[12,2,64,128]{3,2,0,1:T(8,128)S(1)}, u32[]{:S(2)}, u32[]{:S(2)}) collective-permute-start(f32[12,2,64,128]{3,2,0,1:T(8,128)S(1)} %slice.135), channel_id=1, source_target_pairs={{0,16},{1,3},{2,18},{3,1},{4,20},{5,7},{6,22},{7,5},{8,24},{9,11},... | collective-permute-start | bytes 2359304 | tf_op jit(solution)/shard_map/ppermute | solution.py:299
  43.2 0.2 pad_maximum_fusion.2
  43.4 7.0 %collective-permute-done.3 = f32[16,64,128]{2,1,0:T(8,128)S(1)} collective-permute-done((f32[16,64,128]{2,1,0:T(8,128)S(1)}, f32[16,64,128]{2,1,0:T(8,128)S(1)}, u32[]{:S(2)}, u32[]{:S(2)}) %collective-permute-start.3) | collective-permute-done | bytes 524320 | tf_op jit(solution)/shard_map/ppermute | solution.py:299
  50.5 3.1 %collective-permute-start.4 = (f32[16,64,128]{2,1,0:T(8,128)S(1)}, f32[16,64,128]{2,1,0:T(8,128)S(1)}, u32[]{:S(2)}, u32[]{:S(2)}) collective-permute-start(f32[16,64,128]{2,1,0:T(8,128)S(1)} %fusion.3), channel_id=1, source_target_pairs={{0,8},{1,9},{2,10},{3,11},{4,12},{5,13},{6,14},{7,15},{8,0},{9,1},... | collective-permute-start | bytes 1572872 | tf_op jit(solution)/shard_map/ppermute | solution.py:299
  53.8 1.7 %collective-permute-start.6 = (f32[12,64,128]{2,1,0:T(8,128)S(1)}, f32[12,64,128]{2,1,0:T(8,128)S(1)}, u32[]{:S(2)}, u32[]{:S(2)}) collective-permute-start(f32[12,64,128]{2,1,0:T(8,128)S(1)} %slice_bitcast_fusion.17), channel_id=1, source_target_pairs={{0,2},{1,17},{2,0},{3,19},{4,6},{5,21},{6,4},{7,23},{8,10},{9,25},... | collective-permute-start | bytes 1179656 | tf_op jit(solution)/shard_map/ppermute | solution.py:299
  55.5 5.5 %collective-permute-done.8 = f32[12,2,64,128]{3,2,0,1:T(8,128)S(1)} collective-permute-done((f32[12,2,64,128]{3,2,0,1:T(8,128)S(1)}, f32[12,2,64,128]{3,2,0,1:T(8,128)S(1)}, u32[]{:S(2)}, u32[]{:S(2)}) %collective-permute-start.8) | collective-permute-done | bytes 786464 | tf_op jit(solution)/shard_map/ppermute | solution.py:299
  61.0 2.5 %collective-permute-start.11 = (f32[12,2,64,128]{3,2,0,1:T(8,128)S(1)}, f32[12,2,64,128]{3,2,0,1:T(8,128)S(1)}, u32[]{:S(2)}, u32[]{:S(2)}) collective-permute-start(f32[12,2,64,128]{3,2,0,1:T(8,128)S(1)} %slice.142), channel_id=1, source_target_pairs={{0,16},{1,3},{2,18},{3,1},{4,20},{5,7},{6,22},{7,5},{8,24},{9,11},... | collective-permute-start | bytes 2359304 | tf_op jit(solution)/shard_map/ppermute | solution.py:299
  63.6 1.6 %collective-permute-start.9 = (f32[12,64,128]{2,1,0:T(8,128)S(1)}, f32[12,64,128]{2,1,0:T(8,128)S(1)}, u32[]{:S(2)}, u32[]{:S(2)}) collective-permute-start(f32[12,64,128]{2,1,0:T(8,128)S(1)} %slice_bitcast_fusion.15), channel_id=1, source_target_pairs={{0,2},{1,17},{2,0},{3,19},{4,6},{5,21},{6,4},{7,23},{8,10},{9,25},... | collective-permute-start | bytes 1179656 | tf_op jit(solution)/shard_map/ppermute | solution.py:299
  65.2 0.1 fusion.2
  65.4 1.6 %collective-permute-start.7 = (f32[12,64,128]{2,1,0:T(8,128)S(1)}, f32[12,64,128]{2,1,0:T(8,128)S(1)}, u32[]{:S(2)}, u32[]{:S(2)}) collective-permute-start(f32[12,64,128]{2,1,0:T(8,128)S(1)} %fusion.7), channel_id=1, source_target_pairs={{0,4},{1,5},{2,6},{3,7},{4,8},{5,9},{6,10},{7,11},{8,12},{9,13},{1... | collective-permute-start | bytes 1179656 | tf_op jit(solution)/shard_map/ppermute | solution.py:299
  67.0 7.3 %collective-permute-done.9 = f32[12,64,128]{2,1,0:T(8,128)S(1)} collective-permute-done((f32[12,64,128]{2,1,0:T(8,128)S(1)}, f32[12,64,128]{2,1,0:T(8,128)S(1)}, u32[]{:S(2)}, u32[]{:S(2)}) %collective-permute-start.9) | collective-permute-done | bytes 393248 | tf_op jit(solution)/shard_map/ppermute | solution.py:299
  74.3 0.3 collective-permute-done.11
  74.6 0.1 slice_add_fusion
  74.8 2.1 %collective-permute-start.15 = (f32[4,2,64,128]{3,2,1,0:T(8,128)S(1)}, f32[4,2,64,128]{3,2,1,0:T(8,128)S(1)}, u32[]{:S(2)}, u32[]{:S(2)}) collective-permute-start(f32[4,2,64,128]{3,2,1,0:T(8,128)S(1)} %slice.151), channel_id=1, source_target_pairs={{0,16},{1,3},{2,18},{3,1},{4,20},{5,7},{6,22},{7,5},{8,24},{9,11},... | collective-permute-start | bytes 786440 | tf_op jit(solution)/shard_map/ppermute | solution.py:299
  76.9 4.7 %collective-permute-start.10 = (f32[12,64,128]{2,1,0:T(8,128)S(1)}, f32[12,64,128]{2,1,0:T(8,128)S(1)}, u32[]{:S(2)}, u32[]{:S(2)}) collective-permute-start(f32[12,64,128]{2,1,0:T(8,128)S(1)} %fusion.6), channel_id=1, source_target_pairs={{0,12},{1,13},{2,14},{3,15},{4,0},{5,1},{6,2},{7,3},{8,4},{9,5},{1... | collective-permute-start | bytes 1179656 | tf_op jit(solution)/shard_map/ppermute | solution.py:299
  81.7 0.8 collective-permute-start.12
  82.5 2.6 %collective-permute-done.4 = f32[16,64,128]{2,1,0:T(8,128)S(1)} collective-permute-done((f32[16,64,128]{2,1,0:T(8,128)S(1)}, f32[16,64,128]{2,1,0:T(8,128)S(1)}, u32[]{:S(2)}, u32[]{:S(2)}) %collective-permute-start.4) | collective-permute-done | bytes 524320 | tf_op jit(solution)/shard_map/ppermute | solution.py:299
  85.1 1.6 %collective-permute-start.16 = (f32[4,64,128]{2,1,0:T(8,128)S(1)}, f32[4,64,128]{2,1,0:T(8,128)S(1)}, u32[]{:S(2)}, u32[]{:S(2)}) collective-permute-start(f32[4,64,128]{2,1,0:T(8,128)S(1)} %slice_bitcast_fusion.19), channel_id=1, source_target_pairs={{0,2},{1,17},{2,0},{3,19},{4,6},{5,21},{6,4},{7,23},{8,10},{9,25},... | collective-permute-start | bytes 393224 | tf_op jit(solution)/shard_map/ppermute | solution.py:299
  86.6 2.9 %collective-permute-done.12 = f32[12,64,128]{2,1,0:T(8,128)S(1)} collective-permute-done((f32[12,64,128]{2,1,0:T(8,128)S(1)}, f32[12,64,128]{2,1,0:T(8,128)S(1)}, u32[]{:S(2)}, u32[]{:S(2)}) %collective-permute-start.12) | collective-permute-done | bytes 393248 | tf_op jit(solution)/shard_map/ppermute | solution.py:299
  89.5 2.7 %collective-permute-done.10 = f32[12,64,128]{2,1,0:T(8,128)S(1)} collective-permute-done((f32[12,64,128]{2,1,0:T(8,128)S(1)}, f32[12,64,128]{2,1,0:T(8,128)S(1)}, u32[]{:S(2)}, u32[]{:S(2)}) %collective-permute-start.10) | collective-permute-done | bytes 393248 | tf_op jit(solution)/shard_map/ppermute | solution.py:299
  92.2 0.2 fusion.5
  92.5 0.8 copy.17
  (41 shorter events, 1.7 us)
Async XLA Ops:
  6.6 5.6 %collective-permute-start = (f32[20,2,128,128]{3,2,1,0:T(8,128)S(1)}, f32[20,2,128,128]{3,2,1,0:T(8,128)S(1)}, u32[]{:S(2)}, u32[]{:S(2)}) collective-permute-start(f32[20,2,128,128]{3,2,1,0:T(8,128)S(1)} %sibling_contributions.2), channel_id=1, source_target_pairs={{0,1},{1,0},{2,3},{3,2},{4,5},{5,4},{6,7},{7,6},{8,9},{9,8},{10,11... | collective-permute-start | bytes 7864328 | tf_op jit(solution)/shard_map/ppermute | solution.py:299
  18.2 5.0 %collective-permute-start.2 = (f32[20,2,128,128]{3,2,1,0:T(8,128)S(1)}, f32[20,2,128,128]{3,2,1,0:T(8,128)S(1)}, u32[]{:S(2)}, u32[]{:S(2)}) collective-permute-start(f32[20,2,128,128]{3,2,1,0:T(8,128)S(1)} %sibling_contributions.3), channel_id=1, source_target_pairs={{0,1},{1,0},{2,3},{3,2},{4,5},{5,4},{6,7},{7,6},{8,9},{9,8},{10,11... | collective-permute-start | bytes 7864328 | tf_op jit(solution)/shard_map/ppermute | solution.py:299
  19.5 15.9 %collective-permute-start.1 = (f32[16,2,64,128]{3,2,0,1:T(8,128)S(1)}, f32[16,2,64,128]{3,2,0,1:T(8,128)S(1)}, u32[]{:S(2)}, u32[]{:S(2)}) collective-permute-start(f32[16,2,64,128]{3,2,0,1:T(8,128)S(1)} %fusion), channel_id=1, source_target_pairs={{0,16},{1,3},{2,18},{3,1},{4,20},{5,7},{6,22},{7,5},{8,24},{9,11},... | collective-permute-start | bytes 3145736 | tf_op jit(solution)/shard_map/ppermute | solution.py:299
  23.2 40.5 %collective-permute-start.13 = (f32[4,4,64,128]{3,2,0,1:T(8,128)S(1)}, f32[4,4,64,128]{3,2,0,1:T(8,128)S(1)}, u32[]{:S(2)}, u32[]{:S(2)}) collective-permute-start(f32[4,4,64,128]{3,2,0,1:T(8,128)S(1)} %get-tuple-element.21), channel_id=1, source_target_pairs={{0,4},{1,5},{2,6},{3,7},{4,8},{5,9},{6,10},{7,11},{8,12},{9,13},{1... | collective-permute-start | bytes 1572872 | tf_op jit(solution)/shard_map/ppermute | solution.py:299
  26.0 27.7 %collective-permute-start.5 = (f32[12,2,64,128]{3,2,0,1:T(8,128)S(1)}, f32[12,2,64,128]{3,2,0,1:T(8,128)S(1)}, u32[]{:S(2)}, u32[]{:S(2)}) collective-permute-start(f32[12,2,64,128]{3,2,0,1:T(8,128)S(1)} %slice.128), channel_id=1, source_target_pairs={{0,16},{1,3},{2,18},{3,1},{4,20},{5,7},{6,22},{7,5},{8,24},{9,11},... | collective-permute-start | bytes 2359304 | tf_op jit(solution)/shard_map/ppermute | solution.py:299
  35.5 14.9 %collective-permute-start.3 = (f32[16,64,128]{2,1,0:T(8,128)S(1)}, f32[16,64,128]{2,1,0:T(8,128)S(1)}, u32[]{:S(2)}, u32[]{:S(2)}) collective-permute-start(f32[16,64,128]{2,1,0:T(8,128)S(1)} %slice_bitcast_fusion.11), channel_id=1, source_target_pairs={{0,2},{1,17},{2,0},{3,19},{4,6},{5,21},{6,4},{7,23},{8,10},{9,25},... | collective-permute-start | bytes 1572872 | tf_op jit(solution)/shard_map/ppermute | solution.py:299
  37.8 27.4 %collective-permute-start.14 = (f32[4,4,64,128]{3,2,0,1:T(8,128)S(1)}, f32[4,4,64,128]{3,2,0,1:T(8,128)S(1)}, u32[]{:S(2)}, u32[]{:S(2)}) collective-permute-start(f32[4,4,64,128]{3,2,0,1:T(8,128)S(1)} %get-tuple-element.22), channel_id=1, source_target_pairs={{0,12},{1,13},{2,14},{3,15},{4,0},{5,1},{6,2},{7,3},{8,4},{9,5},{1... | collective-permute-start | bytes 1572872 | tf_op jit(solution)/shard_map/ppermute | solution.py:299
  41.5 19.5 %collective-permute-start.8 = (f32[12,2,64,128]{3,2,0,1:T(8,128)S(1)}, f32[12,2,64,128]{3,2,0,1:T(8,128)S(1)}, u32[]{:S(2)}, u32[]{:S(2)}) collective-permute-start(f32[12,2,64,128]{3,2,0,1:T(8,128)S(1)} %slice.135), channel_id=1, source_target_pairs={{0,16},{1,3},{2,18},{3,1},{4,20},{5,7},{6,22},{7,5},{8,24},{9,11},... | collective-permute-start | bytes 2359304 | tf_op jit(solution)/shard_map/ppermute | solution.py:299
  50.5 34.5 %collective-permute-start.4 = (f32[16,64,128]{2,1,0:T(8,128)S(1)}, f32[16,64,128]{2,1,0:T(8,128)S(1)}, u32[]{:S(2)}, u32[]{:S(2)}) collective-permute-start(f32[16,64,128]{2,1,0:T(8,128)S(1)} %fusion.3), channel_id=1, source_target_pairs={{0,8},{1,9},{2,10},{3,11},{4,12},{5,13},{6,14},{7,15},{8,0},{9,1},... | collective-permute-start | bytes 1572872 | tf_op jit(solution)/shard_map/ppermute | solution.py:299
  53.8 11.5 %collective-permute-start.6 = (f32[12,64,128]{2,1,0:T(8,128)S(1)}, f32[12,64,128]{2,1,0:T(8,128)S(1)}, u32[]{:S(2)}, u32[]{:S(2)}) collective-permute-start(f32[12,64,128]{2,1,0:T(8,128)S(1)} %slice_bitcast_fusion.17), channel_id=1, source_target_pairs={{0,2},{1,17},{2,0},{3,19},{4,6},{5,21},{6,4},{7,23},{8,10},{9,25},... | collective-permute-start | bytes 1179656 | tf_op jit(solution)/shard_map/ppermute | solution.py:299
  61.0 13.6 %collective-permute-start.11 = (f32[12,2,64,128]{3,2,0,1:T(8,128)S(1)}, f32[12,2,64,128]{3,2,0,1:T(8,128)S(1)}, u32[]{:S(2)}, u32[]{:S(2)}) collective-permute-start(f32[12,2,64,128]{3,2,0,1:T(8,128)S(1)} %slice.142), channel_id=1, source_target_pairs={{0,16},{1,3},{2,18},{3,1},{4,20},{5,7},{6,22},{7,5},{8,24},{9,11},... | collective-permute-start | bytes 2359304 | tf_op jit(solution)/shard_map/ppermute | solution.py:299
  63.6 10.7 %collective-permute-start.9 = (f32[12,64,128]{2,1,0:T(8,128)S(1)}, f32[12,64,128]{2,1,0:T(8,128)S(1)}, u32[]{:S(2)}, u32[]{:S(2)}) collective-permute-start(f32[12,64,128]{2,1,0:T(8,128)S(1)} %slice_bitcast_fusion.15), channel_id=1, source_target_pairs={{0,2},{1,17},{2,0},{3,19},{4,6},{5,21},{6,4},{7,23},{8,10},{9,25},... | collective-permute-start | bytes 1179656 | tf_op jit(solution)/shard_map/ppermute | solution.py:299
  65.4 24.1 %collective-permute-start.7 = (f32[12,64,128]{2,1,0:T(8,128)S(1)}, f32[12,64,128]{2,1,0:T(8,128)S(1)}, u32[]{:S(2)}, u32[]{:S(2)}) collective-permute-start(f32[12,64,128]{2,1,0:T(8,128)S(1)} %fusion.7), channel_id=1, source_target_pairs={{0,4},{1,5},{2,6},{3,7},{4,8},{5,9},{6,10},{7,11},{8,12},{9,13},{1... | collective-permute-start | bytes 1179656 | tf_op jit(solution)/shard_map/ppermute | solution.py:299
  74.8 7.6 %collective-permute-start.15 = (f32[4,2,64,128]{3,2,1,0:T(8,128)S(1)}, f32[4,2,64,128]{3,2,1,0:T(8,128)S(1)}, u32[]{:S(2)}, u32[]{:S(2)}) collective-permute-start(f32[4,2,64,128]{3,2,1,0:T(8,128)S(1)} %slice.151), channel_id=1, source_target_pairs={{0,16},{1,3},{2,18},{3,1},{4,20},{5,7},{6,22},{7,5},{8,24},{9,11},... | collective-permute-start | bytes 786440 | tf_op jit(solution)/shard_map/ppermute | solution.py:299
  76.9 15.3 %collective-permute-start.10 = (f32[12,64,128]{2,1,0:T(8,128)S(1)}, f32[12,64,128]{2,1,0:T(8,128)S(1)}, u32[]{:S(2)}, u32[]{:S(2)}) collective-permute-start(f32[12,64,128]{2,1,0:T(8,128)S(1)} %fusion.6), channel_id=1, source_target_pairs={{0,12},{1,13},{2,14},{3,15},{4,0},{5,1},{6,2},{7,3},{8,4},{9,5},{1... | collective-permute-start | bytes 1179656 | tf_op jit(solution)/shard_map/ppermute | solution.py:299
  81.7 7.8 %collective-permute-start.12 = (f32[12,64,128]{2,1,0:T(8,128)S(1)}, f32[12,64,128]{2,1,0:T(8,128)S(1)}, u32[]{:S(2)}, u32[]{:S(2)}) collective-permute-start(f32[12,64,128]{2,1,0:T(8,128)S(1)} %slice_bitcast_fusion.13), channel_id=1, source_target_pairs={{0,2},{1,17},{2,0},{3,19},{4,6},{5,21},{6,4},{7,23},{8,10},{9,25},... | collective-permute-start | bytes 1179656 | tf_op jit(solution)/shard_map/ppermute | solution.py:299
  85.1 7.3 %collective-permute-start.16 = (f32[4,64,128]{2,1,0:T(8,128)S(1)}, f32[4,64,128]{2,1,0:T(8,128)S(1)}, u32[]{:S(2)}, u32[]{:S(2)}) collective-permute-start(f32[4,64,128]{2,1,0:T(8,128)S(1)} %slice_bitcast_fusion.19), channel_id=1, source_target_pairs={{0,2},{1,17},{2,0},{3,19},{4,6},{5,21},{6,4},{7,23},{8,10},{9,25},... | collective-permute-start | bytes 393224 | tf_op jit(solution)/shard_map/ppermute | solution.py:299

commit v4 on v3

--- a/solution.py
+++ b/solution.py
@@ -9,6 +9,7 @@
 
 CORES = 2
 PLANES = 2
+VECTORS = 2
 MOST_IN_GROUP = 10
 
 
@@ -124,15 +125,30 @@
     lax.fori_loop(0, groups, one, 0)
 
 
-def dense_kernel(
-    low, size, group, x_count, codes, psi, left, right, arrived, total,
-    listed, rows, rows_in, left_buf, right_buf, psi_raw, psi_pairs, sems, psi_sem,
+def adder(total, x_count):
+    sectors, height = total.shape[2] // VECTORS, total.shape[4]
+    x, core = lax.axis_index("ops"), lax.axis_index("sec") % CORES
+
+    def add(code, block):
+        row, y_rel = code // PLANES, code % PLANES
+        plane, local = row // sectors, row % sectors
+        for h in range(x_count):
+            x_rel = lax.rem(h - x + x_count, x_count)
+            p, q = x_rel, y_rel
+            if x_count == PLANES:
+                p, q = jnp.where(core == 0, x_rel, y_rel), jnp.where(core == 0, y_rel, x_rel)
+            for v in range(VECTORS):
+                total[plane, p, v * sectors + local, q] += block(v, h * height)
+
+    return add
+
+
+def own_kernel(
+    low, size, group, x_count, codes, psi, left, right, total,
+    listed, rows, left_buf, right_buf, psi_raw, psi_pairs, sems, psi_sem,
 ):
     terms, sectors, m, _ = left.shape
-    vectors = psi.shape[1]
-    pairs = terms * sectors
     height = m // x_count
-    x, core = lax.axis_index("ops"), lax.axis_index("sec") % CORES
     pltpu.make_async_copy(psi, psi_raw, psi_sem).start()
 
     def take(i, p, row):
@@ -141,30 +157,16 @@
         for copy in fetch(left, right, left_buf, right_buf, sems, p, i, sectors):
             copy.start()
 
-    def take_in(i, p, row):
-        rows_in[i] = row
-
-    count = collect(codes, 0, pairs, low, size, take)
+    count = collect(codes, 0, terms * sectors, low, size, take)
     groups = padded(count, group, take, size)
-    count_in = collect(codes, pairs, pairs, low, size, take_in)
 
     def clear(t, carry):
-        total[t // sectors, t % sectors] = jnp.zeros(total.shape[2:], jnp.float32)
-        return carry
-
-    lax.fori_loop(0, size // PLANES + 1, clear, 0)
+        total[t // x_count, t % x_count] = jnp.zeros(total.shape[2:], jnp.float32)
+        return carry
+
+    lax.fori_loop(0, total.shape[0] * x_count, clear, 0)
     prepare(psi, psi_raw, psi_pairs, psi_sem)
-
-    def add(code, block):
-        row, y_rel = code // PLANES, code % PLANES
-        plane, local = row // sectors, row % sectors
-        for h in range(x_count):
-            x_rel = lax.rem(h - x + x_count, x_count)
-            place = x_rel * PLANES + y_rel
-            if x_count == PLANES:
-                place = jnp.where(core == 0, place, y_rel * PLANES + x_rel)
-            for v in range(vectors):
-                total[plane, local, v, place] += block(v, h * height)
+    add = adder(total, x_count)
 
     def one(g, carry):
         at, products = group_products(
@@ -176,11 +178,26 @@
 
     lax.fori_loop(0, groups, one, 0)
 
-    def merge(i, carry):
-        add(rows_in[i], lambda v, h: arrived[i, v, h : h + height])
-        return carry
-
-    lax.fori_loop(0, count_in, merge, 0)
+
+def merge_kernel(low, size, x_count, pairs, codes, own, *refs):
+    del own
+    *arrived, total, rows = refs
+    height = arrived[0].shape[2] // x_count
+
+    def take(i, p, row):
+        rows[i] = row
+
+    count = collect(codes, pairs, pairs, low, size, take)
+    add = adder(total, x_count)
+    start = 0
+    for piece in arrived:
+
+        def merge(i, carry, piece=piece, start=start):
+            add(rows[i], lambda v, h: piece[i - start, v, h : h + height])
+            return carry
+
+        lax.fori_loop(start, jnp.minimum(count, start + piece.shape[0]), merge, 0)
+        start += piece.shape[0]
 
 
 def group_of(slots):
@@ -200,7 +217,7 @@
 
 def cost(slots, vectors, m):
     return pl.CostEstimate(
-        flops=slots * vectors * 16 * m**3,
+        flops=slots * vectors * 4 * m**3,
         bytes_accessed=slots * (2 + vectors) * m * m * 4,
         transcendentals=0,
     )
@@ -225,24 +242,36 @@
     )(codes, *in_hbm(psi, left, right))
 
 
-def run_dense(low, size, slots, x_count, codes, psi, left, right, arrived):
+def run_own(low, size, slots, x_count, codes, psi, left, right):
     sectors, m = left.shape[1], left.shape[2]
     vectors = psi.shape[1]
     planes = size // (PLANES * sectors)
-    shape = (planes + 1, sectors, vectors, x_count * PLANES, m // x_count, m)
+    shape = (planes + 1, x_count, vectors * sectors, PLANES, m // x_count, m)
     return pl.pallas_call(
-        functools.partial(dense_kernel, low, size, group_of(slots), x_count),
+        functools.partial(own_kernel, low, size, group_of(slots), x_count),
         out_shape=pltpu.VMEM(shape, jnp.float32),
-        in_specs=[pl.BlockSpec(memory_space=pltpu.SMEM)]
-        + [pl.BlockSpec(memory_space=pl.ANY)] * 3
-        + [pl.BlockSpec(memory_space=pltpu.VMEM)],
+        in_specs=[pl.BlockSpec(memory_space=pltpu.SMEM)] + [pl.BlockSpec(memory_space=pl.ANY)] * 3,
         out_specs=pl.BlockSpec(memory_space=pltpu.VMEM),
-        scratch_shapes=[pltpu.SMEM((slots,), jnp.int32)] * 3
+        scratch_shapes=[pltpu.SMEM((slots,), jnp.int32)] * 2
         + buffers(slots, sectors, vectors, m),
         compiler_params=pltpu.CompilerParams(vmem_limit_bytes=32 << 20),
         cost_estimate=cost(slots, vectors, m),
-        name="dense_sums",
-    )(codes, *in_hbm(psi, left, right), arrived)
+        name="own_sums",
+    )(codes, *in_hbm(psi, left, right))
+
+
+def run_merge(low, size, slots, x_count, pairs, codes, own, *arrived):
+    return pl.pallas_call(
+        functools.partial(merge_kernel, low, size, x_count, pairs),
+        out_shape=pltpu.VMEM(own.shape, jnp.float32),
+        in_specs=[pl.BlockSpec(memory_space=pltpu.SMEM)]
+        + [pl.BlockSpec(memory_space=pltpu.VMEM)] * (1 + len(arrived)),
+        out_specs=pl.BlockSpec(memory_space=pltpu.VMEM),
+        scratch_shapes=[pltpu.SMEM((slots,), jnp.int32)],
+        input_output_aliases={1: 0},
+        compiler_params=pltpu.CompilerParams(vmem_limit_bytes=32 << 20),
+        name="merge_sibling",
+    )(codes, own, *arrived)
 
 
 def shards(wavefunction, left_blocks, right_blocks, target_owner, target_local):
@@ -298,62 +327,58 @@
     def send(message, perm):
         return lax.ppermute(message, ("ops", "sec"), perm)
 
-    def ring(parts, perm, *done):
-        moving = parts[-1]
+    def ring(parts, perm, before=(), done=()):
+        moving = after(parts[-1], *before)
         for part in parts[-2::-1]:
             moving = after(send(moving, perm), *done) + part
         return moving
 
-    def fold_first(sums, *done):
-        parts = [sums[:, p * PLANES : (p + 1) * PLANES] for p in range(x_count)]
-        return ring(parts, first, *done)
-
-    def fold_second(sums):
-        return ring([sums[:, q] for q in range(PLANES)], second)
+    def fold_first(sums, count, before=(), done=()):
+        return ring([sums[p, count] for p in range(x_count)], first, before, done)
+
+    def fold_second(sums, before=()):
+        return ring([sums[:, q] for q in range(PLANES)], second, before)
 
     def after(value, *done):
-        return lax.optimization_barrier((value, done))[0]
+        return lax.optimization_barrier((value, done))[0] if done else value
 
     arrays = (wavefunction, left_blocks, right_blocks)
-    spans, sent = [], []
+    cut = sectors + sectors // 2
+    beside = (1, depth - 1)
+
+    def share(r):
+        return slice(0, cut if r == 0 or r in beside else VECTORS * sectors)
+
+    sums, by_rel, halves = [], {}, []
     start = 0
     for rels in chunks:
         span = [PLANES * n for n in (start * sectors, len(rels) * sectors, len(rels) * capacity)]
-        spans.append(span)
-        sent.append(run_sibling(span[0] + depth * PLANES * sectors, *span[1:], codes, *arrays))
-        start += len(rels)
-    sums, arrived, by_rel = [], [], {}
-    for rels, span, message in zip(chunks, spans, sent):
-        arrived.append(send(after(message, *sums[-1:]), swap_core))
-        sums.append(run_dense(*span, x_count, codes, *arrays, arrived[-1]))
+        sent = run_sibling(
+            span[0] + depth * PLANES * sectors, *span[1:], after(codes, *sums), *arrays
+        )
+        own = run_own(*span, x_count, after(codes, sent), *arrays)
+        arrived = [send(part, swap_core) for part in jnp.split(sent, 1 + len(sums))]
+        if sums:
+            halves = [fold_first(by_rel[order[0]], share(order[0]), done=[own])]
+            own = after(own, *halves)
+        sums.append(run_merge(*span, x_count, pairs, codes, own, *arrived))
         for i, r in enumerate(rels):
             by_rel[r] = sums[-1][i]
-
-    cut = sectors // 2
-    early = {
-        r: send(after(by_rel[r][cut:, 1], arrived[-1]), shift[r]) for r in (1, depth - 1)
-    }
-
-    def piece_of(r):
-        count = cut if r == 0 or r in early else sectors
-        return jnp.concatenate([by_rel[r][:, 0], by_rel[r][:count, 1]])
-
-    halves, late = [], []
+        start += len(rels)
+
+    early = [send(by_rel[r][:, cut:], shift[r]) for r in beside]
+    late = []
     for i, r in enumerate(order):
-        piece = piece_of(r)
         if i == 1:
-            piece = after(piece, arrived[-1])
+            halves.append(fold_first(by_rel[r], share(r), done=[sums[-1], whole]))
         if i > 1:
-            piece = after(piece, halves[i - 2])
-        done = [sums[-1]] if i == 0 else [whole] if i == 1 else []
-        halves.append(fold_first(piece, *done))
+            halves.append(fold_first(by_rel[r], share(r), before=[halves[i - 2]]))
         whole = fold_second(halves[i])
         late.append(send(whole, shift[r]) if r else whole)
-    tail = after(by_rel[0][cut:, 1] + sum(early.values()), halves[-1])
-    tail = fold_second(after(fold_first(tail), late[0]))
-    common = sectors + cut
-    total = sum(w[:common] for w in late)
-    tail = tail + sum(w[common:] for w in late if w.shape[0] > common)
+    tail = fold_first(by_rel[0][:, cut:] + sum(early), slice(None), before=[halves[-2]])
+    tail = fold_second(tail, before=late[:1])
+    total = sum(w[:cut] for w in late)
+    tail = tail + sum(w[cut:] for w in late if w.shape[0] > cut)
     return jnp.stack([total[:sectors], jnp.concatenate([total[sectors:], tail])], axis=1)
 
 

time: 93.6 us -> 91 us (0.972)
  starting transfers between devices: 35 us -> 29.5 us
  waiting for transfers between devices: 29.5 us -> 31.8 us
  Pallas kernels: 22.1 us -> 23.5 us
    ppermute x17 -> x18, starting transfers between devices: 35 us -> 29.5 us  [send(): return lax.ppermute(message, ('ops', 'sec'), perm)]
    ppermute x17 -> x18, waiting for transfers between devices: 29.5 us -> 31.8 us  [send(): return lax.ppermute(message, ('ops', 'sec'), perm)]
    pallas_call x2 -> x4, Pallas kernels: 11.9 us -> 13.2 us  [the longest x2 10.6 us: run_own(): pl.pallas_call(functools.partial(own_kernel, low, size, group_of(slots),...]
  transfers between devices with their start and end apart: 17 -> 18, of which waited for: 9 -> 7; matrix products, arithmetic and copies ran while one was open for 4% -> 3% of each run, Pallas kernels for 12% -> 19%
where the time goes in v4:
time: 91 us; the launch traced here: 90.6 us
  waiting for transfers between devices  31.8 us (35%)
  starting transfers between devices  29.5 us (32%)
  Pallas kernels  23.5 us (26%)
  local copies, waits for them, and re-layouts  4.4 us (5%)
  other arithmetic  1.15 us (1%)
    ppermute x18, waiting for transfers between devices, send(): return lax.ppermute(message, ('ops', 'sec'), perm)  31.8 us
    ppermute x18, starting transfers between devices, send(): return lax.ppermute(message, ('ops', 'sec'), perm)  29.5 us
    pallas_call x2, Pallas kernels, run_own(): pl.pallas_call(functools.partial(own_kernel, low, size, group_of(slots),...  10.6 us
    pallas_call x2, Pallas kernels, run_sibling(): pl.pallas_call(functools.partial(sibling_kernel, low, size, group_of(slot...  10.2 us
    pallas_call x2, Pallas kernels, run_merge(): pl.pallas_call(functools.partial(merge_kernel, low, size, x_count, pairs)...  2.65 us
  transfers between devices with their start and end apart: 18, of which 7 were waited for; matrix products, arithmetic and copies ran while one was open for 3% of the time, Pallas kernels for 19%

profile of v4, /device:TPU:0, one launch (start us, length us, event | category | flops | bytes accessed | tf_op | source)
XLA Modules:
  0.0 90.6 jit_solution(9791411320445840762)
XLA Ops:
  0.0 0.9 %constant_dynamic-slice_fusion.1 = (s32[1,64]{0,1:T(8,128)S(1)}, s32[1,64]{0,1:T(8,128)S(1)}, s32[1,64]{0,1:T(8,128)S(1)}, s32[1,64]{0,1:T(8,128)S(1)}) fusion(s32[16,64]{0,1:T(8,128)} %bitcast.86, s32[]{:T(128)S(6)} %select_n.67, s32[]{:T(128)S(6)} %select_n.69, s32[16,64]{0,1:T(8,128)} %bitcast.87), kind=kLoop, calls=%fused_computation.62 | loop fusion | bytes 2056 | tf_op jit(solution)/shard_map/dynamic_slice | solution.py:292
  1.1 0.1 reshape.11
  1.4 0.1 reshape.10
  1.5 5.1 %sibling_contributions.2 = f32[20,2,128,128]{3,2,1,0:T(8,128)S(1)} custom-call(s32[128]{0:T(128)S(1)} %fusion.12.codes, f32[8,2,128,128]{3,2,1,0:T(8,128)} %psi.7, f32[8,8,128,128]{3,2,1,0:T(8,128)} %left.7, f32[8,8,128,128]{3,2,1,0:T(8,128)} %right.7), custom_call_target="tpu_custom_call" | custom-call | flops 335544320 | bytes 5242880 | tf_op jit(solution)/shard_map/sibling_contributions/pallas_call | solution.py:233
  6.6 0.6 collective-permute-start
  7.2 5.3 %own_sums.2.own = f32[3,2,16,2,64,128]{5,4,3,2,1,0:T(8,128)S(1)} custom-call(s32[128]{0:T(128)S(1)} %fusion.12.codes, f32[8,2,128,128]{3,2,1,0:T(8,128)} %psi.7, f32[8,8,128,128]{3,2,1,0:T(8,128)} %left.7, f32[8,8,128,128]{3,2,1,0:T(8,128)} %right.7), custom_call_target="tpu_custom_call" | custom-call | flops 335544320 | bytes 5242880 | tf_op jit(solution)/shard_map/own_sums/pallas_call | solution.py:250
  12.5 1.3 %merge_sibling.2 = f32[3,2,16,2,64,128]{5,4,3,2,1,0:T(8,128)S(1)} custom-call(s32[128]{0:T(128)S(1)} %fusion.12.codes, f32[3,2,16,2,64,128]{5,4,3,2,1,0:T(8,128)S(1)} %own_sums.2.own, f32[20,2,128,128]{3,2,1,0:T(8,128)S(1)} %collective-permute-done.refs_0_), custom_call_target="tpu_custom_call", output_to_operand_aliasing={{}: (1, {})} | custom-call | tf_op jit(solution)/shard_map/merge_sibling/pallas_call | solution.py:264
  13.7 0.2 fusion.26
  14.0 0.1 copy.44
  14.1 2.4 %collective-permute-start.1 = (f32[16,2,64,128]{3,2,0,1:T(8,128)S(1)}, f32[16,2,64,128]{3,2,0,1:T(8,128)S(1)}, u32[]{:S(2)}, u32[]{:S(2)}) collective-permute-start(f32[16,2,64,128]{3,2,0,1:T(8,128)S(1)} %bitcast.84), channel_id=1, source_target_pairs={{0,16},{1,3},{2,18},{3,1},{4,20},{5,7},{6,22},{7,5},{8,24},{9,11},... | collective-permute-start | bytes 3145736 | tf_op jit(solution)/shard_map/ppermute | solution.py:328
  16.5 5.1 %sibling_contributions.3 = f32[20,2,128,128]{3,2,1,0:T(8,128)S(1)} custom-call(s32[128]{0:T(128)S(1)} %fusion.12.codes, f32[8,2,128,128]{3,2,1,0:T(8,128)} %psi.7, f32[8,8,128,128]{3,2,1,0:T(8,128)} %left.7, f32[8,8,128,128]{3,2,1,0:T(8,128)} %right.7), custom_call_target="tpu_custom_call" | custom-call | flops 335544320 | bytes 5242880 | tf_op jit(solution)/shard_map/sibling_contributions/pallas_call | solution.py:233
  21.7 0.3 fusion.27
  22.0 0.4 collective-permute-start.6
  22.4 0.2 collective-permute-start.5
  22.5 0.2 copy_bitcast_fusion.1
  22.8 1.8 %collective-permute-start.14 = (f32[2,4,2,64,128]{4,3,1,2,0:T(8,128)S(1)}, f32[2,4,2,64,128]{4,3,1,2,0:T(8,128)S(1)}, u32[]{:S(2)}, u32[]{:S(2)}) collective-permute-start(f32[2,4,2,64,128]{4,3,1,2,0:T(8,128)S(1)} %slice.148), channel_id=1, source_target_pairs={{0,4},{1,5},{2,6},{3,7},{4,8},{5,9},{6,10},{7,11},{8,12},{9,13},{1... | collective-permute-start | bytes 1572872 | tf_op jit(solution)/shard_map/ppermute | solution.py:328
  24.7 1.5 %collective-permute-start.4 = (f32[12,2,64,128]{3,2,0,1:T(8,128)S(1)}, f32[12,2,64,128]{3,2,0,1:T(8,128)S(1)}, u32[]{:S(2)}, u32[]{:S(2)}) collective-permute-start(f32[12,2,64,128]{3,2,0,1:T(8,128)S(1)} %slice_bitcast_fusion.4), channel_id=1, source_target_pairs={{0,16},{1,3},{2,18},{3,1},{4,20},{5,7},{6,22},{7,5},{8,24},{9,11},... | collective-permute-start | bytes 2359304 | tf_op jit(solution)/shard_map/ppermute | solution.py:328
  26.2 5.3 %own_sums.3.own = f32[3,2,16,2,64,128]{5,4,3,2,1,0:T(8,128)S(1)} custom-call(s32[128]{0:T(128)S(1)} %fusion.12.codes, f32[8,2,128,128]{3,2,1,0:T(8,128)} %psi.7, f32[8,8,128,128]{3,2,1,0:T(8,128)} %left.7, f32[8,8,128,128]{3,2,1,0:T(8,128)} %right.7), custom_call_target="tpu_custom_call" | custom-call | flops 335544320 | bytes 5242880 | tf_op jit(solution)/shard_map/own_sums/pallas_call | solution.py:250
  31.5 0.2 fusion
  31.7 0.7 collective-permute-start.2
  32.4 1.4 %merge_sibling.3 = f32[3,2,16,2,64,128]{5,4,3,2,1,0:T(8,128)S(1)} custom-call(s32[128]{0:T(128)S(1)} %fusion.12.codes, f32[3,2,16,2,64,128]{5,4,3,2,1,0:T(8,128)S(1)} %own_sums.3.own, f32[10,2,128,128]{3,2,1,0:T(8,128)S(1)} %collective-permute-done.5.refs_0_, f32[10,2,128,128]{3,2,1,0:T(8,128)S(1)} %collective-permute-done.6.refs_1_), custom_call_target="tpu_custom_call", output_to_operand_aliasing={{}: (1, {})} | custom-call | tf_op jit(solution)/shard_map/merge_sibling/pallas_call | solution.py:264
  33.8 0.6 fusion.25
  34.4 0.1 copy.43
  34.5 3.1 %collective-permute-start.15 = (f32[2,4,2,64,128]{4,3,1,2,0:T(8,128)S(1)}, f32[2,4,2,64,128]{4,3,1,2,0:T(8,128)S(1)}, u32[]{:S(2)}, u32[]{:S(2)}) collective-permute-start(f32[2,4,2,64,128]{4,3,1,2,0:T(8,128)S(1)} %slice.149), channel_id=1, source_target_pairs={{0,12},{1,13},{2,14},{3,15},{4,0},{5,1},{6,2},{7,3},{8,4},{9,5},{1... | collective-permute-start | bytes 1572872 | tf_op jit(solution)/shard_map/ppermute | solution.py:328
  37.6 0.2 fusion.28
  38.0 1.4 %collective-permute-start.9 = (f32[12,2,64,128]{3,2,0,1:T(8,128)S(1)}, f32[12,2,64,128]{3,2,0,1:T(8,128)S(1)}, u32[]{:S(2)}, u32[]{:S(2)}) collective-permute-start(f32[12,2,64,128]{3,2,0,1:T(8,128)S(1)} %slice_bitcast_fusion.2), channel_id=1, source_target_pairs={{0,16},{1,3},{2,18},{3,1},{4,20},{5,7},{6,22},{7,5},{8,24},{9,11},... | collective-permute-start | bytes 2359304 | tf_op jit(solution)/shard_map/ppermute | solution.py:328
  39.4 7.2 %collective-permute-done.2 = f32[16,64,128]{2,1,0:T(8,128)S(1)} collective-permute-done((f32[16,64,128]{2,1,0:T(8,128)S(1)}, f32[16,64,128]{2,1,0:T(8,128)S(1)}, u32[]{:S(2)}, u32[]{:S(2)}) %collective-permute-start.2) | collective-permute-done | bytes 524320 | tf_op jit(solution)/shard_map/ppermute | solution.py:328
  46.7 2.5 %collective-permute-start.3 = (f32[16,64,128]{2,1,0:T(8,128)S(1)}, f32[16,64,128]{2,1,0:T(8,128)S(1)}, u32[]{:S(2)}, u32[]{:S(2)}) collective-permute-start(f32[16,64,128]{2,1,0:T(8,128)S(1)} %fusion.4), channel_id=1, source_target_pairs={{0,8},{1,9},{2,10},{3,11},{4,12},{5,13},{6,14},{7,15},{8,0},{9,1},... | collective-permute-start | bytes 1572872 | tf_op jit(solution)/shard_map/ppermute | solution.py:328
  49.2 0.1 fusion.2
  49.3 1.0 %collective-permute-start.7 = (f32[12,64,128]{2,1,0:T(8,128)S(1)}, f32[12,64,128]{2,1,0:T(8,128)S(1)}, u32[]{:S(2)}, u32[]{:S(2)}) collective-permute-start(f32[12,64,128]{2,1,0:T(8,128)S(1)} %slice_bitcast_fusion.12), channel_id=1, source_target_pairs={{0,2},{1,17},{2,0},{3,19},{4,6},{5,21},{6,4},{7,23},{8,10},{9,25},... | collective-permute-start | bytes 1179656 | tf_op jit(solution)/shard_map/ppermute | solution.py:328
  50.3 1.3 %collective-permute-start.12 = (f32[12,2,64,128]{3,2,0,1:T(8,128)S(1)}, f32[12,2,64,128]{3,2,0,1:T(8,128)S(1)}, u32[]{:S(2)}, u32[]{:S(2)}) collective-permute-start(f32[12,2,64,128]{3,2,0,1:T(8,128)S(1)} %bitcast.85), channel_id=1, source_target_pairs={{0,16},{1,3},{2,18},{3,1},{4,20},{5,7},{6,22},{7,5},{8,24},{9,11},... | collective-permute-start | bytes 2359304 | tf_op jit(solution)/shard_map/ppermute | solution.py:328
  51.7 0.1 slice_add_fusion
  51.8 9.6 %collective-permute-done.7 = f32[12,64,128]{2,1,0:T(8,128)S(1)} collective-permute-done((f32[12,64,128]{2,1,0:T(8,128)S(1)}, f32[12,64,128]{2,1,0:T(8,128)S(1)}, u32[]{:S(2)}, u32[]{:S(2)}) %collective-permute-start.7) | collective-permute-done | bytes 393248 | tf_op jit(solution)/shard_map/ppermute | solution.py:328
  61.5 1.3 %collective-permute-start.8 = (f32[12,64,128]{2,1,0:T(8,128)S(1)}, f32[12,64,128]{2,1,0:T(8,128)S(1)}, u32[]{:S(2)}, u32[]{:S(2)}) collective-permute-start(f32[12,64,128]{2,1,0:T(8,128)S(1)} %fusion.8), channel_id=1, source_target_pairs={{0,4},{1,5},{2,6},{3,7},{4,8},{5,9},{6,10},{7,11},{8,12},{9,13},{1... | collective-permute-start | bytes 1179656 | tf_op jit(solution)/shard_map/ppermute | solution.py:328
  62.8 0.1 fusion.1
  62.9 1.4 %collective-permute-start.16 = (f32[4,2,64,128]{3,2,1,0:T(8,128)S(1)}, f32[4,2,64,128]{3,2,1,0:T(8,128)S(1)}, u32[]{:S(2)}, u32[]{:S(2)}) collective-permute-start(f32[4,2,64,128]{3,2,1,0:T(8,128)S(1)} %slice_bitcast_fusion.14), channel_id=1, source_target_pairs={{0,16},{1,3},{2,18},{3,1},{4,20},{5,7},{6,22},{7,5},{8,24},{9,11},... | collective-permute-start | bytes 786440 | tf_op jit(solution)/shard_map/ppermute | solution.py:328
  64.3 0.8 collective-permute-start.10
  65.1 0.5 collective-permute-done.12
  65.6 0.1 fusion.3
  65.7 3.5 %collective-permute-start.13 = (f32[12,64,128]{2,1,0:T(8,128)S(1)}, f32[12,64,128]{2,1,0:T(8,128)S(1)}, u32[]{:S(2)}, u32[]{:S(2)}) collective-permute-start(f32[12,64,128]{2,1,0:T(8,128)S(1)} %slice_bitcast_fusion.8), channel_id=1, source_target_pairs={{0,2},{1,17},{2,0},{3,19},{4,6},{5,21},{6,4},{7,23},{8,10},{9,25},... | collective-permute-start | bytes 1179656 | tf_op jit(solution)/shard_map/ppermute | solution.py:328
  69.3 2.9 %collective-permute-done.16 = f32[4,2,64,128]{3,2,1,0:T(8,128)S(1)} collective-permute-done((f32[4,2,64,128]{3,2,1,0:T(8,128)S(1)}, f32[4,2,64,128]{3,2,1,0:T(8,128)S(1)}, u32[]{:S(2)}, u32[]{:S(2)}) %collective-permute-start.16) | collective-permute-done | bytes 262176 | tf_op jit(solution)/shard_map/ppermute | solution.py:328
  72.3 4.7 %collective-permute-start.11 = (f32[12,64,128]{2,1,0:T(8,128)S(1)}, f32[12,64,128]{2,1,0:T(8,128)S(1)}, u32[]{:S(2)}, u32[]{:S(2)}) collective-permute-start(f32[12,64,128]{2,1,0:T(8,128)S(1)} %fusion.7), channel_id=1, source_target_pairs={{0,12},{1,13},{2,14},{3,15},{4,0},{5,1},{6,2},{7,3},{8,4},{9,5},{1... | collective-permute-start | bytes 1179656 | tf_op jit(solution)/shard_map/ppermute | solution.py:328
  77.0 4.6 %collective-permute-done.3 = f32[16,64,128]{2,1,0:T(8,128)S(1)} collective-permute-done((f32[16,64,128]{2,1,0:T(8,128)S(1)}, f32[16,64,128]{2,1,0:T(8,128)S(1)}, u32[]{:S(2)}, u32[]{:S(2)}) %collective-permute-start.3) | collective-permute-done | bytes 524320 | tf_op jit(solution)/shard_map/ppermute | solution.py:328
  81.6 1.0 %collective-permute-start.17 = (f32[4,64,128]{2,1,0:T(8,128)S(1)}, f32[4,64,128]{2,1,0:T(8,128)S(1)}, u32[]{:S(2)}, u32[]{:S(2)}) collective-permute-start(f32[4,64,128]{2,1,0:T(8,128)S(1)} %slice_bitcast_fusion.17), channel_id=1, source_target_pairs={{0,2},{1,17},{2,0},{3,19},{4,6},{5,21},{6,4},{7,23},{8,10},{9,25},... | collective-permute-start | bytes 393224 | tf_op jit(solution)/shard_map/ppermute | solution.py:328
  82.6 4.0 %collective-permute-done.17 = f32[4,64,128]{2,1,0:T(8,128)S(1)} collective-permute-done((f32[4,64,128]{2,1,0:T(8,128)S(1)}, f32[4,64,128]{2,1,0:T(8,128)S(1)}, u32[]{:S(2)}, u32[]{:S(2)}) %collective-permute-start.17) | collective-permute-done | bytes 131104 | tf_op jit(solution)/shard_map/ppermute | solution.py:328
  86.7 2.9 %collective-permute-done.11 = f32[12,64,128]{2,1,0:T(8,128)S(1)} collective-permute-done((f32[12,64,128]{2,1,0:T(8,128)S(1)}, f32[12,64,128]{2,1,0:T(8,128)S(1)}, u32[]{:S(2)}, u32[]{:S(2)}) %collective-permute-start.11) | collective-permute-done | bytes 393248 | tf_op jit(solution)/shard_map/ppermute | solution.py:328
  89.5 0.2 fusion.6
  89.8 0.8 copy.20
  (38 shorter events, 1.1 us)
Async XLA Ops:
  6.6 5.9 %collective-permute-start = (f32[20,2,128,128]{3,2,1,0:T(8,128)S(1)}, f32[20,2,128,128]{3,2,1,0:T(8,128)S(1)}, u32[]{:S(2)}, u32[]{:S(2)}) collective-permute-start(f32[20,2,128,128]{3,2,1,0:T(8,128)S(1)} %sibling_contributions.2), channel_id=1, source_target_pairs={{0,1},{1,0},{2,3},{3,2},{4,5},{5,4},{6,7},{7,6},{8,9},{9,8},{10,11... | collective-permute-start | bytes 7864328 | tf_op jit(solution)/shard_map/ppermute | solution.py:328
  14.1 17.4 %collective-permute-start.1 = (f32[16,2,64,128]{3,2,0,1:T(8,128)S(1)}, f32[16,2,64,128]{3,2,0,1:T(8,128)S(1)}, u32[]{:S(2)}, u32[]{:S(2)}) collective-permute-start(f32[16,2,64,128]{3,2,0,1:T(8,128)S(1)} %bitcast.84), channel_id=1, source_target_pairs={{0,16},{1,3},{2,18},{3,1},{4,20},{5,7},{6,22},{7,5},{8,24},{9,11},... | collective-permute-start | bytes 3145736 | tf_op jit(solution)/shard_map/ppermute | solution.py:328
  22.0 10.4 %collective-permute-start.6 = (f32[10,2,128,128]{3,2,1,0:T(8,128)S(1)}, f32[10,2,128,128]{3,2,1,0:T(8,128)S(1)}, u32[]{:S(2)}, u32[]{:S(2)}) collective-permute-start(f32[10,2,128,128]{3,2,1,0:T(8,128)S(1)} %get-tuple-element.29), channel_id=1, source_target_pairs={{0,1},{1,0},{2,3},{3,2},{4,5},{5,4},{6,7},{7,6},{8,9},{9,8},{10,11... | collective-permute-start | bytes 3932168 | tf_op jit(solution)/shard_map/ppermute | solution.py:328
  22.4 10.0 %collective-permute-start.5 = (f32[10,2,128,128]{3,2,1,0:T(8,128)S(1)}, f32[10,2,128,128]{3,2,1,0:T(8,128)S(1)}, u32[]{:S(2)}, u32[]{:S(2)}) collective-permute-start(f32[10,2,128,128]{3,2,1,0:T(8,128)S(1)} %get-tuple-element.30), channel_id=1, source_target_pairs={{0,1},{1,0},{2,3},{3,2},{4,5},{5,4},{6,7},{7,6},{8,9},{9,8},{10,11... | collective-permute-start | bytes 3932168 | tf_op jit(solution)/shard_map/ppermute | solution.py:328
  22.8 27.5 %collective-permute-start.14 = (f32[2,4,2,64,128]{4,3,1,2,0:T(8,128)S(1)}, f32[2,4,2,64,128]{4,3,1,2,0:T(8,128)S(1)}, u32[]{:S(2)}, u32[]{:S(2)}) collective-permute-start(f32[2,4,2,64,128]{4,3,1,2,0:T(8,128)S(1)} %slice.148), channel_id=1, source_target_pairs={{0,4},{1,5},{2,6},{3,7},{4,8},{5,9},{6,10},{7,11},{8,12},{9,13},{1... | collective-permute-start | bytes 1572872 | tf_op jit(solution)/shard_map/ppermute | solution.py:328
  24.7 24.5 %collective-permute-start.4 = (f32[12,2,64,128]{3,2,0,1:T(8,128)S(1)}, f32[12,2,64,128]{3,2,0,1:T(8,128)S(1)}, u32[]{:S(2)}, u32[]{:S(2)}) collective-permute-start(f32[12,2,64,128]{3,2,0,1:T(8,128)S(1)} %slice_bitcast_fusion.4), channel_id=1, source_target_pairs={{0,16},{1,3},{2,18},{3,1},{4,20},{5,7},{6,22},{7,5},{8,24},{9,11},... | collective-permute-start | bytes 2359304 | tf_op jit(solution)/shard_map/ppermute | solution.py:328
  31.7 14.9 %collective-permute-start.2 = (f32[16,64,128]{2,1,0:T(8,128)S(1)}, f32[16,64,128]{2,1,0:T(8,128)S(1)}, u32[]{:S(2)}, u32[]{:S(2)}) collective-permute-start(f32[16,64,128]{2,1,0:T(8,128)S(1)} %slice_bitcast_fusion.6), channel_id=1, source_target_pairs={{0,2},{1,17},{2,0},{3,19},{4,6},{5,21},{6,4},{7,23},{8,10},{9,25},... | collective-permute-start | bytes 1572872 | tf_op jit(solution)/shard_map/ppermute | solution.py:328
  34.5 17.1 %collective-permute-start.15 = (f32[2,4,2,64,128]{4,3,1,2,0:T(8,128)S(1)}, f32[2,4,2,64,128]{4,3,1,2,0:T(8,128)S(1)}, u32[]{:S(2)}, u32[]{:S(2)}) collective-permute-start(f32[2,4,2,64,128]{4,3,1,2,0:T(8,128)S(1)} %slice.149), channel_id=1, source_target_pairs={{0,12},{1,13},{2,14},{3,15},{4,0},{5,1},{6,2},{7,3},{8,4},{9,5},{1... | collective-permute-start | bytes 1572872 | tf_op jit(solution)/shard_map/ppermute | solution.py:328
  38.0 24.8 %collective-permute-start.9 = (f32[12,2,64,128]{3,2,0,1:T(8,128)S(1)}, f32[12,2,64,128]{3,2,0,1:T(8,128)S(1)}, u32[]{:S(2)}, u32[]{:S(2)}) collective-permute-start(f32[12,2,64,128]{3,2,0,1:T(8,128)S(1)} %slice_bitcast_fusion.2), channel_id=1, source_target_pairs={{0,16},{1,3},{2,18},{3,1},{4,20},{5,7},{6,22},{7,5},{8,24},{9,11},... | collective-permute-start | bytes 2359304 | tf_op jit(solution)/shard_map/ppermute | solution.py:328
  46.7 34.9 %collective-permute-start.3 = (f32[16,64,128]{2,1,0:T(8,128)S(1)}, f32[16,64,128]{2,1,0:T(8,128)S(1)}, u32[]{:S(2)}, u32[]{:S(2)}) collective-permute-start(f32[16,64,128]{2,1,0:T(8,128)S(1)} %fusion.4), channel_id=1, source_target_pairs={{0,8},{1,9},{2,10},{3,11},{4,12},{5,13},{6,14},{7,15},{8,0},{9,1},... | collective-permute-start | bytes 1572872 | tf_op jit(solution)/shard_map/ppermute | solution.py:328
  49.3 12.1 %collective-permute-start.7 = (f32[12,64,128]{2,1,0:T(8,128)S(1)}, f32[12,64,128]{2,1,0:T(8,128)S(1)}, u32[]{:S(2)}, u32[]{:S(2)}) collective-permute-start(f32[12,64,128]{2,1,0:T(8,128)S(1)} %slice_bitcast_fusion.12), channel_id=1, source_target_pairs={{0,2},{1,17},{2,0},{3,19},{4,6},{5,21},{6,4},{7,23},{8,10},{9,25},... | collective-permute-start | bytes 1179656 | tf_op jit(solution)/shard_map/ppermute | solution.py:328
  50.3 15.3 %collective-permute-start.12 = (f32[12,2,64,128]{3,2,0,1:T(8,128)S(1)}, f32[12,2,64,128]{3,2,0,1:T(8,128)S(1)}, u32[]{:S(2)}, u32[]{:S(2)}) collective-permute-start(f32[12,2,64,128]{3,2,0,1:T(8,128)S(1)} %bitcast.85), channel_id=1, source_target_pairs={{0,16},{1,3},{2,18},{3,1},{4,20},{5,7},{6,22},{7,5},{8,24},{9,11},... | collective-permute-start | bytes 2359304 | tf_op jit(solution)/shard_map/ppermute | solution.py:328
  61.5 25.1 %collective-permute-start.8 = (f32[12,64,128]{2,1,0:T(8,128)S(1)}, f32[12,64,128]{2,1,0:T(8,128)S(1)}, u32[]{:S(2)}, u32[]{:S(2)}) collective-permute-start(f32[12,64,128]{2,1,0:T(8,128)S(1)} %fusion.8), channel_id=1, source_target_pairs={{0,4},{1,5},{2,6},{3,7},{4,8},{5,9},{6,10},{7,11},{8,12},{9,13},{1... | collective-permute-start | bytes 1179656 | tf_op jit(solution)/shard_map/ppermute | solution.py:328
  62.9 9.3 %collective-permute-start.16 = (f32[4,2,64,128]{3,2,1,0:T(8,128)S(1)}, f32[4,2,64,128]{3,2,1,0:T(8,128)S(1)}, u32[]{:S(2)}, u32[]{:S(2)}) collective-permute-start(f32[4,2,64,128]{3,2,1,0:T(8,128)S(1)} %slice_bitcast_fusion.14), channel_id=1, source_target_pairs={{0,16},{1,3},{2,18},{3,1},{4,20},{5,7},{6,22},{7,5},{8,24},{9,11},... | collective-permute-start | bytes 786440 | tf_op jit(solution)/shard_map/ppermute | solution.py:328
  64.3 7.9 %collective-permute-start.10 = (f32[12,64,128]{2,1,0:T(8,128)S(1)}, f32[12,64,128]{2,1,0:T(8,128)S(1)}, u32[]{:S(2)}, u32[]{:S(2)}) collective-permute-start(f32[12,64,128]{2,1,0:T(8,128)S(1)} %slice_bitcast_fusion.10), channel_id=1, source_target_pairs={{0,2},{1,17},{2,0},{3,19},{4,6},{5,21},{6,4},{7,23},{8,10},{9,25},... | collective-permute-start | bytes 1179656 | tf_op jit(solution)/shard_map/ppermute | solution.py:328
  65.7 20.9 %collective-permute-start.13 = (f32[12,64,128]{2,1,0:T(8,128)S(1)}, f32[12,64,128]{2,1,0:T(8,128)S(1)}, u32[]{:S(2)}, u32[]{:S(2)}) collective-permute-start(f32[12,64,128]{2,1,0:T(8,128)S(1)} %slice_bitcast_fusion.8), channel_id=1, source_target_pairs={{0,2},{1,17},{2,0},{3,19},{4,6},{5,21},{6,4},{7,23},{8,10},{9,25},... | collective-permute-start | bytes 1179656 | tf_op jit(solution)/shard_map/ppermute | solution.py:328
  72.3 17.2 %collective-permute-start.11 = (f32[12,64,128]{2,1,0:T(8,128)S(1)}, f32[12,64,128]{2,1,0:T(8,128)S(1)}, u32[]{:S(2)}, u32[]{:S(2)}) collective-permute-start(f32[12,64,128]{2,1,0:T(8,128)S(1)} %fusion.7), channel_id=1, source_target_pairs={{0,12},{1,13},{2,14},{3,15},{4,0},{5,1},{6,2},{7,3},{8,4},{9,5},{1... | collective-permute-start | bytes 1179656 | tf_op jit(solution)/shard_map/ppermute | solution.py:328
  81.6 5.0 %collective-permute-start.17 = (f32[4,64,128]{2,1,0:T(8,128)S(1)}, f32[4,64,128]{2,1,0:T(8,128)S(1)}, u32[]{:S(2)}, u32[]{:S(2)}) collective-permute-start(f32[4,64,128]{2,1,0:T(8,128)S(1)} %slice_bitcast_fusion.17), channel_id=1, source_target_pairs={{0,2},{1,17},{2,0},{3,19},{4,6},{5,21},{6,4},{7,23},{8,10},{9,25},... | collective-permute-start | bytes 393224 | tf_op jit(solution)/shard_map/ppermute | solution.py:328

commit v5 on v4

--- a/solution.py
+++ b/solution.py
@@ -72,7 +72,11 @@
 
         return count + hit.astype(jnp.int32)
 
-    return lax.fori_loop(0, pairs, one, jnp.int32(0), unroll=4)
+    return lax.fori_loop(0, pairs, one, jnp.int32(0), unroll=16)
+
+
+def row_of(other, pairs):
+    return ((lax.axis_index("sec") + other) % CORES) * pairs
 
 
 def padded(count, group, take, row):
@@ -109,7 +113,7 @@
         for copy in fetch(left, right, left_buf, right_buf, sems, p, i, sectors):
             copy.start()
 
-    count = collect(codes, 0, terms * sectors, low, size, take)
+    count = collect(codes, row_of(0, terms * sectors), terms * sectors, low, size, take)
     groups = padded(count, group, take, 0)
     prepare(psi, psi_raw, psi_pairs, psi_sem)
 
@@ -157,7 +161,7 @@
         for copy in fetch(left, right, left_buf, right_buf, sems, p, i, sectors):
             copy.start()
 
-    count = collect(codes, 0, terms * sectors, low, size, take)
+    count = collect(codes, row_of(0, terms * sectors), terms * sectors, low, size, take)
     groups = padded(count, group, take, size)
 
     def clear(t, carry):
@@ -187,7 +191,7 @@
     def take(i, p, row):
         rows[i] = row
 
-    count = collect(codes, pairs, pairs, low, size, take)
+    count = collect(codes, row_of(1, pairs), pairs, low, size, take)
     add = adder(total, x_count)
     start = 0
     for piece in arrived:
@@ -287,13 +291,11 @@
     chunks = [list(range(depth // 2, 0, -1)), [*range(depth // 2 + 1, depth), 0]]
     order = [r for chunk in chunks for r in chunk]
 
-    def rows_of(table):
-        return jnp.concatenate(
-            [lax.dynamic_slice_in_dim(table, d, 1, 0) for d in (me, me + 1 - 2 * c)]
-        ).reshape(2 * pairs)
-
-    owner = rows_of(target_owner[0, :, :, :, 0].reshape(sec_count, pairs))
-    local = rows_of(target_local[0].reshape(sec_count, pairs))
+    def of_chip(table):
+        return lax.dynamic_slice_in_dim(table, me - c, CORES, 0).reshape(CORES * pairs)
+
+    owner = of_chip(target_owner.reshape(sec_count, pairs))
+    local = of_chip(target_local.reshape(sec_count, pairs))
     z_rel = (owner // (CORES * PLANES) - z + depth) % depth
     z_place = sum(jnp.where(z_rel == r, i, 0) for i, r in enumerate(order))
     y_rel = ((owner // CORES) % PLANES - y + PLANES) % PLANES

time: 91 us -> 90.6 us (level)
  transfers between devices with their start and end apart: 18 -> 18, of which waited for: 7 -> 8; matrix products, arithmetic and copies ran while one was open for 3% -> 3% of each run, Pallas kernels for 19% -> 19%
where the time goes in v5:
time: 90.6 us; the launch traced here: 90.2 us
  waiting for transfers between devices  31.1 us (34%)
  starting transfers between devices  30.3 us (33%)
  Pallas kernels  23.2 us (26%)
  local copies, waits for them, and re-layouts  4.2 us (5%)
  other arithmetic  1.12 us (1%)
    ppermute x18, waiting for transfers between devices, send(): return lax.ppermute(message, ('ops', 'sec'), perm)  31.1 us
    ppermute x18, starting transfers between devices, send(): return lax.ppermute(message, ('ops', 'sec'), perm)  30.3 us
    pallas_call x2, Pallas kernels, run_own(): pl.pallas_call(functools.partial(own_kernel, low, size, group_of(slots),...  10.5 us
    pallas_call x2, Pallas kernels, run_sibling(): pl.pallas_call(functools.partial(sibling_kernel, low, size, group_of(slot...  10.3 us
    pallas_call x2, Pallas kernels, run_merge(): pl.pallas_call(functools.partial(merge_kernel, low, size, x_count, pairs)...  2.5 us
  transfers between devices with their start and end apart: 18, of which 8 were waited for; matrix products, arithmetic and copies ran while one was open for 3% of the time, Pallas kernels for 19%

profile of v5, /device:TPU:0, one launch (start us, length us, event | category | flops | bytes accessed | tf_op | source)
XLA Modules:
  0.0 90.2 jit_solution(15575020034007720345)
XLA Ops:
  0.0 0.8 constant_dynamic-slice_fusion
  1.1 0.1 reshape.17
  1.2 5.1 %sibling_contributions.2 = f32[20,2,128,128]{3,2,1,0:T(8,128)S(1)} custom-call(s32[128]{0:T(128)S(1)} %fusion.12.codes, f32[8,2,128,128]{3,2,1,0:T(8,128)} %psi.7, f32[8,8,128,128]{3,2,1,0:T(8,128)} %left.7, f32[8,8,128,128]{3,2,1,0:T(8,128)} %right.7), custom_call_target="tpu_custom_call" | custom-call | flops 335544320 | bytes 5242880 | tf_op jit(solution)/shard_map/sibling_contributions/pallas_call | solution.py:237
  6.4 0.5 collective-permute-start
  6.9 5.3 %own_sums.2.own = f32[3,2,16,2,64,128]{5,4,3,2,1,0:T(8,128)S(1)} custom-call(s32[128]{0:T(128)S(1)} %fusion.12.codes, f32[8,2,128,128]{3,2,1,0:T(8,128)} %psi.7, f32[8,8,128,128]{3,2,1,0:T(8,128)} %left.7, f32[8,8,128,128]{3,2,1,0:T(8,128)} %right.7), custom_call_target="tpu_custom_call" | custom-call | flops 335544320 | bytes 5242880 | tf_op jit(solution)/shard_map/own_sums/pallas_call | solution.py:254
  12.1 1.3 %merge_sibling.2 = f32[3,2,16,2,64,128]{5,4,3,2,1,0:T(8,128)S(1)} custom-call(s32[128]{0:T(128)S(1)} %fusion.12.codes, f32[3,2,16,2,64,128]{5,4,3,2,1,0:T(8,128)S(1)} %own_sums.2.own, f32[20,2,128,128]{3,2,1,0:T(8,128)S(1)} %collective-permute-done.refs_0_), custom_call_target="tpu_custom_call", output_to_operand_aliasing={{}: (1, {})} | custom-call | tf_op jit(solution)/shard_map/merge_sibling/pallas_call | solution.py:268
  13.4 0.2 fusion.26
  13.7 0.1 copy.40
  13.8 2.5 %collective-permute-start.1 = (f32[16,2,64,128]{3,2,0,1:T(8,128)S(1)}, f32[16,2,64,128]{3,2,0,1:T(8,128)S(1)}, u32[]{:S(2)}, u32[]{:S(2)}) collective-permute-start(f32[16,2,64,128]{3,2,0,1:T(8,128)S(1)} %bitcast.84), channel_id=1, source_target_pairs={{0,16},{1,3},{2,18},{3,1},{4,20},{5,7},{6,22},{7,5},{8,24},{9,11},... | collective-permute-start | bytes 3145736 | tf_op jit(solution)/shard_map/ppermute | solution.py:330
  16.3 5.1 %sibling_contributions.3 = f32[20,2,128,128]{3,2,1,0:T(8,128)S(1)} custom-call(s32[128]{0:T(128)S(1)} %fusion.12.codes, f32[8,2,128,128]{3,2,1,0:T(8,128)} %psi.7, f32[8,8,128,128]{3,2,1,0:T(8,128)} %left.7, f32[8,8,128,128]{3,2,1,0:T(8,128)} %right.7), custom_call_target="tpu_custom_call" | custom-call | flops 335544320 | bytes 5242880 | tf_op jit(solution)/shard_map/sibling_contributions/pallas_call | solution.py:237
  21.5 0.3 fusion.27
  21.8 0.2 collective-permute-start.6
  22.0 0.3 collective-permute-start.5
  22.3 0.2 copy_bitcast_fusion.1
  22.6 1.6 %collective-permute-start.14 = (f32[2,4,2,64,128]{4,3,1,2,0:T(8,128)S(1)}, f32[2,4,2,64,128]{4,3,1,2,0:T(8,128)S(1)}, u32[]{:S(2)}, u32[]{:S(2)}) collective-permute-start(f32[2,4,2,64,128]{4,3,1,2,0:T(8,128)S(1)} %slice.148), channel_id=1, source_target_pairs={{0,4},{1,5},{2,6},{3,7},{4,8},{5,9},{6,10},{7,11},{8,12},{9,13},{1... | collective-permute-start | bytes 1572872 | tf_op jit(solution)/shard_map/ppermute | solution.py:330
  24.3 1.4 %collective-permute-start.4 = (f32[12,2,64,128]{3,2,0,1:T(8,128)S(1)}, f32[12,2,64,128]{3,2,0,1:T(8,128)S(1)}, u32[]{:S(2)}, u32[]{:S(2)}) collective-permute-start(f32[12,2,64,128]{3,2,0,1:T(8,128)S(1)} %slice_bitcast_fusion.4), channel_id=1, source_target_pairs={{0,16},{1,3},{2,18},{3,1},{4,20},{5,7},{6,22},{7,5},{8,24},{9,11},... | collective-permute-start | bytes 2359304 | tf_op jit(solution)/shard_map/ppermute | solution.py:330
  25.7 5.2 %own_sums.3.own = f32[3,2,16,2,64,128]{5,4,3,2,1,0:T(8,128)S(1)} custom-call(s32[128]{0:T(128)S(1)} %fusion.12.codes, f32[8,2,128,128]{3,2,1,0:T(8,128)} %psi.7, f32[8,8,128,128]{3,2,1,0:T(8,128)} %left.7, f32[8,8,128,128]{3,2,1,0:T(8,128)} %right.7), custom_call_target="tpu_custom_call" | custom-call | flops 335544320 | bytes 5242880 | tf_op jit(solution)/shard_map/own_sums/pallas_call | solution.py:254
  31.0 0.2 fusion
  31.2 0.8 collective-permute-start.2
  32.0 1.2 %merge_sibling.3 = f32[3,2,16,2,64,128]{5,4,3,2,1,0:T(8,128)S(1)} custom-call(s32[128]{0:T(128)S(1)} %fusion.12.codes, f32[3,2,16,2,64,128]{5,4,3,2,1,0:T(8,128)S(1)} %own_sums.3.own, f32[10,2,128,128]{3,2,1,0:T(8,128)S(1)} %collective-permute-done.5.refs_0_, f32[10,2,128,128]{3,2,1,0:T(8,128)S(1)} %collective-permute-done.6.refs_1_), custom_call_target="tpu_custom_call", output_to_operand_aliasing={{}: (1, {})} | custom-call | tf_op jit(solution)/shard_map/merge_sibling/pallas_call | solution.py:268
  33.2 0.6 fusion.25
  33.8 0.1 copy.39
  34.0 3.1 %collective-permute-start.15 = (f32[2,4,2,64,128]{4,3,1,2,0:T(8,128)S(1)}, f32[2,4,2,64,128]{4,3,1,2,0:T(8,128)S(1)}, u32[]{:S(2)}, u32[]{:S(2)}) collective-permute-start(f32[2,4,2,64,128]{4,3,1,2,0:T(8,128)S(1)} %slice.149), channel_id=1, source_target_pairs={{0,12},{1,13},{2,14},{3,15},{4,0},{5,1},{6,2},{7,3},{8,4},{9,5},{1... | collective-permute-start | bytes 1572872 | tf_op jit(solution)/shard_map/ppermute | solution.py:330
  37.1 0.2 fusion.28
  37.4 1.5 %collective-permute-start.9 = (f32[12,2,64,128]{3,2,0,1:T(8,128)S(1)}, f32[12,2,64,128]{3,2,0,1:T(8,128)S(1)}, u32[]{:S(2)}, u32[]{:S(2)}) collective-permute-start(f32[12,2,64,128]{3,2,0,1:T(8,128)S(1)} %slice_bitcast_fusion.2), channel_id=1, source_target_pairs={{0,16},{1,3},{2,18},{3,1},{4,20},{5,7},{6,22},{7,5},{8,24},{9,11},... | collective-permute-start | bytes 2359304 | tf_op jit(solution)/shard_map/ppermute | solution.py:330
  39.0 7.1 %collective-permute-done.2 = f32[16,64,128]{2,1,0:T(8,128)S(1)} collective-permute-done((f32[16,64,128]{2,1,0:T(8,128)S(1)}, f32[16,64,128]{2,1,0:T(8,128)S(1)}, u32[]{:S(2)}, u32[]{:S(2)}) %collective-permute-start.2) | collective-permute-done | bytes 524320 | tf_op jit(solution)/shard_map/ppermute | solution.py:330
  46.2 2.7 %collective-permute-start.3 = (f32[16,64,128]{2,1,0:T(8,128)S(1)}, f32[16,64,128]{2,1,0:T(8,128)S(1)}, u32[]{:S(2)}, u32[]{:S(2)}) collective-permute-start(f32[16,64,128]{2,1,0:T(8,128)S(1)} %fusion.4), channel_id=1, source_target_pairs={{0,8},{1,9},{2,10},{3,11},{4,12},{5,13},{6,14},{7,15},{8,0},{9,1},... | collective-permute-start | bytes 1572872 | tf_op jit(solution)/shard_map/ppermute | solution.py:330
  48.9 0.1 fusion.2
  49.0 0.9 collective-permute-start.7
  49.9 1.5 %collective-permute-start.12 = (f32[12,2,64,128]{3,2,0,1:T(8,128)S(1)}, f32[12,2,64,128]{3,2,0,1:T(8,128)S(1)}, u32[]{:S(2)}, u32[]{:S(2)}) collective-permute-start(f32[12,2,64,128]{3,2,0,1:T(8,128)S(1)} %bitcast.85), channel_id=1, source_target_pairs={{0,16},{1,3},{2,18},{3,1},{4,20},{5,7},{6,22},{7,5},{8,24},{9,11},... | collective-permute-start | bytes 2359304 | tf_op jit(solution)/shard_map/ppermute | solution.py:330
  51.4 0.1 slice_add_fusion
  51.5 9.6 %collective-permute-done.7 = f32[12,64,128]{2,1,0:T(8,128)S(1)} collective-permute-done((f32[12,64,128]{2,1,0:T(8,128)S(1)}, f32[12,64,128]{2,1,0:T(8,128)S(1)}, u32[]{:S(2)}, u32[]{:S(2)}) %collective-permute-start.7) | collective-permute-done | bytes 393248 | tf_op jit(solution)/shard_map/ppermute | solution.py:330
  61.2 0.9 %collective-permute-start.8 = (f32[12,64,128]{2,1,0:T(8,128)S(1)}, f32[12,64,128]{2,1,0:T(8,128)S(1)}, u32[]{:S(2)}, u32[]{:S(2)}) collective-permute-start(f32[12,64,128]{2,1,0:T(8,128)S(1)} %fusion.8), channel_id=1, source_target_pairs={{0,4},{1,5},{2,6},{3,7},{4,8},{5,9},{6,10},{7,11},{8,12},{9,13},{1... | collective-permute-start | bytes 1179656 | tf_op jit(solution)/shard_map/ppermute | solution.py:330
  62.1 0.1 fusion.1
  62.2 1.6 %collective-permute-start.16 = (f32[4,2,64,128]{3,2,1,0:T(8,128)S(1)}, f32[4,2,64,128]{3,2,1,0:T(8,128)S(1)}, u32[]{:S(2)}, u32[]{:S(2)}) collective-permute-start(f32[4,2,64,128]{3,2,1,0:T(8,128)S(1)} %slice_bitcast_fusion.14), channel_id=1, source_target_pairs={{0,16},{1,3},{2,18},{3,1},{4,20},{5,7},{6,22},{7,5},{8,24},{9,11},... | collective-permute-start | bytes 786440 | tf_op jit(solution)/shard_map/ppermute | solution.py:330
  63.8 0.9 %collective-permute-start.10 = (f32[12,64,128]{2,1,0:T(8,128)S(1)}, f32[12,64,128]{2,1,0:T(8,128)S(1)}, u32[]{:S(2)}, u32[]{:S(2)}) collective-permute-start(f32[12,64,128]{2,1,0:T(8,128)S(1)} %slice_bitcast_fusion.10), channel_id=1, source_target_pairs={{0,2},{1,17},{2,0},{3,19},{4,6},{5,21},{6,4},{7,23},{8,10},{9,25},... | collective-permute-start | bytes 1179656 | tf_op jit(solution)/shard_map/ppermute | solution.py:330
  64.8 0.7 collective-permute-done.12
  65.4 0.1 fusion.3
  65.6 3.4 %collective-permute-start.13 = (f32[12,64,128]{2,1,0:T(8,128)S(1)}, f32[12,64,128]{2,1,0:T(8,128)S(1)}, u32[]{:S(2)}, u32[]{:S(2)}) collective-permute-start(f32[12,64,128]{2,1,0:T(8,128)S(1)} %slice_bitcast_fusion.8), channel_id=1, source_target_pairs={{0,2},{1,17},{2,0},{3,19},{4,6},{5,21},{6,4},{7,23},{8,10},{9,25},... | collective-permute-start | bytes 1179656 | tf_op jit(solution)/shard_map/ppermute | solution.py:330
  69.0 2.5 %collective-permute-done.16 = f32[4,2,64,128]{3,2,1,0:T(8,128)S(1)} collective-permute-done((f32[4,2,64,128]{3,2,1,0:T(8,128)S(1)}, f32[4,2,64,128]{3,2,1,0:T(8,128)S(1)}, u32[]{:S(2)}, u32[]{:S(2)}) %collective-permute-start.16) | collective-permute-done | bytes 262176 | tf_op jit(solution)/shard_map/ppermute | solution.py:330
  71.6 0.1 collective-permute-done.10
  71.7 4.9 %collective-permute-start.11 = (f32[12,64,128]{2,1,0:T(8,128)S(1)}, f32[12,64,128]{2,1,0:T(8,128)S(1)}, u32[]{:S(2)}, u32[]{:S(2)}) collective-permute-start(f32[12,64,128]{2,1,0:T(8,128)S(1)} %fusion.7), channel_id=1, source_target_pairs={{0,12},{1,13},{2,14},{3,15},{4,0},{5,1},{6,2},{7,3},{8,4},{9,5},{1... | collective-permute-start | bytes 1179656 | tf_op jit(solution)/shard_map/ppermute | solution.py:330
  76.7 4.3 %collective-permute-done.3 = f32[16,64,128]{2,1,0:T(8,128)S(1)} collective-permute-done((f32[16,64,128]{2,1,0:T(8,128)S(1)}, f32[16,64,128]{2,1,0:T(8,128)S(1)}, u32[]{:S(2)}, u32[]{:S(2)}) %collective-permute-start.3) | collective-permute-done | bytes 524320 | tf_op jit(solution)/shard_map/ppermute | solution.py:330
  81.0 1.4 %collective-permute-start.17 = (f32[4,64,128]{2,1,0:T(8,128)S(1)}, f32[4,64,128]{2,1,0:T(8,128)S(1)}, u32[]{:S(2)}, u32[]{:S(2)}) collective-permute-start(f32[4,64,128]{2,1,0:T(8,128)S(1)} %slice_bitcast_fusion.17), channel_id=1, source_target_pairs={{0,2},{1,17},{2,0},{3,19},{4,6},{5,21},{6,4},{7,23},{8,10},{9,25},... | collective-permute-start | bytes 393224 | tf_op jit(solution)/shard_map/ppermute | solution.py:330
  82.3 3.6 %collective-permute-done.17 = f32[4,64,128]{2,1,0:T(8,128)S(1)} collective-permute-done((f32[4,64,128]{2,1,0:T(8,128)S(1)}, f32[4,64,128]{2,1,0:T(8,128)S(1)}, u32[]{:S(2)}, u32[]{:S(2)}) %collective-permute-start.17) | collective-permute-done | bytes 131104 | tf_op jit(solution)/shard_map/ppermute | solution.py:330
  86.0 3.1 %collective-permute-done.11 = f32[12,64,128]{2,1,0:T(8,128)S(1)} collective-permute-done((f32[12,64,128]{2,1,0:T(8,128)S(1)}, f32[12,64,128]{2,1,0:T(8,128)S(1)}, u32[]{:S(2)}, u32[]{:S(2)}) %collective-permute-start.11) | collective-permute-done | bytes 393248 | tf_op jit(solution)/shard_map/ppermute | solution.py:330
  89.1 0.2 fusion.6
  89.4 0.8 copy.18
  (34 shorter events, 1.1 us)
Async XLA Ops:
  6.4 5.8 %collective-permute-start = (f32[20,2,128,128]{3,2,1,0:T(8,128)S(1)}, f32[20,2,128,128]{3,2,1,0:T(8,128)S(1)}, u32[]{:S(2)}, u32[]{:S(2)}) collective-permute-start(f32[20,2,128,128]{3,2,1,0:T(8,128)S(1)} %sibling_contributions.2), channel_id=1, source_target_pairs={{0,1},{1,0},{2,3},{3,2},{4,5},{5,4},{6,7},{7,6},{8,9},{9,8},{10,11... | collective-permute-start | bytes 7864328 | tf_op jit(solution)/shard_map/ppermute | solution.py:330
  13.8 17.2 %collective-permute-start.1 = (f32[16,2,64,128]{3,2,0,1:T(8,128)S(1)}, f32[16,2,64,128]{3,2,0,1:T(8,128)S(1)}, u32[]{:S(2)}, u32[]{:S(2)}) collective-permute-start(f32[16,2,64,128]{3,2,0,1:T(8,128)S(1)} %bitcast.84), channel_id=1, source_target_pairs={{0,16},{1,3},{2,18},{3,1},{4,20},{5,7},{6,22},{7,5},{8,24},{9,11},... | collective-permute-start | bytes 3145736 | tf_op jit(solution)/shard_map/ppermute | solution.py:330
  21.8 10.3 %collective-permute-start.6 = (f32[10,2,128,128]{3,2,1,0:T(8,128)S(1)}, f32[10,2,128,128]{3,2,1,0:T(8,128)S(1)}, u32[]{:S(2)}, u32[]{:S(2)}) collective-permute-start(f32[10,2,128,128]{3,2,1,0:T(8,128)S(1)} %get-tuple-element.29), channel_id=1, source_target_pairs={{0,1},{1,0},{2,3},{3,2},{4,5},{5,4},{6,7},{7,6},{8,9},{9,8},{10,11... | collective-permute-start | bytes 3932168 | tf_op jit(solution)/shard_map/ppermute | solution.py:330
  22.0 10.0 %collective-permute-start.5 = (f32[10,2,128,128]{3,2,1,0:T(8,128)S(1)}, f32[10,2,128,128]{3,2,1,0:T(8,128)S(1)}, u32[]{:S(2)}, u32[]{:S(2)}) collective-permute-start(f32[10,2,128,128]{3,2,1,0:T(8,128)S(1)} %get-tuple-element.30), channel_id=1, source_target_pairs={{0,1},{1,0},{2,3},{3,2},{4,5},{5,4},{6,7},{7,6},{8,9},{9,8},{10,11... | collective-permute-start | bytes 3932168 | tf_op jit(solution)/shard_map/ppermute | solution.py:330
  22.6 27.2 %collective-permute-start.14 = (f32[2,4,2,64,128]{4,3,1,2,0:T(8,128)S(1)}, f32[2,4,2,64,128]{4,3,1,2,0:T(8,128)S(1)}, u32[]{:S(2)}, u32[]{:S(2)}) collective-permute-start(f32[2,4,2,64,128]{4,3,1,2,0:T(8,128)S(1)} %slice.148), channel_id=1, source_target_pairs={{0,4},{1,5},{2,6},{3,7},{4,8},{5,9},{6,10},{7,11},{8,12},{9,13},{1... | collective-permute-start | bytes 1572872 | tf_op jit(solution)/shard_map/ppermute | solution.py:330
  24.3 24.5 %collective-permute-start.4 = (f32[12,2,64,128]{3,2,0,1:T(8,128)S(1)}, f32[12,2,64,128]{3,2,0,1:T(8,128)S(1)}, u32[]{:S(2)}, u32[]{:S(2)}) collective-permute-start(f32[12,2,64,128]{3,2,0,1:T(8,128)S(1)} %slice_bitcast_fusion.4), channel_id=1, source_target_pairs={{0,16},{1,3},{2,18},{3,1},{4,20},{5,7},{6,22},{7,5},{8,24},{9,11},... | collective-permute-start | bytes 2359304 | tf_op jit(solution)/shard_map/ppermute | solution.py:330
  31.2 14.9 %collective-permute-start.2 = (f32[16,64,128]{2,1,0:T(8,128)S(1)}, f32[16,64,128]{2,1,0:T(8,128)S(1)}, u32[]{:S(2)}, u32[]{:S(2)}) collective-permute-start(f32[16,64,128]{2,1,0:T(8,128)S(1)} %slice_bitcast_fusion.6), channel_id=1, source_target_pairs={{0,2},{1,17},{2,0},{3,19},{4,6},{5,21},{6,4},{7,23},{8,10},{9,25},... | collective-permute-start | bytes 1572872 | tf_op jit(solution)/shard_map/ppermute | solution.py:330
  34.0 17.3 %collective-permute-start.15 = (f32[2,4,2,64,128]{4,3,1,2,0:T(8,128)S(1)}, f32[2,4,2,64,128]{4,3,1,2,0:T(8,128)S(1)}, u32[]{:S(2)}, u32[]{:S(2)}) collective-permute-start(f32[2,4,2,64,128]{4,3,1,2,0:T(8,128)S(1)} %slice.149), channel_id=1, source_target_pairs={{0,12},{1,13},{2,14},{3,15},{4,0},{5,1},{6,2},{7,3},{8,4},{9,5},{1... | collective-permute-start | bytes 1572872 | tf_op jit(solution)/shard_map/ppermute | solution.py:330
  37.4 24.6 %collective-permute-start.9 = (f32[12,2,64,128]{3,2,0,1:T(8,128)S(1)}, f32[12,2,64,128]{3,2,0,1:T(8,128)S(1)}, u32[]{:S(2)}, u32[]{:S(2)}) collective-permute-start(f32[12,2,64,128]{3,2,0,1:T(8,128)S(1)} %slice_bitcast_fusion.2), channel_id=1, source_target_pairs={{0,16},{1,3},{2,18},{3,1},{4,20},{5,7},{6,22},{7,5},{8,24},{9,11},... | collective-permute-start | bytes 2359304 | tf_op jit(solution)/shard_map/ppermute | solution.py:330
  46.2 34.8 %collective-permute-start.3 = (f32[16,64,128]{2,1,0:T(8,128)S(1)}, f32[16,64,128]{2,1,0:T(8,128)S(1)}, u32[]{:S(2)}, u32[]{:S(2)}) collective-permute-start(f32[16,64,128]{2,1,0:T(8,128)S(1)} %fusion.4), channel_id=1, source_target_pairs={{0,8},{1,9},{2,10},{3,11},{4,12},{5,13},{6,14},{7,15},{8,0},{9,1},... | collective-permute-start | bytes 1572872 | tf_op jit(solution)/shard_map/ppermute | solution.py:330
  49.0 12.1 %collective-permute-start.7 = (f32[12,64,128]{2,1,0:T(8,128)S(1)}, f32[12,64,128]{2,1,0:T(8,128)S(1)}, u32[]{:S(2)}, u32[]{:S(2)}) collective-permute-start(f32[12,64,128]{2,1,0:T(8,128)S(1)} %slice_bitcast_fusion.12), channel_id=1, source_target_pairs={{0,2},{1,17},{2,0},{3,19},{4,6},{5,21},{6,4},{7,23},{8,10},{9,25},... | collective-permute-start | bytes 1179656 | tf_op jit(solution)/shard_map/ppermute | solution.py:330
  49.9 15.6 %collective-permute-start.12 = (f32[12,2,64,128]{3,2,0,1:T(8,128)S(1)}, f32[12,2,64,128]{3,2,0,1:T(8,128)S(1)}, u32[]{:S(2)}, u32[]{:S(2)}) collective-permute-start(f32[12,2,64,128]{3,2,0,1:T(8,128)S(1)} %bitcast.85), channel_id=1, source_target_pairs={{0,16},{1,3},{2,18},{3,1},{4,20},{5,7},{6,22},{7,5},{8,24},{9,11},... | collective-permute-start | bytes 2359304 | tf_op jit(solution)/shard_map/ppermute | solution.py:330
  61.2 24.8 %collective-permute-start.8 = (f32[12,64,128]{2,1,0:T(8,128)S(1)}, f32[12,64,128]{2,1,0:T(8,128)S(1)}, u32[]{:S(2)}, u32[]{:S(2)}) collective-permute-start(f32[12,64,128]{2,1,0:T(8,128)S(1)} %fusion.8), channel_id=1, source_target_pairs={{0,4},{1,5},{2,6},{3,7},{4,8},{5,9},{6,10},{7,11},{8,12},{9,13},{1... | collective-permute-start | bytes 1179656 | tf_op jit(solution)/shard_map/ppermute | solution.py:330
  62.2 9.3 %collective-permute-start.16 = (f32[4,2,64,128]{3,2,1,0:T(8,128)S(1)}, f32[4,2,64,128]{3,2,1,0:T(8,128)S(1)}, u32[]{:S(2)}, u32[]{:S(2)}) collective-permute-start(f32[4,2,64,128]{3,2,1,0:T(8,128)S(1)} %slice_bitcast_fusion.14), channel_id=1, source_target_pairs={{0,16},{1,3},{2,18},{3,1},{4,20},{5,7},{6,22},{7,5},{8,24},{9,11},... | collective-permute-start | bytes 786440 | tf_op jit(solution)/shard_map/ppermute | solution.py:330
  63.8 7.8 %collective-permute-start.10 = (f32[12,64,128]{2,1,0:T(8,128)S(1)}, f32[12,64,128]{2,1,0:T(8,128)S(1)}, u32[]{:S(2)}, u32[]{:S(2)}) collective-permute-start(f32[12,64,128]{2,1,0:T(8,128)S(1)} %slice_bitcast_fusion.10), channel_id=1, source_target_pairs={{0,2},{1,17},{2,0},{3,19},{4,6},{5,21},{6,4},{7,23},{8,10},{9,25},... | collective-permute-start | bytes 1179656 | tf_op jit(solution)/shard_map/ppermute | solution.py:330
  65.6 20.4 %collective-permute-start.13 = (f32[12,64,128]{2,1,0:T(8,128)S(1)}, f32[12,64,128]{2,1,0:T(8,128)S(1)}, u32[]{:S(2)}, u32[]{:S(2)}) collective-permute-start(f32[12,64,128]{2,1,0:T(8,128)S(1)} %slice_bitcast_fusion.8), channel_id=1, source_target_pairs={{0,2},{1,17},{2,0},{3,19},{4,6},{5,21},{6,4},{7,23},{8,10},{9,25},... | collective-permute-start | bytes 1179656 | tf_op jit(solution)/shard_map/ppermute | solution.py:330
  71.7 17.4 %collective-permute-start.11 = (f32[12,64,128]{2,1,0:T(8,128)S(1)}, f32[12,64,128]{2,1,0:T(8,128)S(1)}, u32[]{:S(2)}, u32[]{:S(2)}) collective-permute-start(f32[12,64,128]{2,1,0:T(8,128)S(1)} %fusion.7), channel_id=1, source_target_pairs={{0,12},{1,13},{2,14},{3,15},{4,0},{5,1},{6,2},{7,3},{8,4},{9,5},{1... | collective-permute-start | bytes 1179656 | tf_op jit(solution)/shard_map/ppermute | solution.py:330
  81.0 5.0 %collective-permute-start.17 = (f32[4,64,128]{2,1,0:T(8,128)S(1)}, f32[4,64,128]{2,1,0:T(8,128)S(1)}, u32[]{:S(2)}, u32[]{:S(2)}) collective-permute-start(f32[4,64,128]{2,1,0:T(8,128)S(1)} %slice_bitcast_fusion.17), channel_id=1, source_target_pairs={{0,2},{1,17},{2,0},{3,19},{4,6},{5,21},{6,4},{7,23},{8,10},{9,25},... | collective-permute-start | bytes 393224 | tf_op jit(solution)/shard_map/ppermute | solution.py:330
